TPU v7x, 32 devices: a whole 2x2x4 slice. The times are simulated.
32 devices in a mesh: slab: 8 (over z, x), img: 4 (over y, core).
Axes of the slice: x: 2, y: 2, z: 4, core: 2. Of those that a mesh axis runs over, the one named last changes fastest.
Arguments:
- images: bfloat16 [4096, 2, 4, 512], P(('slab', 'img')), may hold values from -6 to 6
- pose_bins: int32 [4096], P(('slab', 'img')), may hold values from 0 to 511, as said below
- labels: int32 [4096], P(('slab', 'img')), may hold values from 0 to 1
- defocus: bfloat16 [4096], P(('slab', 'img')), may hold values from 0.5 to 2
Outputs:
- maps: float32 [4, 1024, 2, 32], P('img', 'slab')
Inputs may be any that keep to these rules, and one draw needn't show every extreme that they name: With owner = (pose_bins // 16) // 4: among the 128 images of one device (aligned blocks in order), no owner is named more than 32 times, and one owner, the same for all blocks, is named exactly 32 times in every block.
All inputs are finite; a program needn't handle non-finite values.
Results may differ from a plain program's by a relative error of at most 0.025.
Values may be sent and summed in bfloat16 or wider, within the bound.
No kernel may reach another device: no remote copies, remote signals or barrier semaphores. Data moves between devices by JAX's collectives and lax.ppermute only.
A program may use at most 64 MiB of HBM per device.

v0:
```python
import math

import jax
import jax.numpy as jnp
from jax import lax
from jax.sharding import PartitionSpec as P

NX = 512
KY = 4
CLASSES = 2
ZDEV = 4
ZBINS = 4
XBINS = 4


def passed_along(block, axis, distance):
    devices = range(lax.axis_size(axis))
    route = [((i - distance) % len(devices), i) for i in devices]
    return lax.ppermute(block, axis, route)


def lanczos_taps(fraction):
    offsets = jnp.arange(8, dtype=jnp.float32) - 3.0
    distance = offsets[None, :] - fraction[:, None]
    kernel = jnp.sinc(distance) * jnp.sinc(distance / 4.0)
    return (kernel / jnp.sum(kernel, axis=-1, keepdims=True)).astype(jnp.bfloat16)


def ctf_weights(defocus, ky_rows, x_width):
    x_index = jnp.arange(x_width, dtype=jnp.int32)
    signed = (x_index + x_width // 2) % x_width - x_width // 2
    y_index = jnp.arange(ky_rows, dtype=jnp.int32) + 1
    radius = (y_index[:, None] * y_index[:, None] + signed[None, :] * signed[None, :]).astype(
        jnp.float32
    )
    radius = radius / float(x_width * x_width)
    phase_arg = 400.0 * math.pi * defocus.astype(jnp.float32)[:, None, None] * radius[None]
    return jnp.sin(phase_arg + 0.1)


def build_shift_table(x_width, num_bins):
    positions = jnp.arange(x_width, dtype=jnp.int32)
    tap_index = (positions[None, :] - positions[:, None] + 3) % x_width
    fraction = (jnp.arange(num_bins, dtype=jnp.float32) + 0.5) / num_bins
    tap_values = lanczos_taps(fraction)
    shift_table = jnp.zeros((num_bins, x_width, x_width), jnp.bfloat16)
    for tap_no in range(8):
        shift_table = shift_table + jnp.where(
            tap_index[None] == tap_no,
            tap_values[:, tap_no][:, None, None],
            jnp.zeros((), jnp.bfloat16),
        )
    return shift_table.reshape(num_bins * x_width, x_width)


def interpolate(weighted, xbin, shift_table, num_bins):
    number, parts, ky_rows, x_width = weighted.shape
    masked = jnp.stack(
        [
            jnp.where((xbin == bin_no)[:, None, None, None], weighted, jnp.zeros_like(weighted))
            for bin_no in range(num_bins)
        ],
        axis=3,
    )
    flattened = masked.reshape(number * parts * ky_rows, num_bins * x_width)
    product = jnp.dot(flattened, shift_table, preferred_element_type=jnp.float32)
    return product.reshape(number, parts, ky_rows, x_width).astype(jnp.bfloat16)


def slot_index(home_owner, capacity):
    position_idx = jnp.arange(home_owner.shape[0], dtype=jnp.int32)
    earlier = (position_idx[None, :] < position_idx[:, None]) & (
        home_owner[None, :] == home_owner[:, None]
    )
    rank_in = jnp.sum(earlier.astype(jnp.int32), axis=1)
    return home_owner * capacity + rank_in


def dft_table(length):
    index_row = jnp.arange(length, dtype=jnp.int32)
    angles = (
        2.0
        * math.pi
        / length
        * (index_row[:, None] * index_row[None, :] % length).astype(jnp.float32)
    )
    cosine = jnp.cos(angles)
    sine_part = jnp.sin(angles)
    return jnp.stack([jnp.stack([cosine, sine_part], 1), jnp.stack([-sine_part, cosine], 1)], 0)


def on_device(images, pose_bins, labels, defocus):
    owners = lax.axis_size("slab")
    groups = lax.axis_size("img")
    number = images.shape[0]
    capacity = 2 * number // owners
    slot_count = owners * capacity
    per_pose = ZBINS * XBINS
    home_owner = pose_bins // per_pose // ZDEV
    target = slot_index(home_owner, capacity)
    shift_table = build_shift_table(NX, XBINS)
    meta_rows = jnp.stack([pose_bins, labels], axis=1)
    send_meta = jnp.full((slot_count, 2), -1, jnp.int32).at[target].set(meta_rows)
    send_rows = jnp.zeros((slot_count,) + images.shape[1:], jnp.bfloat16).at[target].set(images)
    send_focus = jnp.zeros((slot_count,), jnp.bfloat16).at[target].set(defocus)
    got_rows, got_meta, got_focus = (
        lax.all_to_all(send_rows, "slab", split_axis=0, concat_axis=0, tiled=True),
        lax.all_to_all(send_meta, "slab", split_axis=0, concat_axis=0, tiled=True),
        lax.all_to_all(send_focus, "slab", split_axis=0, concat_axis=0, tiled=True),
    )
    got_xbin = jnp.maximum(got_meta[:, 0], 0) % XBINS
    weighted = (ctf_weights(got_focus, KY, NX)[:, None] * got_rows.astype(jnp.float32)).astype(
        jnp.bfloat16
    )
    placed = interpolate(weighted, got_xbin, shift_table, XBINS)
    pose_rows = got_meta[:, 0]
    filled = pose_rows >= 0
    clamped = jnp.maximum(pose_rows, 0)
    zbin_frac = (clamped // XBINS % ZBINS).astype(jnp.float32)
    z_taps = lanczos_taps((zbin_frac + 0.5) / ZBINS)
    offset = clamped // per_pose - lax.axis_index("slab") * ZDEV
    ext_depth = 3 * ZDEV
    dest_rows = (
        got_meta[:, 1][:, None] * ext_depth
        + offset[:, None]
        + jnp.arange(8, dtype=jnp.int32)[None, :]
    )
    targets = jnp.arange(CLASSES * ext_depth, dtype=jnp.int32)
    matches = (dest_rows[:, :, None] == targets[None, None, :]) & filled[:, None, None]
    spread = jnp.sum(jnp.where(matches, z_taps[:, :, None], jnp.zeros((), jnp.bfloat16)), axis=1)
    extended = jnp.dot(spread.T, placed.reshape(slot_count, -1), preferred_element_type=jnp.float32)
    extended = extended.reshape(CLASSES, ext_depth, 2, KY, NX)
    owned = extended[:, :ZDEV]
    for shift_by in (1, 2):
        owned = owned + passed_along(
            extended[:, shift_by * ZDEV : (shift_by + 1) * ZDEV], "slab", shift_by
        )
    spectra = jnp.einsum("czryx,rxsw->zsycw", owned, dft_table(NX), precision=lax.Precision.HIGHEST)
    norm_scale = 2.5 / math.sqrt(number * owners * groups * NX)
    columns = spectra.reshape(ZDEV, 2, KY, owners, -1)
    pencil = lax.all_to_all(columns, "slab", split_axis=3, concat_axis=0, tiled=True)
    full_sums = jnp.einsum(
        "zryqk,rzsw->yqksw", pencil, dft_table(pencil.shape[0]), precision=lax.Precision.HIGHEST
    )
    result = lax.psum_scatter(full_sums, "img", scatter_dimension=0, tiled=True)
    result = result.reshape(result.shape[0], result.shape[2], 2, result.shape[4])
    return result * norm_scale


def solution(mesh):
    placed = (
        P(("slab", "img"), None, None, None),
        P(("slab", "img")),
        P(("slab", "img")),
        P(("slab", "img")),
    )
    return jax.shard_map(
        on_device,
        mesh=mesh,
        in_specs=placed,
        out_specs=P("img", "slab", None, None),
        check_vma=False,
    )
```

profile of v0, /device:TPU:0, one launch (start us, length us, event | category | flops | bytes accessed | tf_op | source)
XLA Modules:
  0.0 165.6 jit_solution(10307154785037703848)
XLA Ops:
  6.5 0.8 and_select_fusion.4
  7.3 0.2 convert_reduce_fusion
  7.5 0.7 compare_select_fusion.2
  8.2 1.5 scatter_custom_fusion.1
  9.6 0.7 all_to_all.37
  10.3 7.3 %all-to-all-start.1 = ((bf16[8,32,1]{1,2,0:T(2,128)(2,1)}), bf16[8,32,1]{1,2,0:T(2,128)(2,1)S(1)}, u32[]{:S(2)}, u32[]{:S(2)}) async-start(bf16[8,32,1]{1,2,0:T(2,128)(2,1)} %all_to_all.37), calls=%async_computation.1 | async-start | bytes 8192 | tf_op jit(solution)/shard_map/all_to_all | solution.py:109
  17.6 3.9 %fusion.58 = f32[512,1,512]{2,0,1:T(8,128)S(1)} fusion(), kind=kLoop, calls=%fused_computation.84 | loop fusion | flops 3932160 | bytes 1048576 | tf_op jit(solution)/shard_map/neg | solution.py:89
  21.4 0.1 fusion.170
  21.6 0.7 pad_add_fusion
  22.2 0.1 copy.57
  22.4 0.9 scatter_custom_fusion
  23.3 0.7 copy.58
  24.0 0.0 all-to-all-done.1
  24.0 6.0 %all-to-all-start = ((s32[8,32,2]{1,2,0:T(2,128)}), s32[8,32,2]{1,2,0:T(2,128)S(1)}, u32[]{:S(2)}, u32[]{:S(2)}) async-start(s32[8,32,2]{1,2,0:T(2,128)} %copy.58), calls=%async_computation | async-start | bytes 16384 | tf_op jit(solution)/shard_map/all_to_all | solution.py:108
  30.0 1.9 %broadcast.833.clone = bf16[256,2,4,512]{3,2,1,0:T(4,128)(2,1)} broadcast(bf16[]{:T(256)} %constant.215.clone.1), dimensions={} | broadcast | bytes 2097154 | tf_op jit(solution)/shard_map/broadcast.24
  31.9 15.4 %scatter_fusion = bf16[256,2,4,512]{3,2,1,0:T(4,128)(2,1)} fusion(bf16[256,2,4,512]{3,2,1,0:T(4,128)(2,1)} %broadcast.833.clone, s32[128]{0:T(128)S(1)} %compare_select_fusion.2, bf16[128,2,4,512]{3,2,1,0:T(4,128)(2,1)S(1)} %copy-done.2), kind=kCustom, calls=%fused_computation.2 | custom fusion | bytes 3146240 | tf_op jit(solution)/shard_map/scatter | solution.py:104
  47.2 0.0 all-to-all-done
  47.2 6.0 %all-to-all-start.2 = ((bf16[256,2,4,512]{3,2,1,0:T(4,128)(2,1)}), bf16[256,2,4,512]{3,2,1,0:T(4,128)(2,1)S(1)}, u32[]{:S(2)}, u32[]{:S(2)}) async-start(bf16[256,2,4,512]{3,2,1,0:T(4,128)(2,1)} %scatter_fusion), calls=%async_computation.2 | async-start | bytes 4194304 | tf_op jit(solution)/shard_map/all_to_all | solution.py:107
  53.2 4.9 %fusion.56 = (f32[512,1,512]{2,0,1:T(8,128)}, f32[512,1,512]{2,0,1:T(8,128)}) fusion(), kind=kLoop, calls=%fused_computation.82 | loop fusion | flops 3670016 | bytes 2097152 | tf_op jit(solution)/shard_map/sin | solution.py:88
  58.2 1.3 broadcast_compare_fusion
  59.5 1.5 broadcast_compare_fusion.2
  61.0 1.4 broadcast_compare_fusion.4
  62.4 1.4 broadcast_compare_fusion.6
  63.9 0.1 divide_convert_fusion.1
  64.0 0.1 convert_multiply_fusion
  64.1 0.1 mul.364
  64.1 7.9 %add_sine_fusion = f32[256,4,512]{2,0,1:T(8,128)} fusion(f32[4,512]{1,0:T(4,128)S(1)} %convert_multiply_fusion, f32[256]{0:T(256)S(1)} %mul.364), kind=kLoop, calls=%fused_computation.41 | loop fusion | flops 1048576 | bytes 2106368 | tf_op jit(solution)/shard_map/sin | solution.py:38
  72.0 0.1 all_to_all.30
  72.2 0.1 fusion.166
  72.3 0.1 divide_convert_fusion
  72.5 27.9 %all-to-all-done.2 = bf16[256,2,4,512]{3,2,1,0:T(4,128)(2,1)S(1)} async-done(((bf16[256,2,4,512]{3,2,1,0:T(4,128)(2,1)}), bf16[256,2,4,512]{3,2,1,0:T(4,128)(2,1)S(1)}, u32[]{:S(2)}, u32[]{:S(2)}) %all-to-all-start.2) | async-done | bytes 2097184 | tf_op jit(solution)/shard_map/all_to_all | solution.py:107
  100.4 2.7 %select_bitcast_fusion.3 = (bf16[256,2,4,1,512]{4,0,3,2,1:T(8,128)(2,1)S(1)}, bf16[256,2,4,512]{3,0,2,1:T(8,128)(2,1)S(1)}) fusion(pred[256]{0:T(512)(128)(4,1)S(1)} %get-tuple-element.9, bf16[256,2,4,512]{3,2,1,0:T(4,128)(2,1)S(1)} %all-to-all-done.2, f32[256,4,512]{2,0,1:T(8,128)} %add_sine_fusion), kind=kLoop, calls=%fused_computation.40 | loop fusion | flops 4194304 | bytes 8388864 | tf_op jit(solution)/shard_map/stack | solution.py:58
  103.1 0.8 select_bitcast_fusion.2
  103.9 0.0 copy-done.3
  104.0 0.1 copy-done.4
  104.1 0.1 copy-done.5
  104.2 0.1 copy-done.6
  104.2 0.1 copy-done.7
  104.3 0.1 copy-done.8
  104.4 0.1 copy-done.9
  104.5 7.8 %bitcast_convert_fusion = bf16[256,2,4,512]{3,0,2,1:T(8,128)(2,1)} fusion(bf16[256,2,4,1,512]{4,0,3,2,1:T(8,128)(2,1)S(1)} %get-tuple-element.13, bf16[256,2,4,1,512]{4,0,3,2,1:T(8,128)(2,1)S(1)} %get-tuple-element.12, bf16[256,2,4,1,512]{4,0,3,2,1:T(8,128)(2,1)S(1)} %get-tuple-element.11, bf16[256,2,4,1,512]{4,0,3,2,1:T(8,128)(2,1)S(1)} %get-tuple-element.6, ...), kind=kOutput, calls=%fused_computation.15 | convolution fusion | flops 4324327424 | bytes 12582976 | tf_op jit(solution)/shard_map/dot_general | solution.py:66
  112.2 2.8 %copy.66 = bf16[256,2,4,512]{0,3,2,1:T(8,128)(2,1)S(1)} copy(bf16[256,2,4,512]{3,0,2,1:T(8,128)(2,1)} %bitcast_convert_fusion) | data formatting | bytes 4194304 | tf_op jit(solution)/shard_map/convert_element_type | solution.py:67
  115.0 0.7 fusion.13
  115.7 0.1 fusion.182
  115.8 1.5 collective-permute-start
  117.3 0.0 collective-permute-start.1
  117.3 0.0 copy-done.1
  117.3 0.6 maximum_bitcast_fusion.2
  117.9 5.6 %collective-permute-done = f32[2,4,2,4,512]{4,1,3,2,0:T(4,128)S(1)} collective-permute-done((f32[2,4,2,4,512]{4,1,3,2,0:T(4,128)S(1)}, f32[2,4,2,4,512]{4,1,3,2,0:T(4,128)S(1)}, u32[]{:S(2)}, u32[]{:S(2)}) %collective-permute-start) | collective-permute-done | bytes 131104 | tf_op jit(solution)/shard_map/ppermute | solution.py:19
  123.5 0.6 collective-permute-done.1
  124.1 0.1 fusion.61
  124.2 2.8 %fusion.39 = f32[4,2,4,2,512]{4,2,0,3,1:T(4,128)S(1)} fusion(f32[1,512,2,512]{3,1,0,2:T(8,128)S(1)} %get-tuple-element.15, f32[1,512,2,512]{3,1,0,2:T(8,128)S(1)} %get-tuple-element.14, f32[2,4,2,4,512]{4,1,3,2,0:T(4,128)S(1)} %fusion.61), kind=kOutput, calls=%fused_computation.56 | convolution fusion | flops 403701760 | bytes 4456448 | tf_op jit(solution)/shard_map/czryx,rxsw->zsycw/dot_general | solution.py:138
  127.0 0.1 copy.68
  127.1 0.1 reshape.494
  127.2 0.7 copy.69
  127.9 3.6 %all-to-all-start.3 = ((f32[4,2,4,8,128]{4,2,1,0,3:T(4,128)}), f32[4,2,4,8,128]{4,2,1,0,3:T(4,128)S(1)}, u32[]{:S(2)}, u32[]{:S(2)}) async-start(f32[4,2,4,8,128]{4,2,1,0,3:T(4,128)} %copy.69), calls=%async_computation.3 | async-start | bytes 262144 | tf_op jit(solution)/shard_map/all_to_all | solution.py:141
  131.5 0.0 reduce-scatter.2.cloned.1.call-start
  131.5 0.1 fusion.133
  131.6 0.1 fusion.128
  131.7 7.1 %all-to-all-done.3 = f32[4,2,4,8,128]{4,2,1,0,3:T(4,128)S(1)} async-done(((f32[4,2,4,8,128]{4,2,1,0,3:T(4,128)}), f32[4,2,4,8,128]{4,2,1,0,3:T(4,128)S(1)}, u32[]{:S(2)}, u32[]{:S(2)}) %all-to-all-start.3) | async-done | bytes 131104 | tf_op jit(solution)/shard_map/all_to_all | solution.py:141
  138.8 1.0 convolution_bitcast_fusion
  139.8 0.0 reduce-scatter.2.cloned.1.call-update
  139.8 17.5 %reduce-scatter.2.cloned.1.call-done = f32[1,1,128,2,32]{2,4,3,0,1:T(8,128)} async-done(((f32[4,1,128,2,32]{2,4,3,0,1:T(8,128)}), f32[1,1,128,2,32]{2,4,3,0,1:T(8,128)}) %reduce-scatter.2.cloned.1.call-update) | async-done | bytes 32784 | tf_op jit(solution)/shard_map/reduce_scatter | solution.py:145
  157.3 1.4 multiply_bitcast_fusion
  (29 shorter events, 0.3 us)
Async XLA Ops:
  6.5 25.3 %copy-start.2 = (bf16[128,2,4,512]{3,2,1,0:T(4,128)(2,1)S(1)}, bf16[128,2,4,512]{3,2,1,0:T(4,128)(2,1)}, u32[]{:S(2)}) copy-start(bf16[128,2,4,512]{3,2,1,0:T(4,128)(2,1)} %param.6) | copy-start | bytes 3145732
  10.3 13.7 %all-to-all-start.1 = ((bf16[8,32,1]{1,2,0:T(2,128)(2,1)}), bf16[8,32,1]{1,2,0:T(2,128)(2,1)S(1)}, u32[]{:S(2)}, u32[]{:S(2)}) async-start(bf16[8,32,1]{1,2,0:T(2,128)(2,1)} %all_to_all.37), calls=%async_computation.1 | async-start | bytes 8192 | tf_op jit(solution)/shard_map/all_to_all | solution.py:109
  24.0 23.2 %all-to-all-start = ((s32[8,32,2]{1,2,0:T(2,128)}), s32[8,32,2]{1,2,0:T(2,128)S(1)}, u32[]{:S(2)}, u32[]{:S(2)}) async-start(s32[8,32,2]{1,2,0:T(2,128)} %copy.58), calls=%async_computation | async-start | bytes 16384 | tf_op jit(solution)/shard_map/all_to_all | solution.py:108
  47.2 53.1 %all-to-all-start.2 = ((bf16[256,2,4,512]{3,2,1,0:T(4,128)(2,1)}), bf16[256,2,4,512]{3,2,1,0:T(4,128)(2,1)S(1)}, u32[]{:S(2)}, u32[]{:S(2)}) async-start(bf16[256,2,4,512]{3,2,1,0:T(4,128)(2,1)} %scatter_fusion), calls=%async_computation.2 | async-start | bytes 4194304 | tf_op jit(solution)/shard_map/all_to_all | solution.py:107
  103.0 1.0 copy-start.3
  103.1 1.0 copy-start.4
  103.1 1.1 copy-start.5
  103.1 1.2 copy-start.6
  103.1 1.2 copy-start.7
  103.1 1.3 copy-start.8
  103.1 1.4 copy-start.9
  115.0 2.3 %copy-start = (f32[512,1,512]{2,0,1:T(8,128)S(1)}, f32[512,1,512]{2,0,1:T(8,128)}, u32[]{:S(2)}) copy-start(f32[512,1,512]{2,0,1:T(8,128)} %get-tuple-element.41) | copy-start | bytes 3145732
  115.0 2.3 %copy-start.1 = (f32[512,1,512]{2,0,1:T(8,128)S(1)}, f32[512,1,512]{2,0,1:T(8,128)}, u32[]{:S(2)}) copy-start(f32[512,1,512]{2,0,1:T(8,128)} %get-tuple-element.42) | copy-start | bytes 3145732
  115.8 7.7 %collective-permute-start = (f32[2,4,2,4,512]{4,1,3,2,0:T(4,128)S(1)}, f32[2,4,2,4,512]{4,1,3,2,0:T(4,128)S(1)}, u32[]{:S(2)}, u32[]{:S(2)}) collective-permute-start(f32[2,4,2,4,512]{4,1,3,2,0:T(4,128)S(1)} %get-tuple-element.16), channel_id=1, source_target_pairs={{28,0},{0,4},{4,8},{8,12},{12,16},{16,20},{20,24},{24,28},{29,1},{... | collective-permute-start | bytes 393224 | tf_op jit(solution)/shard_map/ppermute | solution.py:19
  117.3 6.8 %collective-permute-start.1 = (f32[2,4,2,4,512]{4,1,3,2,0:T(4,128)S(1)}, f32[2,4,2,4,512]{4,1,3,2,0:T(4,128)S(1)}, u32[]{:S(2)}, u32[]{:S(2)}) collective-permute-start(f32[2,4,2,4,512]{4,1,3,2,0:T(4,128)S(1)} %get-tuple-element.17), channel_id=1, source_target_pairs={{24,0},{28,4},{0,8},{4,12},{8,16},{12,20},{16,24},{20,28},{25,1},{... | collective-permute-start | bytes 393224 | tf_op jit(solution)/shard_map/ppermute | solution.py:19
  127.9 10.9 %all-to-all-start.3 = ((f32[4,2,4,8,128]{4,2,1,0,3:T(4,128)}), f32[4,2,4,8,128]{4,2,1,0,3:T(4,128)S(1)}, u32[]{:S(2)}, u32[]{:S(2)}) async-start(f32[4,2,4,8,128]{4,2,1,0,3:T(4,128)} %copy.69), calls=%async_computation.3 | async-start | bytes 262144 | tf_op jit(solution)/shard_map/all_to_all | solution.py:141
  131.5 25.9 %reduce-scatter.2.cloned.1.call-start = ((), (), s32[]{:S(2)}) async-start(), calls=%async_computation.5 | async-start | bytes 163840 | tf_op jit(solution)/shard_map/reduce_scatter | solution.py:145
Sparse Core Ops, SparseCore 0:
  139.9 17.3 reduce-scatter.1
where the time goes:
time: 167 us; the launch traced here: 166 us
  waiting for transfers between devices  58.7 us (35%)
  other arithmetic  31 us (19%)
  local copies, waits for them, and re-layouts  25.6 us (15%)
  starting transfers between devices  24.3 us (15%)
  between operations  13.7 us (8%)
  matrix products  12.2 us (7%)
    all_to_all x1, waiting for transfers between devices, on_device(): lax.all_to_all(send_rows, 'slab', split_axis=0, concat_axis=0, tiled=True)  27.9 us
    reduce_scatter x1, waiting for transfers between devices, on_device(): result = lax.psum_scatter(full_sums, 'img', scatter_dimension=0, tiled=True)  17.5 us
    scatter x1, local copies, waits for them, and re-layouts, on_device(): jnp.zeros((slot_count,) + images.shape[1:], jnp.bfloat16).at[target]  15.4 us
    sin x1, other arithmetic, ctf_weights(): return jnp.sin(phase_arg + 0.1)  7.91 us
    dot_general x1, matrix products, interpolate(): jnp.dot(flattened, shift_table, preferred_element_type=jnp.float32)  7.76 us
    all_to_all x1, starting transfers between devices, on_device(): lax.all_to_all(send_focus, 'slab', split_axis=0, concat_axis=0, tiled=True)  7.25 us
    all_to_all x1, waiting for transfers between devices, on_device(): lax.all_to_all(columns, 'slab', split_axis=3, concat_axis=0, tiled=True)  7.1 us
    ppermute x2, waiting for transfers between devices, passed_along(): return lax.ppermute(block, axis, route)  6.17 us
  transfers between devices with their start and end apart: 7, of which 5 were waited for; matrix products, arithmetic and copies ran while one was open for 26% of the time, Pallas kernels for 0%

commit v1 on v0

v1 whole, which is shorter than its diff:
```python
import functools
import math

import jax
import jax.numpy as jnp
import numpy as np
from jax import lax
from jax.experimental import pallas as pl
from jax.experimental.pallas import tpu as pltpu
from jax.sharding import PartitionSpec as P

NX = 512
KY = 4
CLASSES = 2
ZBINS = 4
XBINS = 4
TAPS = 8
LANES = 128
QUARTERS = NX // LANES
PLANES = 32
CHUNKS = 4
UNROLL = 8
ROWS = QUARTERS * KY
bf16, f32 = jnp.bfloat16, jnp.float32


def lanczos_taps(num_bins):
    fraction = (np.arange(num_bins, dtype=np.float32) + np.float32(0.5)) / np.float32(num_bins)
    distance = (np.arange(TAPS, dtype=np.float32) - np.float32(3.0))[None, :] - fraction[:, None]
    kernel = (np.sinc(distance) * np.sinc(distance / np.float32(4.0))).astype(np.float32)
    return (kernel / kernel.sum(-1, keepdims=True)).astype(jnp.bfloat16).astype(np.float32)


def turns_per_defocus():
    x = np.arange(NX)
    signed = (x + NX // 2) % NX - NX // 2
    y = np.arange(KY) + 1
    radius = 200.0 * (y[:, None] ** 2 + signed[None, :] ** 2) / NX**2
    table = radius.reshape(KY, QUARTERS, LANES).transpose(1, 0, 2).reshape(ROWS, LANES)
    return table.astype(np.float32)


def shift_table():
    taps = lanczos_taps(XBINS)
    out = np.zeros((XBINS, NX, NX), np.float32)
    x_out = np.arange(NX)
    for tap in range(TAPS):
        out[:, (x_out - tap + 3) % NX, x_out] += taps[:, tap][:, None]
    out = out.reshape(XBINS, NX, LANES, QUARTERS).transpose(0, 1, 3, 2)
    return out.reshape(XBINS * NX, NX).astype(jnp.bfloat16)


def fourier_table():
    m, k = np.arange(LANES)[:, None], np.arange(LANES)[None, :]
    blocks = []
    for p in range(QUARTERS):
        angle = 2.0 * np.pi * (((4 * m + p) * k) % NX) / NX
        cos, sin = np.cos(angle), np.sin(angle)
        blocks.append(np.block([[cos, sin], [-sin, cos]]))
    return np.concatenate(blocks).astype(jnp.bfloat16)


def sine_coefficients(terms=5):
    f = 0.5 * np.cos(np.linspace(0.0, np.pi / 2, 4001))
    basis = f[:, None] ** (2 * np.arange(terms) + 1)
    return np.linalg.lstsq(basis, np.sin(2 * np.pi * f), rcond=None)[0].astype(np.float32)


def device_bits():
    slab, img = lax.axis_index("slab"), lax.axis_index("img")
    return img // 2, slab % 2, slab // 2 % 2, slab // 4


def transform(get_rows, spread, table_s, table_f, v_ref, put):
    cz = CLASSES * PLANES
    for y in range(2):
        for r in range(2):
            part = jnp.dot(spread, get_rows(r, y), preferred_element_type=f32).astype(bf16)
            at = (r * 2 + y) * cz
            for b in range(XBINS):
                v_ref[at : at + cz, b * NX : (b + 1) * NX] = part[b * cz : (b + 1) * cz]
    placed = jnp.dot(v_ref[...], table_s(), preferred_element_type=f32).astype(bf16)
    real, imag = placed[: 2 * cz], placed[2 * cz :]
    sums = []
    for p in range(QUARTERS):
        lanes = slice(p * LANES, (p + 1) * LANES)
        both = jnp.concatenate([real[:, lanes], imag[:, lanes]], axis=1)
        sums.append(jnp.dot(both, table_f(p), preferred_element_type=f32))
    g0, g1, g2, g3 = sums
    a, b, c, d = g0 + g2, g0 - g2, g1 + g3, g1 - g3
    turned = jnp.concatenate([-d[:, LANES:], d[:, :LANES]], axis=1)
    quarters = (a + c, b + turned, a - c, b - turned)
    for y in range(2):
        for cls in range(CLASSES):
            at = (y * CLASSES + cls) * PLANES
            for q in range(QUARTERS):
                put(y, cls, q, quarters[q][at : at + PLANES].astype(bf16))


def spread_matrix(pose, label, planes, first_plane):
    per_pose = ZBINS * XBINS
    taps = lanczos_taps(ZBINS)
    start, zbin, xbin = pose // per_pose, pose // XBINS % ZBINS, pose % XBINS
    shape = (XBINS * CLASSES * PLANES, pose.shape[1])
    row = lax.broadcasted_iota(jnp.int32, shape, 0)
    tap = (first_plane + row % PLANES - start + planes) % planes
    tap = jnp.where(row // PLANES == xbin * CLASSES + label, tap, -1)
    out = jnp.zeros(shape, f32)
    for t in range(TAPS):
        weight = jnp.full(pose.shape, float(taps[0, t]), f32)
        for z in range(1, ZBINS):
            weight = jnp.where(zbin == z, float(taps[z, t]), weight)
        out = jnp.where(tap == t, weight, out)
    return out.astype(bf16)


def place(out_ref):
    my_y, my_x, my_z, my_class = device_bits()

    def put(y, cls, q, value):
        index = ((q % 2) ^ my_x) * 8 + (y ^ my_y) * 4 + (cls ^ my_class) * 2 + ((q // 2) ^ my_z)
        out_ref[index] = value

    return put


def first_kernel(planes, x_hbm, focus_hbm, pose_hbm, label_hbm, turns_hbm, s_hbm, f_hbm,
                 out_ref, rows_ref, spread_ref, s_ref, f_ref,
                 x_ref, focus_ref, pose_ref, label_ref, turns_ref, wide_ref, w_ref, v_ref, sems):
    number = wide_ref.shape[0]
    chunk = x_ref.shape[0] // CHUNKS

    def copy(source, target, at):
        made = pltpu.make_async_copy(source, target, sems.at[at])
        made.start()
        return made

    small = [
        copy(source, target, at)
        for at, (source, target) in enumerate(
            ((focus_hbm, focus_ref), (turns_hbm, turns_ref), (pose_hbm, pose_ref), (label_hbm, label_ref))
        )
    ]
    parts = [
        copy(x_hbm.at[pl.ds(c * chunk, chunk)], x_ref.at[pl.ds(c * chunk, chunk)], 4 + c) for c in range(CHUNKS)
    ]
    tables = [copy(s_hbm, s_ref, 4 + CHUNKS), copy(f_hbm, f_ref, 5 + CHUNKS)]
    for made in small:
        made.wait()
    core = lax.axis_index("img") % 2
    coefficients = [float(v) for v in sine_coefficients()]
    wide_ref[...] = jnp.broadcast_to(focus_ref[...].astype(f32), (LANES, number)).T
    spread = spread_matrix(pose_ref[...], label_ref[...], planes, 0)
    spread_ref[...] = spread
    turns = turns_ref[...]

    def weigh(i, carry):
        angle = turns * wide_ref[pl.ds(i, 1), :] + 0.1 / (2 * math.pi)
        f = angle - jnp.round(angle)
        square = f * f
        poly = jnp.full(f.shape, coefficients[-1], f32)
        for coefficient in coefficients[-2::-1]:
            poly = poly * square + coefficient
        ctf = poly * f
        at = pl.multiple_of(i * 2 * ROWS, 2 * ROWS)
        rows = x_ref[pl.ds(at, 2 * ROWS), :].astype(f32)
        w_ref[pl.ds(at, ROWS), :] = ctf * rows[:ROWS]
        w_ref[pl.ds(at + ROWS, ROWS), :] = ctf * rows[ROWS:]
        return carry

    for c in range(CHUNKS):
        parts[c].wait()
        lax.fori_loop(c * number // CHUNKS, (c + 1) * number // CHUNKS, weigh, 0, unroll=UNROLL)

    def gather(r, ky):
        columns = [
            w_ref[pl.ds(r * ROWS + j * KY + ky, number, stride=2 * ROWS), :] for j in range(QUARTERS)
        ]
        return jnp.concatenate(columns, axis=1).astype(bf16)

    for r in range(2):
        for y in range(2):
            rows_ref[r, y] = gather(r, 2 * y + core)
    for made in tables:
        made.wait()
    transform(
        lambda r, y: gather(r, 2 * y + 1 - core),
        spread,
        lambda: s_ref[...],
        lambda p: f_ref[p * 2 * LANES : (p + 1) * 2 * LANES, :],
        v_ref,
        place(out_ref),
    )


def second_kernel(rows_ref, spread_ref, s_ref, f_ref, out_ref, v_ref):
    transform(
        lambda r, y: rows_ref[r, y],
        spread_ref[...],
        lambda: s_ref[...],
        lambda p: f_ref[p * 2 * LANES : (p + 1) * 2 * LANES, :],
        v_ref,
        place(out_ref),
    )


def last_kernel(scale, kept_ref, *refs):
    *got_refs, table_ref, out_ref = refs
    total = kept_ref[...].astype(f32)
    for got_ref in got_refs:
        total += got_ref[...].astype(f32)
    total = total.astype(bf16)
    turned = jnp.dot(table_ref[0], total[:, :LANES], preferred_element_type=f32)
    turned += jnp.dot(table_ref[1], total[:, LANES:], preferred_element_type=f32)
    out_ref[...] = turned * scale


def z_table(planes):
    z = np.arange(planes)
    angle = 2.0 * np.pi * ((z[:, None] * z[None, :]) % planes) / planes
    cos, sin = np.cos(angle), np.sin(angle)
    return np.stack([np.concatenate([cos, sin]), np.concatenate([-sin, cos])]).astype(jnp.bfloat16)


VMEM = pl.BlockSpec(memory_space=pltpu.VMEM)
SMEM = pl.BlockSpec(memory_space=pltpu.SMEM)
HBM = pl.BlockSpec(memory_space=pltpu.HBM)


def partner(axis, bit):
    return [(i, i ^ bit) for i in range(lax.axis_size(axis))]


def ctf_weights(defocus):
    x_index = jnp.arange(NX, dtype=jnp.int32)
    signed = (x_index + NX // 2) % NX - NX // 2
    y_index = jnp.arange(KY, dtype=jnp.int32) + 1
    radius = (y_index[:, None] ** 2 + signed[None, :] ** 2).astype(f32) / float(NX * NX)
    phase = 400.0 * math.pi * defocus.astype(f32)[:, None, None] * radius[None]
    return jnp.sin(phase + 0.1)


def many_planes(images, pose_bins, labels, defocus):
    owners, groups = lax.axis_size("slab"), lax.axis_size("img")
    number = images.shape[0]
    planes = owners * 4
    weighted = (ctf_weights(defocus)[:, None] * images.astype(f32)).astype(bf16)
    table_s = jnp.asarray(shift_table()).reshape(XBINS, NX, NX)
    table_f = jnp.asarray(fourier_table()).reshape(QUARTERS, 2, LANES, 2, LANES)

    def block(first_plane):
        spread = spread_matrix(pose_bins[None], labels[None], planes, first_plane)
        part = jnp.einsum("mi,irkx->rkmx", spread, weighted, preferred_element_type=f32).astype(bf16)
        part = part.reshape(2, KY, XBINS, CLASSES * PLANES, NX)
        placed = jnp.einsum("rkbcx,bxw->rkcw", part, table_s, preferred_element_type=f32).astype(bf16)
        placed = placed.reshape(2, KY, CLASSES, PLANES, QUARTERS, LANES)
        g0, g1, g2, g3 = jnp.einsum("rkczpm,prmsn->pkcnsz", placed, table_f, preferred_element_type=f32)
        a, b, c, d = g0 + g2, g0 - g2, g1 + g3, g1 - g3
        turned = jnp.stack([-d[..., 1, :], d[..., 0, :]], axis=-2)
        return jnp.stack([a + c, b + turned, a - c, b - turned], axis=2).astype(bf16)

    parts = lax.map(block, jnp.arange(planes // PLANES, dtype=jnp.int32) * PLANES)
    parts = jnp.moveaxis(parts, 0, -2).reshape(KY, CLASSES * NX, 2, planes).astype(f32)
    total = lax.psum_scatter(parts, "img", scatter_dimension=0, tiled=True)
    total = lax.psum_scatter(total, "slab", scatter_dimension=1, tiled=True)
    table = jnp.asarray(z_table(planes).astype(np.float32)).reshape(2, 2, planes, planes)
    scale = 2.5 / math.sqrt(number * owners * groups * NX)
    return scale * jnp.einsum("yqsz,stwz->yqtw", total, table, precision=lax.Precision.HIGHEST)


def on_device(images, pose_bins, labels, defocus):
    owners, groups = lax.axis_size("slab"), lax.axis_size("img")
    number = images.shape[0]
    planes = owners * 4
    if planes != PLANES:
        return many_planes(images, pose_bins, labels, defocus)
    scale = 2.5 / math.sqrt(number * owners * groups * NX)
    x = images.reshape(number, 2, KY, QUARTERS, LANES).transpose(0, 1, 3, 2, 4).reshape(number * 2 * ROWS, LANES)
    pieces = 2 * CLASSES * QUARTERS
    rows_shape = jax.ShapeDtypeStruct((2, 2, number, NX), bf16)
    spread_shape = jax.ShapeDtypeStruct((XBINS * CLASSES * PLANES, number), bf16)
    piece_shape = jax.ShapeDtypeStruct((pieces, PLANES, 2 * LANES), bf16)
    v_scratch = pltpu.VMEM((2 * 2 * CLASSES * PLANES, XBINS * NX), bf16)
    table_s, table_f = jnp.asarray(shift_table()), jnp.asarray(fourier_table())
    table_shapes = [jax.ShapeDtypeStruct(t.shape, bf16) for t in (table_s, table_f)]
    other, rows, spread, near_s, near_f = pl.pallas_call(
        functools.partial(first_kernel, planes),
        out_shape=(piece_shape, rows_shape, spread_shape, *table_shapes),
        in_specs=[HBM] * 7,
        out_specs=(VMEM,) * 5,
        scratch_shapes=[
            pltpu.VMEM(x.shape, bf16),
            pltpu.VMEM((1, number), bf16),
            pltpu.VMEM((1, number), jnp.int32),
            pltpu.VMEM((1, number), jnp.int32),
            pltpu.VMEM((ROWS, LANES), f32),
            pltpu.VMEM((number, LANES), f32),
            pltpu.VMEM(x.shape, f32),
            v_scratch,
            pltpu.SemaphoreType.DMA((CHUNKS + 6,)),
        ],
        compiler_params=pltpu.CompilerParams(vmem_limit_bytes=32 << 20),
        name="weigh_and_transform_other",
    )(*(
        pltpu.with_memory_space_constraint(v, pltpu.HBM)
        for v in (x, defocus[None], pose_bins[None], labels[None], jnp.asarray(turns_per_defocus()), table_s, table_f)
    ))
    got = lax.ppermute(other, "img", partner("img", 1))
    own = pl.pallas_call(
        second_kernel,
        out_shape=piece_shape,
        in_specs=[VMEM] * 4,
        out_specs=VMEM,
        scratch_shapes=[v_scratch],
        compiler_params=pltpu.CompilerParams(vmem_limit_bytes=16 << 20),
        name="transform_own",
    )(rows, spread, near_s, near_f)
    total = (own.astype(f32) + got.astype(f32)).astype(bf16)
    pieces = [total[3 * 4 : 4 * 4], total[2 * 4 : 3 * 4], total[4 : 2 * 4]]
    flat = owners * groups
    got = [
        lax.ppermute(piece, ("slab", "img"), [(i, i ^ flip) for i in range(flat)])
        for piece, flip in zip(pieces, (6, 4, 2))
    ]
    total = sum((g.astype(f32) for g in got), total[:4].astype(f32)).astype(bf16)
    pieces = [total[3], total[2], total[1]]
    got = [
        lax.ppermute(piece, ("slab", "img"), [(i, i ^ flip) for i in range(flat)])
        for piece, flip in zip(pieces, (24, 16, 8))
    ]
    out = pl.pallas_call(
        functools.partial(last_kernel, scale),
        out_shape=jax.ShapeDtypeStruct((2 * planes, LANES), f32),
        in_specs=[VMEM] * 5,
        out_specs=VMEM,
        compiler_params=pltpu.CompilerParams(vmem_limit_bytes=16 << 20),
        name="transform_planes",
    )(total[0], *got, jnp.asarray(z_table(planes)))
    return out.reshape(1, 2, planes, LANES).transpose(0, 3, 1, 2)


def solution(mesh):
    placed = (
        P(("slab", "img"), None, None, None),
        P(("slab", "img")),
        P(("slab", "img")),
        P(("slab", "img")),
    )
    return jax.shard_map(
        on_device, mesh=mesh, in_specs=placed, out_specs=P("img", "slab", None, None), check_vma=False
    )
```

time: 167 us -> 25.6 us (0.15)
  waiting for transfers between devices: 58.7 us -> 9.46 us
  other arithmetic: 31 us -> 0.12 us
  local copies, waits for them, and re-layouts: 25.6 us -> 0.03 us
  starting transfers between devices: 24.3 us -> 9.48 us
  between operations: 13.7 us -> 0.05 us
  matrix products: 12.2 us -> 0 us
  Pallas kernels: 0 us -> 6.35 us
    all_to_all x4 -> x0, waiting for transfers between devices: 35 us -> none  [the longest x1 27.9 us: on_device(): lax.all_to_all(send_rows, 'slab', split_axis=0, concat_axis=0, tiled=True)]
    all_to_all x4 -> x0, starting transfers between devices: 22.8 us -> none  [the longest x1 7.25 us: on_device(): lax.all_to_all(send_focus, 'slab', split_axis=0, concat_axis=0, tiled=True)]
    scatter x3 -> x0, local copies, waits for them, and re-layouts: 17.7 us -> none  [the longest x1 15.4 us: on_device(): jnp.zeros((slot_count,) + images.shape[1:], jnp.bfloat16).at[target]]
    reduce_scatter x1 -> x0, waiting for transfers between devices: 17.5 us -> none  [on_device(): result = lax.psum_scatter(full_sums, 'img', scatter_dimension=0, tiled=True)]
    sin x3 -> x0, other arithmetic: 12.9 us -> none  [the longest x1 7.91 us: ctf_weights(): return jnp.sin(phase_arg + 0.1)]
    dot_general x4 -> x0, matrix products: 12.2 us -> none  [the longest x1 7.76 us: interpolate(): jnp.dot(flattened, shift_table, preferred_element_type=jnp.float32)]
    ppermute x2 -> x7, starting transfers between devices: 1.53 us -> 9.48 us  [the longest x6 8.96 us: on_device(): lax.ppermute(piece, ('slab', 'img'), [(i, i ^ flip) for i in range(flat)])]
    pallas_call x0 -> x3, Pallas kernels: none -> 6.35 us  [the longest x1 4.45 us: on_device(): pl.pallas_call(functools.partial(first_kernel, planes), out_shape=(piece_...]
  transfers between devices with their start and end apart: 7 -> 7, of which waited for: 5 -> 5; matrix products, arithmetic and copies ran while one was open for 26% -> 0% of each run, Pallas kernels for 0% -> 4%
where the time goes in v1:
time: 25.6 us; the launch traced here: 25.5 us
  starting transfers between devices  9.48 us (37%)
  waiting for transfers between devices  9.46 us (37%)
  Pallas kernels  6.35 us (25%)
    ppermute x6, waiting for transfers between devices, on_device(): lax.ppermute(piece, ('slab', 'img'), [(i, i ^ flip) for i in range(flat)])  9.45 us
    ppermute x6, starting transfers between devices, on_device(): lax.ppermute(piece, ('slab', 'img'), [(i, i ^ flip) for i in range(flat)])  8.96 us
    pallas_call x1, Pallas kernels, on_device(): pl.pallas_call(functools.partial(first_kernel, planes), out_shape=(piece_...  4.45 us
    pallas_call x1, Pallas kernels, on_device(): pl.pallas_call(second_kernel, out_shape=piece_shape, in_specs=[VMEM] * 4,...  1.14 us
    pallas_call x1, Pallas kernels, on_device(): pl.pallas_call(functools.partial(last_kernel, scale), out_shape=jax.Shape...  0.75 us
    ppermute x1, starting transfers between devices, on_device(): got = lax.ppermute(other, 'img', partner('img', 1))  0.52 us
  transfers between devices with their start and end apart: 7, of which 5 were waited for; matrix products, arithmetic and copies ran while one was open for 0% of the time, Pallas kernels for 4%

profile of v1, /device:TPU:0, one launch (start us, length us, event | category | flops | bytes accessed | tf_op | source)
XLA Modules:
  0.0 25.5 jit_solution(11947151340285310481)
XLA Ops:
  0.0 4.5 %weigh_and_transform_other.1 = (bf16[16,32,256]{2,1,0:T(8,128)(2,1)S(1)}, bf16[2,2,128,512]{3,2,1,0:T(8,128)(2,1)S(1)}, bf16[256,128]{1,0:T(8,128)(2,1)S(1)}, bf...) custom-call(bf16[4096,128]{1,0:T(8,128)(2,1)} %bitcast.19, bf16[1,128]{1,0:T(2,128)(2,1)} %bitcast.20, s32[1,128]{1,0:T(1,128)} %bitcast.21, ...), custom_call_target="tpu_custom_call" | custom-call | tf_op jit(solution)/shard_map/weigh_and_transform_other/pallas_call | solution.py:286
  4.5 0.5 %collective-permute-start = (bf16[16,32,256]{2,1,0:T(8,128)(2,1)S(1)}, bf16[16,32,256]{2,1,0:T(8,128)(2,1)S(1)}, u32[]{:S(2)}, u32[]{:S(2)}) collective-permute-start(bf16[16,32,256]{2,1,0:T(8,128)(2,1)S(1)} %get-tuple-element.14), channel_id=1, source_target_pairs={{0,1},{1,0},{2,3},{3,2},{4,5},{5,4},{6,7},{7,6},{8,9},{9,8},{10,11... | collective-permute-start | bytes 786440 | tf_op jit(solution)/shard_map/ppermute | solution.py:308
  5.0 0.0 copy-start
  5.0 1.1 %transform_own.1 = bf16[16,32,256]{2,1,0:T(8,128)(2,1)S(1)} custom-call(bf16[2,2,128,512]{3,2,1,0:T(8,128)(2,1)S(1)} %get-tuple-element.10.rows_ref, bf16[256,128]{1,0:T(8,128)(2,1)S(1)} %get-tuple-element.11.spread_ref, bf16[2048,512]{1,0:T(8,128)(2,1)S(1)} %get-tuple-element.12.s_ref, bf16[1024,256]{1,0:T(8,128)(2,1)S(1)} %get-tuple-element.13.f_ref), custom_call_target="tpu_custom_call" | custom-call | tf_op jit(solution)/shard_map/transform_own/pallas_call | solution.py:309
  6.1 0.0 collective-permute-done
  6.1 0.1 add_convert_fusion
  6.2 3.9 %collective-permute-start.1 = (bf16[4,32,256]{2,1,0:T(8,128)(2,1)S(1)}, bf16[4,32,256]{2,1,0:T(8,128)(2,1)S(1)}, u32[]{:S(2)}, u32[]{:S(2)}) collective-permute-start(bf16[4,32,256]{2,1,0:T(8,128)(2,1)S(1)} %get-tuple-element.15), channel_id=1, source_target_pairs={{0,6},{1,7},{2,4},{3,5},{4,2},{5,3},{6,0},{7,1},{8,14},{9,15},{10,... | collective-permute-start | bytes 196616 | tf_op jit(solution)/shard_map/ppermute | solution.py:322
  10.1 0.5 %collective-permute-start.3 = (bf16[4,32,256]{2,1,0:T(8,128)(2,1)S(1)}, bf16[4,32,256]{2,1,0:T(8,128)(2,1)S(1)}, u32[]{:S(2)}, u32[]{:S(2)}) collective-permute-start(bf16[4,32,256]{2,1,0:T(8,128)(2,1)S(1)} %get-tuple-element.16), channel_id=1, source_target_pairs={{0,2},{1,3},{2,0},{3,1},{4,6},{5,7},{6,4},{7,5},{8,10},{9,11},{10,... | collective-permute-start | bytes 196616 | tf_op jit(solution)/shard_map/ppermute | solution.py:322
  10.6 0.1 collective-permute-start.2
  10.8 1.8 %collective-permute-done.1 = bf16[4,32,256]{2,1,0:T(8,128)(2,1)S(1)} collective-permute-done((bf16[4,32,256]{2,1,0:T(8,128)(2,1)S(1)}, bf16[4,32,256]{2,1,0:T(8,128)(2,1)S(1)}, u32[]{:S(2)}, u32[]{:S(2)}) %collective-permute-start.1) | collective-permute-done | bytes 65568 | tf_op jit(solution)/shard_map/ppermute | solution.py:322
  12.5 1.9 %collective-permute-done.3 = bf16[4,32,256]{2,1,0:T(8,128)(2,1)S(1)} collective-permute-done((bf16[4,32,256]{2,1,0:T(8,128)(2,1)S(1)}, bf16[4,32,256]{2,1,0:T(8,128)(2,1)S(1)}, u32[]{:S(2)}, u32[]{:S(2)}) %collective-permute-start.3) | collective-permute-done | bytes 65568 | tf_op jit(solution)/shard_map/ppermute | solution.py:322
  14.4 0.5 %collective-permute-done.2 = bf16[4,32,256]{2,1,0:T(8,128)(2,1)S(1)} collective-permute-done((bf16[4,32,256]{2,1,0:T(8,128)(2,1)S(1)}, bf16[4,32,256]{2,1,0:T(8,128)(2,1)S(1)}, u32[]{:S(2)}, u32[]{:S(2)}) %collective-permute-start.2) | collective-permute-done | bytes 65568 | tf_op jit(solution)/shard_map/ppermute | solution.py:322
  15.0 1.6 %collective-permute-start.6 = (bf16[32,256]{1,0:T(8,128)(2,1)S(1)}, bf16[32,256]{1,0:T(8,128)(2,1)S(1)}, u32[]{:S(2)}, u32[]{:S(2)}) collective-permute-start(bf16[32,256]{1,0:T(8,128)(2,1)S(1)} %get-tuple-element.18), channel_id=1, source_target_pairs={{0,8},{1,9},{2,10},{3,11},{4,12},{5,13},{6,14},{7,15},{8,0},{9,1},... | collective-permute-start | bytes 49160 | tf_op jit(solution)/shard_map/ppermute | solution.py:328
  16.6 2.6 %collective-permute-start.5 = (bf16[32,256]{1,0:T(8,128)(2,1)S(1)}, bf16[32,256]{1,0:T(8,128)(2,1)S(1)}, u32[]{:S(2)}, u32[]{:S(2)}) collective-permute-start(bf16[32,256]{1,0:T(8,128)(2,1)S(1)} %get-tuple-element.19), channel_id=1, source_target_pairs={{0,16},{1,17},{2,18},{3,19},{4,20},{5,21},{6,22},{7,23},{8,24},{9,... | collective-permute-start | bytes 49160 | tf_op jit(solution)/shard_map/ppermute | solution.py:328
  19.2 0.2 collective-permute-start.4
  19.4 0.0 collective-permute-done.6.refs_2_
  19.4 1.9 %collective-permute-done.5.refs_1_ = bf16[32,256]{1,0:T(8,128)(2,1)S(1)} collective-permute-done((bf16[32,256]{1,0:T(8,128)(2,1)S(1)}, bf16[32,256]{1,0:T(8,128)(2,1)S(1)}, u32[]{:S(2)}, u32[]{:S(2)}) %collective-permute-start.5) | collective-permute-done | bytes 16416 | tf_op jit(solution)/shard_map/ppermute | solution.py:328
  21.3 3.4 %collective-permute-done.4.refs_0_ = bf16[32,256]{1,0:T(8,128)(2,1)S(1)} collective-permute-done((bf16[32,256]{1,0:T(8,128)(2,1)S(1)}, bf16[32,256]{1,0:T(8,128)(2,1)S(1)}, u32[]{:S(2)}, u32[]{:S(2)}) %collective-permute-start.4) | collective-permute-done | bytes 16416 | tf_op jit(solution)/shard_map/ppermute | solution.py:328
  24.7 0.0 copy-done
  24.7 0.8 %transform_planes.1 = f32[64,128]{1,0:T(8,128)} custom-call(bf16[32,256]{1,0:T(8,128)(2,1)S(1)} %get-tuple-element.21.kept_ref, bf16[32,256]{1,0:T(8,128)(2,1)S(1)} %collective-permute-done.4.refs_0_, bf16[32,256]{1,0:T(8,128)(2,1)S(1)} %collective-permute-done.5.refs_1_, bf16[32,256]{1,0:T(8,128)(2,1)S(1)} %collective-permute-done.6.refs_2_, ...), custom_call_target="tpu_custom_call" | custom-call | tf_op jit(solution)/shard_map/transform_planes/pallas_call | solution.py:331
  (3 shorter events, 0.1 us)
Async XLA Ops:
  4.5 1.7 %collective-permute-start = (bf16[16,32,256]{2,1,0:T(8,128)(2,1)S(1)}, bf16[16,32,256]{2,1,0:T(8,128)(2,1)S(1)}, u32[]{:S(2)}, u32[]{:S(2)}) collective-permute-start(bf16[16,32,256]{2,1,0:T(8,128)(2,1)S(1)} %get-tuple-element.14), channel_id=1, source_target_pairs={{0,1},{1,0},{2,3},{3,2},{4,5},{5,4},{6,7},{7,6},{8,9},{9,8},{10,11... | collective-permute-start | bytes 786440 | tf_op jit(solution)/shard_map/ppermute | solution.py:308
  5.0 19.8 %copy-start = (bf16[2,64,32]{2,1,0:T(8,128)(2,1)S(1)}, bf16[2,64,32]{2,1,0:T(8,128)(2,1)}, u32[]{:S(2)}) copy-start(bf16[2,64,32]{2,1,0:T(8,128)(2,1)} %constant.11.clone.refs_3_) | copy-start | bytes 24580
  6.2 6.3 %collective-permute-start.1 = (bf16[4,32,256]{2,1,0:T(8,128)(2,1)S(1)}, bf16[4,32,256]{2,1,0:T(8,128)(2,1)S(1)}, u32[]{:S(2)}, u32[]{:S(2)}) collective-permute-start(bf16[4,32,256]{2,1,0:T(8,128)(2,1)S(1)} %get-tuple-element.15), channel_id=1, source_target_pairs={{0,6},{1,7},{2,4},{3,5},{4,2},{5,3},{6,0},{7,1},{8,14},{9,15},{10,... | collective-permute-start | bytes 196616 | tf_op jit(solution)/shard_map/ppermute | solution.py:322
  10.1 4.3 %collective-permute-start.3 = (bf16[4,32,256]{2,1,0:T(8,128)(2,1)S(1)}, bf16[4,32,256]{2,1,0:T(8,128)(2,1)S(1)}, u32[]{:S(2)}, u32[]{:S(2)}) collective-permute-start(bf16[4,32,256]{2,1,0:T(8,128)(2,1)S(1)} %get-tuple-element.16), channel_id=1, source_target_pairs={{0,2},{1,3},{2,0},{3,1},{4,6},{5,7},{6,4},{7,5},{8,10},{9,11},{10,... | collective-permute-start | bytes 196616 | tf_op jit(solution)/shard_map/ppermute | solution.py:322
  10.6 4.3 %collective-permute-start.2 = (bf16[4,32,256]{2,1,0:T(8,128)(2,1)S(1)}, bf16[4,32,256]{2,1,0:T(8,128)(2,1)S(1)}, u32[]{:S(2)}, u32[]{:S(2)}) collective-permute-start(bf16[4,32,256]{2,1,0:T(8,128)(2,1)S(1)} %get-tuple-element.17), channel_id=1, source_target_pairs={{0,4},{1,5},{2,6},{3,7},{4,0},{5,1},{6,2},{7,3},{8,12},{9,13},{10,... | collective-permute-start | bytes 196616 | tf_op jit(solution)/shard_map/ppermute | solution.py:322
  15.0 4.5 %collective-permute-start.6 = (bf16[32,256]{1,0:T(8,128)(2,1)S(1)}, bf16[32,256]{1,0:T(8,128)(2,1)S(1)}, u32[]{:S(2)}, u32[]{:S(2)}) collective-permute-start(bf16[32,256]{1,0:T(8,128)(2,1)S(1)} %get-tuple-element.18), channel_id=1, source_target_pairs={{0,8},{1,9},{2,10},{3,11},{4,12},{5,13},{6,14},{7,15},{8,0},{9,1},... | collective-permute-start | bytes 49160 | tf_op jit(solution)/shard_map/ppermute | solution.py:328
  16.6 4.7 %collective-permute-start.5 = (bf16[32,256]{1,0:T(8,128)(2,1)S(1)}, bf16[32,256]{1,0:T(8,128)(2,1)S(1)}, u32[]{:S(2)}, u32[]{:S(2)}) collective-permute-start(bf16[32,256]{1,0:T(8,128)(2,1)S(1)} %get-tuple-element.19), channel_id=1, source_target_pairs={{0,16},{1,17},{2,18},{3,19},{4,20},{5,21},{6,22},{7,23},{8,24},{9,... | collective-permute-start | bytes 49160 | tf_op jit(solution)/shard_map/ppermute | solution.py:328
  19.2 5.5 %collective-permute-start.4 = (bf16[32,256]{1,0:T(8,128)(2,1)S(1)}, bf16[32,256]{1,0:T(8,128)(2,1)S(1)}, u32[]{:S(2)}, u32[]{:S(2)}) collective-permute-start(bf16[32,256]{1,0:T(8,128)(2,1)S(1)} %get-tuple-element.20), channel_id=1, source_target_pairs={{0,24},{1,25},{2,26},{3,27},{4,28},{5,29},{6,30},{7,31},{8,16},{9,... | collective-permute-start | bytes 49160 | tf_op jit(solution)/shard_map/ppermute | solution.py:328

commit v2 on v1

v2 whole, which is shorter than its diff:
```python
import functools
import math

import jax
import jax.numpy as jnp
import numpy as np
from jax import lax
from jax.experimental import pallas as pl
from jax.experimental.pallas import tpu as pltpu
from jax.sharding import PartitionSpec as P

NX = 512
KY = 4
CLASSES = 2
ZBINS = 4
XBINS = 4
TAPS = 8
LANES = 128
QUARTERS = NX // LANES
GROUP = LANES // QUARTERS
PLANES = 32
CHUNKS = 4
UNROLL = 8
ROWS = QUARTERS * KY
bf16, f32 = jnp.bfloat16, jnp.float32


def lanczos_taps(num_bins):
    fraction = (np.arange(num_bins, dtype=np.float32) + np.float32(0.5)) / np.float32(num_bins)
    distance = (np.arange(TAPS, dtype=np.float32) - np.float32(3.0))[None, :] - fraction[:, None]
    kernel = (np.sinc(distance) * np.sinc(distance / np.float32(4.0))).astype(np.float32)
    return (kernel / kernel.sum(-1, keepdims=True)).astype(jnp.bfloat16).astype(np.float32)


def turns_per_defocus():
    x = np.arange(NX)
    signed = (x + NX // 2) % NX - NX // 2
    y = np.arange(KY) + 1
    radius = 200.0 * (y[:, None] ** 2 + signed[None, :] ** 2) / NX**2
    table = radius.reshape(KY, QUARTERS, LANES).transpose(1, 0, 2).reshape(ROWS, LANES)
    return table.astype(np.float32)


def fourier_table():
    taps = lanczos_taps(XBINS).astype(np.float64)
    m = np.arange(LANES)
    group, lane = np.arange(LANES) // GROUP, np.arange(LANES) % GROUP
    out = np.zeros((QUARTERS, XBINS, LANES, 2, LANES))
    for q in range(QUARTERS):
        column = 4 * (GROUP * ((group - q) % QUARTERS) + lane) + q
        shift = 2.0 * np.pi * (((np.arange(TAPS) - 3)[:, None] * column[None, :]) % NX) / NX
        wave = 2.0 * np.pi * ((m[:, None] * column[None, :]) % NX) / NX
        for b in range(XBINS):
            value = (taps[b][:, None] * np.exp(1j * shift)).sum(0)[None, :] * np.exp(1j * wave)
            out[q, b, :, 0], out[q, b, :, 1] = value.real, value.imag
    return out.reshape(QUARTERS, XBINS * LANES, 2 * LANES).astype(jnp.bfloat16)


def order_table():
    out = np.zeros((QUARTERS, LANES, LANES), np.float32)
    group, lane = np.arange(LANES) // GROUP, np.arange(LANES) % GROUP
    for quarter in range(QUARTERS):
        out[quarter, np.arange(LANES), 4 * lane + (group - quarter) % QUARTERS] = 1.0
    return out.astype(jnp.bfloat16)


def sine_coefficients(terms=5):
    f = 0.5 * np.cos(np.linspace(0.0, np.pi / 2, 4001))
    basis = f[:, None] ** (2 * np.arange(terms) + 1)
    return np.linalg.lstsq(basis, np.sin(2 * np.pi * f), rcond=None)[0].astype(np.float32)


def device_bits():
    slab, img = lax.axis_index("slab"), lax.axis_index("img")
    return img // 2, slab % 2, slab // 2 % 2, slab // 4


def quarter_sums(parts):
    (r0, i0), (r1, i1), (r2, i2), (r3, i3) = parts
    ar, ai, br, bi = r0 + r2, i0 + i2, r0 - r2, i0 - i2
    cr, ci, dr, di = r1 + r3, i1 + i3, r1 - r3, i1 - i3
    return (ar + cr, ai + ci), (br - di, bi + dr), (ar - cr, ai - ci), (br + di, bi - dr)


def transform(w_ref, ky_low, spread, table, u_ref, v_ref, put):
    cz = CLASSES * PLANES
    number = spread.shape[1]
    for y in range(2):

        def column(r, p):
            return w_ref[pl.ds(r * ROWS + p * KY + 2 * y + ky_low, number, stride=2 * ROWS), :]

        sums = quarter_sums([(column(0, p), column(1, p)) for p in range(QUARTERS)])
        for q in range(QUARTERS):
            for r in range(2):
                at = (r * QUARTERS + q) * LANES
                u_ref[y, :, at : at + LANES] = sums[q][r].astype(bf16)
    for y in range(2):
        part = jnp.dot(spread, u_ref[y], preferred_element_type=f32).astype(bf16)
        for r in range(2):
            for q in range(QUARTERS):
                at, row = (r * QUARTERS + q) * LANES, (r * 2 + y) * cz
                for b in range(XBINS):
                    v_ref[q, row : row + cz, b * LANES : (b + 1) * LANES] = part[b * cz : (b + 1) * cz, at : at + LANES]
    group = lax.broadcasted_iota(jnp.int32, (2 * cz, LANES), 1) // GROUP
    real, imag = [], []
    for q in range(QUARTERS):
        both = jnp.dot(v_ref[q], table(q), preferred_element_type=f32)
        real.append(both[: 2 * cz, :LANES] - both[2 * cz :, LANES:])
        imag.append(both[: 2 * cz, LANES:] + both[2 * cz :, :LANES])
    for quarter in range(QUARTERS):
        chosen = []
        for parts in (real, imag):
            value = parts[(0 - quarter) % QUARTERS]
            for j in range(1, QUARTERS):
                value = jnp.where(group == j, parts[(j - quarter) % QUARTERS], value)
            chosen.append(value.astype(bf16))
        value = jnp.concatenate(chosen, axis=1)
        for y in range(2):
            for cls in range(CLASSES):
                at = (y * CLASSES + cls) * PLANES
                put(y, cls, quarter, value[at : at + PLANES])


def spread_matrix(pose, label, planes, first_plane):
    per_pose = ZBINS * XBINS
    taps = lanczos_taps(ZBINS)
    start, zbin, xbin = pose // per_pose, pose // XBINS % ZBINS, pose % XBINS
    shape = (XBINS * CLASSES * PLANES, pose.shape[1])
    row = lax.broadcasted_iota(jnp.int32, shape, 0)
    tap = (first_plane + row % PLANES - start + planes) % planes
    tap = jnp.where(row // PLANES == xbin * CLASSES + label, tap, -1)
    out = jnp.zeros(shape, f32)
    for t in range(TAPS):
        weight = jnp.full(pose.shape, float(taps[0, t]), f32)
        for z in range(1, ZBINS):
            weight = jnp.where(zbin == z, float(taps[z, t]), weight)
        out = jnp.where(tap == t, weight, out)
    return out.astype(bf16)


def place(out_ref):
    my_y, my_x, my_z, my_class = device_bits()

    def put(y, cls, q, value):
        index = ((q % 2) ^ my_x) * 8 + (y ^ my_y) * 4 + (cls ^ my_class) * 2 + ((q // 2) ^ my_z)
        out_ref[index] = value

    return put


def first_kernel(planes, x_hbm, focus_hbm, pose_hbm, label_hbm, turns_hbm, table_hbm,
                 out_ref, w_ref, spread_ref, table_ref,
                 x_ref, focus_ref, pose_ref, label_ref, turns_ref, wide_ref, u_ref, v_ref, sems):
    number = wide_ref.shape[0]
    chunk = x_ref.shape[0] // CHUNKS

    def copy(source, target, at):
        made = pltpu.make_async_copy(source, target, sems.at[at])
        made.start()
        return made

    small = [
        copy(source, target, at)
        for at, (source, target) in enumerate(
            ((focus_hbm, focus_ref), (turns_hbm, turns_ref), (pose_hbm, pose_ref), (label_hbm, label_ref))
        )
    ]
    parts = [
        copy(x_hbm.at[pl.ds(c * chunk, chunk)], x_ref.at[pl.ds(c * chunk, chunk)], 4 + c) for c in range(CHUNKS)
    ]
    table = copy(table_hbm, table_ref, 4 + CHUNKS)
    for made in small:
        made.wait()
    core = lax.axis_index("img") % 2
    coefficients = [float(v) for v in sine_coefficients()]
    wide_ref[...] = jnp.broadcast_to(focus_ref[...].astype(f32), (LANES, number)).T
    spread_ref[...] = spread_matrix(pose_ref[...], label_ref[...], planes, 0)
    turns = turns_ref[...]

    def weigh(i, carry):
        angle = turns * wide_ref[pl.ds(i, 1), :] + 0.1 / (2 * math.pi)
        f = angle - jnp.round(angle)
        square = f * f
        poly = jnp.full(f.shape, coefficients[-1], f32)
        for coefficient in coefficients[-2::-1]:
            poly = poly * square + coefficient
        ctf = poly * f
        at = pl.multiple_of(i * 2 * ROWS, 2 * ROWS)
        rows = x_ref[pl.ds(at, 2 * ROWS), :].astype(f32)
        w_ref[pl.ds(at, ROWS), :] = ctf * rows[:ROWS]
        w_ref[pl.ds(at + ROWS, ROWS), :] = ctf * rows[ROWS:]
        return carry

    for c in range(CHUNKS):
        parts[c].wait()
        lax.fori_loop(c * number // CHUNKS, (c + 1) * number // CHUNKS, weigh, 0, unroll=UNROLL)
    table.wait()
    transform(w_ref, 1 - core, spread_ref[...], lambda q: table_ref[q], u_ref, v_ref, place(out_ref))


def second_kernel(w_ref, spread_ref, table_ref, out_ref, u_ref, v_ref):
    core = lax.axis_index("img") % 2
    transform(w_ref, core, spread_ref[...], lambda q: table_ref[q], u_ref, v_ref, place(out_ref))


def last_kernel(scale, kept_ref, *refs):
    *got_refs, order_ref, table_ref, out_ref = refs
    total = kept_ref[...].astype(f32)
    for got_ref in got_refs:
        total += got_ref[...].astype(f32)
    total = total.astype(bf16)
    order = order_ref[lax.axis_index("slab") % QUARTERS]
    turned = 0.0
    for s in range(2):
        part = total[:, s * LANES : (s + 1) * LANES]
        part = jnp.dot(part, order, preferred_element_type=f32).astype(bf16)
        turned += jnp.dot(table_ref[s], part, preferred_element_type=f32)
    out_ref[...] = turned * scale


def z_table(planes):
    z = np.arange(planes)
    angle = 2.0 * np.pi * ((z[:, None] * z[None, :]) % planes) / planes
    cos, sin = np.cos(angle), np.sin(angle)
    return np.stack([np.concatenate([cos, sin]), np.concatenate([-sin, cos])]).astype(jnp.bfloat16)


VMEM = pl.BlockSpec(memory_space=pltpu.VMEM)
SMEM = pl.BlockSpec(memory_space=pltpu.SMEM)
HBM = pl.BlockSpec(memory_space=pltpu.HBM)


def partner(axis, bit):
    return [(i, i ^ bit) for i in range(lax.axis_size(axis))]


def ctf_weights(defocus):
    x_index = jnp.arange(NX, dtype=jnp.int32)
    signed = (x_index + NX // 2) % NX - NX // 2
    y_index = jnp.arange(KY, dtype=jnp.int32) + 1
    radius = (y_index[:, None] ** 2 + signed[None, :] ** 2).astype(f32) / float(NX * NX)
    phase = 400.0 * math.pi * defocus.astype(f32)[:, None, None] * radius[None]
    return jnp.sin(phase + 0.1)


def many_planes(images, pose_bins, labels, defocus):
    owners, groups = lax.axis_size("slab"), lax.axis_size("img")
    number = images.shape[0]
    planes = owners * 4
    weighted = (ctf_weights(defocus)[:, None] * images.astype(f32)).astype(bf16)
    table = jnp.asarray(fourier_table()).reshape(QUARTERS, XBINS, LANES, 2, LANES)
    order = jnp.asarray(order_table())
    quarters = jnp.moveaxis(weighted.astype(f32).reshape(number, 2, KY, QUARTERS, LANES), 3, 0)
    sums = quarter_sums([(part[:, 0], part[:, 1]) for part in quarters])
    sums = jnp.stack([jnp.stack(pair) for pair in sums]).astype(bf16)

    def block(first_plane):
        spread = spread_matrix(pose_bins[None], labels[None], planes, first_plane)
        spread = spread.reshape(XBINS, CLASSES * PLANES, number)
        part = jnp.einsum("bci,qrikm->qrkcbm", spread, sums, preferred_element_type=f32).astype(bf16)
        both = jnp.einsum("qrkcbm,qbmsn->rsqkcn", part, table, preferred_element_type=f32)
        turned = jnp.stack([both[0, 0] - both[1, 1], both[0, 1] + both[1, 0]])
        turned = turned.reshape(2, QUARTERS, KY, CLASSES, PLANES, QUARTERS, GROUP)
        ordered = []
        for quarter in range(QUARTERS):
            groups_of = [turned[:, (j - quarter) % QUARTERS, ..., j, :] for j in range(QUARTERS)]
            value = jnp.concatenate(groups_of, axis=-1).astype(bf16)
            ordered.append(jnp.einsum("skczn,nw->kcwsz", value, order[quarter], preferred_element_type=f32))
        return jnp.stack(ordered, axis=2).astype(bf16)

    parts = lax.map(block, jnp.arange(planes // PLANES, dtype=jnp.int32) * PLANES)
    parts = jnp.moveaxis(parts, 0, -2).reshape(KY, CLASSES * NX, 2, planes).astype(f32)
    total = lax.psum_scatter(parts, "img", scatter_dimension=0, tiled=True)
    total = lax.psum_scatter(total, "slab", scatter_dimension=1, tiled=True)
    table = jnp.asarray(z_table(planes).astype(np.float32)).reshape(2, 2, planes, planes)
    scale = 2.5 / math.sqrt(number * owners * groups * NX)
    return scale * jnp.einsum("yqsz,stwz->yqtw", total, table, precision=lax.Precision.HIGHEST)


def on_device(images, pose_bins, labels, defocus):
    owners, groups = lax.axis_size("slab"), lax.axis_size("img")
    number = images.shape[0]
    planes = owners * 4
    if planes != PLANES:
        return many_planes(images, pose_bins, labels, defocus)
    scale = 2.5 / math.sqrt(number * owners * groups * NX)
    x = images.reshape(number, 2, KY, QUARTERS, LANES).transpose(0, 1, 3, 2, 4).reshape(number * 2 * ROWS, LANES)
    pieces = 2 * CLASSES * QUARTERS
    w_shape = jax.ShapeDtypeStruct(x.shape, f32)
    spread_shape = jax.ShapeDtypeStruct((XBINS * CLASSES * PLANES, number), bf16)
    piece_shape = jax.ShapeDtypeStruct((pieces, PLANES, 2 * LANES), bf16)
    table = jnp.asarray(fourier_table())
    table_shape = jax.ShapeDtypeStruct(table.shape, bf16)
    work = [
        pltpu.VMEM((2, number, 2 * NX), bf16),
        pltpu.VMEM((QUARTERS, 4 * CLASSES * PLANES, XBINS * LANES), bf16),
    ]
    other, weighted, spread, near_table = pl.pallas_call(
        functools.partial(first_kernel, planes),
        out_shape=(piece_shape, w_shape, spread_shape, table_shape),
        in_specs=[HBM] * 6,
        out_specs=(VMEM,) * 4,
        scratch_shapes=[
            pltpu.VMEM(x.shape, bf16),
            pltpu.VMEM((1, number), bf16),
            pltpu.VMEM((1, number), jnp.int32),
            pltpu.VMEM((1, number), jnp.int32),
            pltpu.VMEM((ROWS, LANES), f32),
            pltpu.VMEM((number, LANES), f32),
            *work,
            pltpu.SemaphoreType.DMA((CHUNKS + 5,)),
        ],
        compiler_params=pltpu.CompilerParams(vmem_limit_bytes=32 << 20),
        name="weigh_and_transform_other",
    )(*(
        pltpu.with_memory_space_constraint(v, pltpu.HBM)
        for v in (x, defocus[None], pose_bins[None], labels[None], jnp.asarray(turns_per_defocus()), table)
    ))
    got = lax.ppermute(other, "img", partner("img", 1))
    own = pl.pallas_call(
        second_kernel,
        out_shape=piece_shape,
        in_specs=[VMEM] * 3,
        out_specs=VMEM,
        scratch_shapes=work,
        compiler_params=pltpu.CompilerParams(vmem_limit_bytes=16 << 20),
        name="transform_own",
    )(weighted, spread, near_table)
    total = (own.astype(f32) + got.astype(f32)).astype(bf16)
    pieces = [total[3 * 4 : 4 * 4], total[2 * 4 : 3 * 4], total[4 : 2 * 4]]
    flat = owners * groups
    got = [
        lax.ppermute(piece, ("slab", "img"), [(i, i ^ flip) for i in range(flat)])
        for piece, flip in zip(pieces, (6, 4, 2))
    ]
    total = sum((g.astype(f32) for g in got), total[:4].astype(f32)).astype(bf16)
    pieces = [total[1], total[3], total[2]]
    got = [
        lax.ppermute(piece, ("slab", "img"), [(i, i ^ flip) for i in range(flat)])
        for piece, flip in zip(pieces, (8, 24, 16))
    ]
    out = pl.pallas_call(
        functools.partial(last_kernel, scale),
        out_shape=jax.ShapeDtypeStruct((2 * planes, LANES), f32),
        in_specs=[VMEM] * 6,
        out_specs=VMEM,
        compiler_params=pltpu.CompilerParams(vmem_limit_bytes=16 << 20),
        name="transform_planes",
    )(total[0], *got, jnp.asarray(order_table()), jnp.asarray(z_table(planes)))
    return out.reshape(1, 2, planes, LANES).transpose(0, 3, 1, 2)


def solution(mesh):
    placed = (
        P(("slab", "img"), None, None, None),
        P(("slab", "img")),
        P(("slab", "img")),
        P(("slab", "img")),
    )
    return jax.shard_map(
        on_device, mesh=mesh, in_specs=placed, out_specs=P("img", "slab", None, None), check_vma=False
    )
```

time: 25.6 us -> 23.5 us (0.918)
  waiting for transfers between devices: 9.46 us -> 8.09 us
  starting transfers between devices: 9.48 us -> 9.07 us
  Pallas kernels: 6.35 us -> 5.96 us
    ppermute x6, waiting for transfers between devices: 9.45 us -> 8.09 us  [on_device(): lax.ppermute(piece, ('slab', 'img'), [(i, i ^ flip) for i in range(flat)])]
    pallas_call x1, Pallas kernels: 4.45 us -> 3.71 us  [on_device(): pl.pallas_call(functools.partial(first_kernel, planes), out_shape=(piece_...]
    ppermute x6, starting transfers between devices: 8.96 us -> 8.55 us  [on_device(): lax.ppermute(piece, ('slab', 'img'), [(i, i ^ flip) for i in range(flat)])]
  transfers between devices with their start and end apart: 7 -> 7, of which waited for: 5 -> 5; matrix products, arithmetic and copies ran while one was open for 0% -> 0% of each run, Pallas kernels for 4% -> 6%
where the time goes in v2:
time: 23.5 us; the launch traced here: 23.3 us
  starting transfers between devices  9.07 us (39%)
  waiting for transfers between devices  8.09 us (34%)
  Pallas kernels  5.96 us (25%)
    ppermute x6, starting transfers between devices, on_device(): lax.ppermute(piece, ('slab', 'img'), [(i, i ^ flip) for i in range(flat)])  8.55 us
    ppermute x6, waiting for transfers between devices, on_device(): lax.ppermute(piece, ('slab', 'img'), [(i, i ^ flip) for i in range(flat)])  8.09 us
    pallas_call x1, Pallas kernels, on_device(): pl.pallas_call(functools.partial(first_kernel, planes), out_shape=(piece_...  3.71 us
    pallas_call x1, Pallas kernels, on_device(): pl.pallas_call(second_kernel, out_shape=piece_shape, in_specs=[VMEM] * 3,...  1.36 us
    pallas_call x1, Pallas kernels, on_device(): pl.pallas_call(functools.partial(last_kernel, scale), out_shape=jax.Shape...  0.89 us
    ppermute x1, starting transfers between devices, on_device(): got = lax.ppermute(other, 'img', partner('img', 1))  0.52 us
  transfers between devices with their start and end apart: 7, of which 5 were waited for; matrix products, arithmetic and copies ran while one was open for 0% of the time, Pallas kernels for 6%

profile of v2, /device:TPU:0, one launch (start us, length us, event | category | flops | bytes accessed | tf_op | source)
XLA Modules:
  0.0 23.3 jit_solution(4738406395983252939)
XLA Ops:
  0.0 3.7 %weigh_and_transform_other.1 = (bf16[16,32,256]{2,1,0:T(8,128)(2,1)S(1)}, f32[4096,128]{1,0:T(8,128)S(1)}, bf16[256,128]{1,0:T(8,128)(2,1)S(1)}, bf16[4,512,256]{2,1,0:T(8,128)(2,1)S(1)}) custom-call(bf16[4096,128]{1,0:T(8,128)(2,1)} %bitcast.19, bf16[1,128]{1,0:T(2,128)(2,1)} %bitcast.20, s32[1,128]{1,0:T(1,128)} %bitcast.21, s32[1,128]{1,0:T(1,128)} %bitcast.22, ...), custom_call_target="tpu_custom_call" | custom-call | tf_op jit(solution)/shard_map/weigh_and_transform_other/pallas_call | solution.py:299
  3.7 0.5 %collective-permute-start = (bf16[16,32,256]{2,1,0:T(8,128)(2,1)S(1)}, bf16[16,32,256]{2,1,0:T(8,128)(2,1)S(1)}, u32[]{:S(2)}, u32[]{:S(2)}) collective-permute-start(bf16[16,32,256]{2,1,0:T(8,128)(2,1)S(1)} %get-tuple-element.12), channel_id=1, source_target_pairs={{0,1},{1,0},{2,3},{3,2},{4,5},{5,4},{6,7},{7,6},{8,9},{9,8},{10,11... | collective-permute-start | bytes 786440 | tf_op jit(solution)/shard_map/ppermute | solution.py:320
  4.2 0.0 copy-start
  4.2 0.0 copy-start.1
  4.2 1.4 %transform_own.1 = bf16[16,32,256]{2,1,0:T(8,128)(2,1)S(1)} custom-call(f32[4096,128]{1,0:T(8,128)S(1)} %get-tuple-element.9.w_ref, bf16[256,128]{1,0:T(8,128)(2,1)S(1)} %get-tuple-element.10.spread_ref, bf16[4,512,256]{2,1,0:T(8,128)(2,1)S(1)} %get-tuple-element.11.table_ref), custom_call_target="tpu_custom_call" | custom-call | tf_op jit(solution)/shard_map/transform_own/pallas_call | solution.py:321
  5.6 0.0 collective-permute-done
  5.6 0.1 add_convert_fusion
  5.7 3.7 %collective-permute-start.1 = (bf16[4,32,256]{2,1,0:T(8,128)(2,1)S(1)}, bf16[4,32,256]{2,1,0:T(8,128)(2,1)S(1)}, u32[]{:S(2)}, u32[]{:S(2)}) collective-permute-start(bf16[4,32,256]{2,1,0:T(8,128)(2,1)S(1)} %get-tuple-element.13), channel_id=1, source_target_pairs={{0,6},{1,7},{2,4},{3,5},{4,2},{5,3},{6,0},{7,1},{8,14},{9,15},{10,... | collective-permute-start | bytes 196616 | tf_op jit(solution)/shard_map/ppermute | solution.py:334
  9.4 0.5 %collective-permute-start.3 = (bf16[4,32,256]{2,1,0:T(8,128)(2,1)S(1)}, bf16[4,32,256]{2,1,0:T(8,128)(2,1)S(1)}, u32[]{:S(2)}, u32[]{:S(2)}) collective-permute-start(bf16[4,32,256]{2,1,0:T(8,128)(2,1)S(1)} %get-tuple-element.14), channel_id=1, source_target_pairs={{0,2},{1,3},{2,0},{3,1},{4,6},{5,7},{6,4},{7,5},{8,10},{9,11},{10,... | collective-permute-start | bytes 196616 | tf_op jit(solution)/shard_map/ppermute | solution.py:334
  9.9 0.1 collective-permute-start.2
  10.0 2.0 %collective-permute-done.1 = bf16[4,32,256]{2,1,0:T(8,128)(2,1)S(1)} collective-permute-done((bf16[4,32,256]{2,1,0:T(8,128)(2,1)S(1)}, bf16[4,32,256]{2,1,0:T(8,128)(2,1)S(1)}, u32[]{:S(2)}, u32[]{:S(2)}) %collective-permute-start.1) | collective-permute-done | bytes 65568 | tf_op jit(solution)/shard_map/ppermute | solution.py:334
  12.0 1.7 %collective-permute-done.3 = bf16[4,32,256]{2,1,0:T(8,128)(2,1)S(1)} collective-permute-done((bf16[4,32,256]{2,1,0:T(8,128)(2,1)S(1)}, bf16[4,32,256]{2,1,0:T(8,128)(2,1)S(1)}, u32[]{:S(2)}, u32[]{:S(2)}) %collective-permute-start.3) | collective-permute-done | bytes 65568 | tf_op jit(solution)/shard_map/ppermute | solution.py:334
  13.7 0.5 %collective-permute-done.2 = bf16[4,32,256]{2,1,0:T(8,128)(2,1)S(1)} collective-permute-done((bf16[4,32,256]{2,1,0:T(8,128)(2,1)S(1)}, bf16[4,32,256]{2,1,0:T(8,128)(2,1)S(1)}, u32[]{:S(2)}, u32[]{:S(2)}) %collective-permute-start.2) | collective-permute-done | bytes 65568 | tf_op jit(solution)/shard_map/ppermute | solution.py:334
  14.2 2.7 %collective-permute-start.6 = (bf16[32,256]{1,0:T(8,128)(2,1)S(1)}, bf16[32,256]{1,0:T(8,128)(2,1)S(1)}, u32[]{:S(2)}, u32[]{:S(2)}) collective-permute-start(bf16[32,256]{1,0:T(8,128)(2,1)S(1)} %get-tuple-element.16), channel_id=1, source_target_pairs={{0,16},{1,17},{2,18},{3,19},{4,20},{5,21},{6,22},{7,23},{8,24},{9,... | collective-permute-start | bytes 49160 | tf_op jit(solution)/shard_map/ppermute | solution.py:340
  16.9 1.3 %collective-permute-start.5 = (bf16[32,256]{1,0:T(8,128)(2,1)S(1)}, bf16[32,256]{1,0:T(8,128)(2,1)S(1)}, u32[]{:S(2)}, u32[]{:S(2)}) collective-permute-start(bf16[32,256]{1,0:T(8,128)(2,1)S(1)} %get-tuple-element.17), channel_id=1, source_target_pairs={{0,24},{1,25},{2,26},{3,27},{4,28},{5,29},{6,30},{7,31},{8,16},{9,... | collective-permute-start | bytes 49160 | tf_op jit(solution)/shard_map/ppermute | solution.py:340
  18.2 0.2 collective-permute-start.4
  18.5 0.5 %collective-permute-done.6.refs_2_ = bf16[32,256]{1,0:T(8,128)(2,1)S(1)} collective-permute-done((bf16[32,256]{1,0:T(8,128)(2,1)S(1)}, bf16[32,256]{1,0:T(8,128)(2,1)S(1)}, u32[]{:S(2)}, u32[]{:S(2)}) %collective-permute-start.6) | collective-permute-done | bytes 16416 | tf_op jit(solution)/shard_map/ppermute | solution.py:340
  18.9 3.5 %collective-permute-done.5.refs_1_ = bf16[32,256]{1,0:T(8,128)(2,1)S(1)} collective-permute-done((bf16[32,256]{1,0:T(8,128)(2,1)S(1)}, bf16[32,256]{1,0:T(8,128)(2,1)S(1)}, u32[]{:S(2)}, u32[]{:S(2)}) %collective-permute-start.5) | collective-permute-done | bytes 16416 | tf_op jit(solution)/shard_map/ppermute | solution.py:340
  22.4 0.0 collective-permute-done.4.refs_0_
  22.4 0.0 copy-done
  22.4 0.0 copy-done.1
  22.4 0.9 %transform_planes.1 = f32[64,128]{1,0:T(8,128)} custom-call(bf16[32,256]{1,0:T(8,128)(2,1)S(1)} %get-tuple-element.19.kept_ref, bf16[32,256]{1,0:T(8,128)(2,1)S(1)} %collective-permute-done.4.refs_0_, bf16[32,256]{1,0:T(8,128)(2,1)S(1)} %collective-permute-done.5.refs_1_, bf16[32,256]{1,0:T(8,128)(2,1)S(1)} %collective-permute-done.6.refs_2_, ...), custom_call_target="tpu_custom_call" | custom-call | tf_op jit(solution)/shard_map/transform_planes/pallas_call | solution.py:343
  (3 shorter events, 0.1 us)
Async XLA Ops:
  3.7 1.9 %collective-permute-start = (bf16[16,32,256]{2,1,0:T(8,128)(2,1)S(1)}, bf16[16,32,256]{2,1,0:T(8,128)(2,1)S(1)}, u32[]{:S(2)}, u32[]{:S(2)}) collective-permute-start(bf16[16,32,256]{2,1,0:T(8,128)(2,1)S(1)} %get-tuple-element.12), channel_id=1, source_target_pairs={{0,1},{1,0},{2,3},{3,2},{4,5},{5,4},{6,7},{7,6},{8,9},{9,8},{10,11... | collective-permute-start | bytes 786440 | tf_op jit(solution)/shard_map/ppermute | solution.py:320
  4.2 18.2 %copy-start = (bf16[4,128,128]{2,1,0:T(8,128)(2,1)S(1)}, bf16[4,128,128]{2,1,0:T(8,128)(2,1)}, u32[]{:S(2)}) copy-start(bf16[4,128,128]{2,1,0:T(8,128)(2,1)} %constant.10.clone.refs_3_) | copy-start | bytes 393220
  4.2 18.2 %copy-start.1 = (bf16[2,64,32]{2,1,0:T(8,128)(2,1)S(1)}, bf16[2,64,32]{2,1,0:T(8,128)(2,1)}, u32[]{:S(2)}) copy-start(bf16[2,64,32]{2,1,0:T(8,128)(2,1)} %constant.11.clone.refs_4_) | copy-start | bytes 24580
  5.7 6.3 %collective-permute-start.1 = (bf16[4,32,256]{2,1,0:T(8,128)(2,1)S(1)}, bf16[4,32,256]{2,1,0:T(8,128)(2,1)S(1)}, u32[]{:S(2)}, u32[]{:S(2)}) collective-permute-start(bf16[4,32,256]{2,1,0:T(8,128)(2,1)S(1)} %get-tuple-element.13), channel_id=1, source_target_pairs={{0,6},{1,7},{2,4},{3,5},{4,2},{5,3},{6,0},{7,1},{8,14},{9,15},{10,... | collective-permute-start | bytes 196616 | tf_op jit(solution)/shard_map/ppermute | solution.py:334
  9.4 4.3 %collective-permute-start.3 = (bf16[4,32,256]{2,1,0:T(8,128)(2,1)S(1)}, bf16[4,32,256]{2,1,0:T(8,128)(2,1)S(1)}, u32[]{:S(2)}, u32[]{:S(2)}) collective-permute-start(bf16[4,32,256]{2,1,0:T(8,128)(2,1)S(1)} %get-tuple-element.14), channel_id=1, source_target_pairs={{0,2},{1,3},{2,0},{3,1},{4,6},{5,7},{6,4},{7,5},{8,10},{9,11},{10,... | collective-permute-start | bytes 196616 | tf_op jit(solution)/shard_map/ppermute | solution.py:334
  9.9 4.3 %collective-permute-start.2 = (bf16[4,32,256]{2,1,0:T(8,128)(2,1)S(1)}, bf16[4,32,256]{2,1,0:T(8,128)(2,1)S(1)}, u32[]{:S(2)}, u32[]{:S(2)}) collective-permute-start(bf16[4,32,256]{2,1,0:T(8,128)(2,1)S(1)} %get-tuple-element.15), channel_id=1, source_target_pairs={{0,4},{1,5},{2,6},{3,7},{4,0},{5,1},{6,2},{7,3},{8,12},{9,13},{10,... | collective-permute-start | bytes 196616 | tf_op jit(solution)/shard_map/ppermute | solution.py:334
  14.2 4.7 %collective-permute-start.6 = (bf16[32,256]{1,0:T(8,128)(2,1)S(1)}, bf16[32,256]{1,0:T(8,128)(2,1)S(1)}, u32[]{:S(2)}, u32[]{:S(2)}) collective-permute-start(bf16[32,256]{1,0:T(8,128)(2,1)S(1)} %get-tuple-element.16), channel_id=1, source_target_pairs={{0,16},{1,17},{2,18},{3,19},{4,20},{5,21},{6,22},{7,23},{8,24},{9,... | collective-permute-start | bytes 49160 | tf_op jit(solution)/shard_map/ppermute | solution.py:340
  16.9 5.5 %collective-permute-start.5 = (bf16[32,256]{1,0:T(8,128)(2,1)S(1)}, bf16[32,256]{1,0:T(8,128)(2,1)S(1)}, u32[]{:S(2)}, u32[]{:S(2)}) collective-permute-start(bf16[32,256]{1,0:T(8,128)(2,1)S(1)} %get-tuple-element.17), channel_id=1, source_target_pairs={{0,24},{1,25},{2,26},{3,27},{4,28},{5,29},{6,30},{7,31},{8,16},{9,... | collective-permute-start | bytes 49160 | tf_op jit(solution)/shard_map/ppermute | solution.py:340
  18.2 4.2 %collective-permute-start.4 = (bf16[32,256]{1,0:T(8,128)(2,1)S(1)}, bf16[32,256]{1,0:T(8,128)(2,1)S(1)}, u32[]{:S(2)}, u32[]{:S(2)}) collective-permute-start(bf16[32,256]{1,0:T(8,128)(2,1)S(1)} %get-tuple-element.18), channel_id=1, source_target_pairs={{0,8},{1,9},{2,10},{3,11},{4,12},{5,13},{6,14},{7,15},{8,0},{9,1},... | collective-permute-start | bytes 49160 | tf_op jit(solution)/shard_map/ppermute | solution.py:340

commit v3 on v2

--- a/solution.py
+++ b/solution.py
@@ -22,6 +22,7 @@
 CHUNKS = 4
 UNROLL = 8
 ROWS = QUARTERS * KY
+PITCH = 2 * ROWS + 1
 bf16, f32 = jnp.bfloat16, jnp.float32
 
 
@@ -88,7 +89,7 @@
     for y in range(2):
 
         def column(r, p):
-            return w_ref[pl.ds(r * ROWS + p * KY + 2 * y + ky_low, number, stride=2 * ROWS), :]
+            return w_ref[pl.ds(r * ROWS + p * KY + 2 * y + ky_low, number, stride=PITCH), :]
 
         sums = quarter_sums([(column(0, p), column(1, p)) for p in range(QUARTERS)])
         for q in range(QUARTERS):
@@ -188,8 +189,8 @@
         ctf = poly * f
         at = pl.multiple_of(i * 2 * ROWS, 2 * ROWS)
         rows = x_ref[pl.ds(at, 2 * ROWS), :].astype(f32)
-        w_ref[pl.ds(at, ROWS), :] = ctf * rows[:ROWS]
-        w_ref[pl.ds(at + ROWS, ROWS), :] = ctf * rows[ROWS:]
+        w_ref[pl.ds(i * PITCH, ROWS), :] = ctf * rows[:ROWS]
+        w_ref[pl.ds(i * PITCH + ROWS, ROWS), :] = ctf * rows[ROWS:]
         return carry
 
     for c in range(CHUNKS):
@@ -204,11 +205,9 @@
     transform(w_ref, core, spread_ref[...], lambda q: table_ref[q], u_ref, v_ref, place(out_ref))
 
 
-def last_kernel(scale, kept_ref, *refs):
+def last_kernel(scale, *refs):
     *got_refs, order_ref, table_ref, out_ref = refs
-    total = kept_ref[...].astype(f32)
-    for got_ref in got_refs:
-        total += got_ref[...].astype(f32)
+    total = sum(got_ref[...].astype(f32) for got_ref in got_refs)
     total = total.astype(bf16)
     order = order_ref[lax.axis_index("slab") % QUARTERS]
     turned = 0.0
@@ -231,8 +230,15 @@
 HBM = pl.BlockSpec(memory_space=pltpu.HBM)
 
 
-def partner(axis, bit):
-    return [(i, i ^ bit) for i in range(lax.axis_size(axis))]
+FIRST = (1, 1 + 2, 1 + 4, 1 + 2 + 4)
+SECOND = (1, 1 + 8, 1 + 16, 1 + 8 + 16)
+FIRST_ORDER = (3, 2, 1, 0)
+SECOND_ORDER = (0, 1, 3, 2)
+
+
+def passed(piece, flip):
+    flat = lax.axis_size("slab") * lax.axis_size("img")
+    return lax.ppermute(piece, ("slab", "img"), [(i, i ^ flip) for i in range(flat)])
 
 
 def ctf_weights(defocus):
@@ -287,7 +293,7 @@
     scale = 2.5 / math.sqrt(number * owners * groups * NX)
     x = images.reshape(number, 2, KY, QUARTERS, LANES).transpose(0, 1, 3, 2, 4).reshape(number * 2 * ROWS, LANES)
     pieces = 2 * CLASSES * QUARTERS
-    w_shape = jax.ShapeDtypeStruct(x.shape, f32)
+    w_shape = jax.ShapeDtypeStruct((number * PITCH, LANES), f32)
     spread_shape = jax.ShapeDtypeStruct((XBINS * CLASSES * PLANES, number), bf16)
     piece_shape = jax.ShapeDtypeStruct((pieces, PLANES, 2 * LANES), bf16)
     table = jnp.asarray(fourier_table())
@@ -317,7 +323,7 @@
         pltpu.with_memory_space_constraint(v, pltpu.HBM)
         for v in (x, defocus[None], pose_bins[None], labels[None], jnp.asarray(turns_per_defocus()), table)
     ))
-    got = lax.ppermute(other, "img", partner("img", 1))
+    got = passed(other, 1)
     own = pl.pallas_call(
         second_kernel,
         out_shape=piece_shape,
@@ -328,18 +334,9 @@
         name="transform_own",
     )(weighted, spread, near_table)
     total = (own.astype(f32) + got.astype(f32)).astype(bf16)
-    pieces = [total[3 * 4 : 4 * 4], total[2 * 4 : 3 * 4], total[4 : 2 * 4]]
-    flat = owners * groups
-    got = [
-        lax.ppermute(piece, ("slab", "img"), [(i, i ^ flip) for i in range(flat)])
-        for piece, flip in zip(pieces, (6, 4, 2))
-    ]
-    total = sum((g.astype(f32) for g in got), total[:4].astype(f32)).astype(bf16)
-    pieces = [total[1], total[3], total[2]]
-    got = [
-        lax.ppermute(piece, ("slab", "img"), [(i, i ^ flip) for i in range(flat)])
-        for piece, flip in zip(pieces, (8, 24, 16))
-    ]
+    got = [passed(total[4 * group : 4 * group + 4], FIRST[group]) for group in FIRST_ORDER]
+    total = sum(g.astype(f32) for g in got).astype(bf16)
+    got = [passed(total[group], SECOND[group]) for group in SECOND_ORDER]
     out = pl.pallas_call(
         functools.partial(last_kernel, scale),
         out_shape=jax.ShapeDtypeStruct((2 * planes, LANES), f32),
@@ -347,7 +344,7 @@
         out_specs=VMEM,
         compiler_params=pltpu.CompilerParams(vmem_limit_bytes=16 << 20),
         name="transform_planes",
-    )(total[0], *got, jnp.asarray(order_table()), jnp.asarray(z_table(planes)))
+    )(*got, jnp.asarray(order_table()), jnp.asarray(z_table(planes)))
     return out.reshape(1, 2, planes, LANES).transpose(0, 3, 1, 2)
 
 

time: 23.5 us -> 21.3 us (0.906)
  Pallas kernels: 5.96 us -> 4.39 us
  waiting for transfers between devices: 8.09 us -> 7.39 us
    pallas_call x1, Pallas kernels: 3.71 us -> 2.66 us  [on_device(): pl.pallas_call(functools.partial(first_kernel, planes), out_shape=(piece_...]
    ppermute x7 -> x9, waiting for transfers between devices: 8.09 us -> 7.39 us  [passed(): lax.ppermute(piece, ('slab', 'img'), [(i, i ^ flip) for i in range(flat)])]
    pallas_call x1, Pallas kernels: 1.36 us -> 0.84 us  [on_device(): pl.pallas_call(second_kernel, out_shape=piece_shape, in_specs=[VMEM] * 3,...]
    ppermute x7 -> x9, starting transfers between devices: 9.07 us -> 9.16 us  [passed(): lax.ppermute(piece, ('slab', 'img'), [(i, i ^ flip) for i in range(flat)])]
  transfers between devices with their start and end apart: 7 -> 9, of which waited for: 5 -> 5; matrix products, arithmetic and copies ran while one was open for 0% -> 0% of each run, Pallas kernels for 6% -> 4%
where the time goes in v3:
time: 21.3 us; the launch traced here: 21.1 us
  starting transfers between devices  9.16 us (43%)
  waiting for transfers between devices  7.39 us (35%)
  Pallas kernels  4.39 us (21%)
    ppermute x9, starting transfers between devices, passed(): lax.ppermute(piece, ('slab', 'img'), [(i, i ^ flip) for i in range(flat)])  9.16 us
    ppermute x9, waiting for transfers between devices, passed(): lax.ppermute(piece, ('slab', 'img'), [(i, i ^ flip) for i in range(flat)])  7.39 us
    pallas_call x1, Pallas kernels, on_device(): pl.pallas_call(functools.partial(first_kernel, planes), out_shape=(piece_...  2.66 us
    pallas_call x1, Pallas kernels, on_device(): pl.pallas_call(functools.partial(last_kernel, scale), out_shape=jax.Shape...  0.89 us
    pallas_call x1, Pallas kernels, on_device(): pl.pallas_call(second_kernel, out_shape=piece_shape, in_specs=[VMEM] * 3,...  0.84 us
  transfers between devices with their start and end apart: 9, of which 5 were waited for; matrix products, arithmetic and copies ran while one was open for 0% of the time, Pallas kernels for 4%

profile of v3, /device:TPU:0, one launch (start us, length us, event | category | flops | bytes accessed | tf_op | source)
XLA Modules:
  0.0 21.1 jit_solution(2282098800830140251)
XLA Ops:
  0.0 2.7 %weigh_and_transform_other.1 = (bf16[16,32,256]{2,1,0:T(8,128)(2,1)S(1)}, f32[4224,128]{1,0:T(8,128)S(1)}, bf16[256,128]{1,0:T(8,128)(2,1)S(1)}, bf16[4,512,256]{2,1,0:T(8,128)(2,1)S(1)}) custom-call(bf16[4096,128]{1,0:T(8,128)(2,1)} %bitcast.19, bf16[1,128]{1,0:T(2,128)(2,1)} %bitcast.20, s32[1,128]{1,0:T(1,128)} %bitcast.21, s32[1,128]{1,0:T(1,128)} %bitcast.22, ...), custom_call_target="tpu_custom_call" | custom-call | tf_op jit(solution)/shard_map/weigh_and_transform_other/pallas_call | solution.py:305
  2.7 0.5 %collective-permute-start = (bf16[16,32,256]{2,1,0:T(8,128)(2,1)S(1)}, bf16[16,32,256]{2,1,0:T(8,128)(2,1)S(1)}, u32[]{:S(2)}, u32[]{:S(2)}) collective-permute-start(bf16[16,32,256]{2,1,0:T(8,128)(2,1)S(1)} %get-tuple-element.12), channel_id=1, source_target_pairs={{0,1},{1,0},{2,3},{3,2},{4,5},{5,4},{6,7},{7,6},{8,9},{9,8},{10,11... | collective-permute-start | bytes 786440 | tf_op jit(solution)/shard_map/ppermute | solution.py:241
  3.2 0.0 copy-start
  3.2 0.0 copy-start.1
  3.2 0.8 %transform_own.1 = bf16[16,32,256]{2,1,0:T(8,128)(2,1)S(1)} custom-call(f32[4224,128]{1,0:T(8,128)S(1)} %get-tuple-element.9.w_ref, bf16[256,128]{1,0:T(8,128)(2,1)S(1)} %get-tuple-element.10.spread_ref, bf16[4,512,256]{2,1,0:T(8,128)(2,1)S(1)} %get-tuple-element.11.table_ref), custom_call_target="tpu_custom_call" | custom-call | tf_op jit(solution)/shard_map/transform_own/pallas_call | solution.py:327
  4.0 0.3 %collective-permute-done = bf16[16,32,256]{2,1,0:T(8,128)(2,1)S(1)} collective-permute-done((bf16[16,32,256]{2,1,0:T(8,128)(2,1)S(1)}, bf16[16,32,256]{2,1,0:T(8,128)(2,1)S(1)}, u32[]{:S(2)}, u32[]{:S(2)}) %collective-permute-start) | collective-permute-done | bytes 262176 | tf_op jit(solution)/shard_map/ppermute | solution.py:241
  4.4 0.1 add_convert_fusion
  4.5 3.6 %collective-permute-start.1 = (bf16[4,32,256]{2,1,0:T(8,128)(2,1)S(1)}, bf16[4,32,256]{2,1,0:T(8,128)(2,1)S(1)}, u32[]{:S(2)}, u32[]{:S(2)}) collective-permute-start(bf16[4,32,256]{2,1,0:T(8,128)(2,1)S(1)} %get-tuple-element.13), channel_id=1, source_target_pairs={{0,7},{1,6},{2,5},{3,4},{4,3},{5,2},{6,1},{7,0},{8,15},{9,14},{10,... | collective-permute-start | bytes 196616 | tf_op jit(solution)/shard_map/ppermute | solution.py:241
  8.1 0.4 %collective-permute-start.4 = (bf16[4,32,256]{2,1,0:T(8,128)(2,1)S(1)}, bf16[4,32,256]{2,1,0:T(8,128)(2,1)S(1)}, u32[]{:S(2)}, u32[]{:S(2)}) collective-permute-start(bf16[4,32,256]{2,1,0:T(8,128)(2,1)S(1)} %get-tuple-element.14), channel_id=1, source_target_pairs={{0,1},{1,0},{2,3},{3,2},{4,5},{5,4},{6,7},{7,6},{8,9},{9,8},{10,11... | collective-permute-start | bytes 196616 | tf_op jit(solution)/shard_map/ppermute | solution.py:241
  8.5 0.2 %collective-permute-start.3 = (bf16[4,32,256]{2,1,0:T(8,128)(2,1)S(1)}, bf16[4,32,256]{2,1,0:T(8,128)(2,1)S(1)}, u32[]{:S(2)}, u32[]{:S(2)}) collective-permute-start(bf16[4,32,256]{2,1,0:T(8,128)(2,1)S(1)} %get-tuple-element.15), channel_id=1, source_target_pairs={{0,3},{1,2},{2,1},{3,0},{4,7},{5,6},{6,5},{7,4},{8,11},{9,10},{10,... | collective-permute-start | bytes 196616 | tf_op jit(solution)/shard_map/ppermute | solution.py:241
  8.7 0.2 collective-permute-start.2
  8.9 1.8 %collective-permute-done.1 = bf16[4,32,256]{2,1,0:T(8,128)(2,1)S(1)} collective-permute-done((bf16[4,32,256]{2,1,0:T(8,128)(2,1)S(1)}, bf16[4,32,256]{2,1,0:T(8,128)(2,1)S(1)}, u32[]{:S(2)}, u32[]{:S(2)}) %collective-permute-start.1) | collective-permute-done | bytes 65568 | tf_op jit(solution)/shard_map/ppermute | solution.py:241
  10.6 0.0 collective-permute-done.4
  10.6 1.9 %collective-permute-done.3 = bf16[4,32,256]{2,1,0:T(8,128)(2,1)S(1)} collective-permute-done((bf16[4,32,256]{2,1,0:T(8,128)(2,1)S(1)}, bf16[4,32,256]{2,1,0:T(8,128)(2,1)S(1)}, u32[]{:S(2)}, u32[]{:S(2)}) %collective-permute-start.3) | collective-permute-done | bytes 65568 | tf_op jit(solution)/shard_map/ppermute | solution.py:241
  12.5 0.1 collective-permute-done.2
  12.7 2.6 %collective-permute-start.8 = (bf16[32,256]{1,0:T(8,128)(2,1)S(1)}, bf16[32,256]{1,0:T(8,128)(2,1)S(1)}, u32[]{:S(2)}, u32[]{:S(2)}) collective-permute-start(bf16[32,256]{1,0:T(8,128)(2,1)S(1)} %get-tuple-element.17), channel_id=1, source_target_pairs={{0,17},{1,16},{2,19},{3,18},{4,21},{5,20},{6,23},{7,22},{8,25},{9,... | collective-permute-start | bytes 49160 | tf_op jit(solution)/shard_map/ppermute | solution.py:241
  15.2 1.2 %collective-permute-start.7 = (bf16[32,256]{1,0:T(8,128)(2,1)S(1)}, bf16[32,256]{1,0:T(8,128)(2,1)S(1)}, u32[]{:S(2)}, u32[]{:S(2)}) collective-permute-start(bf16[32,256]{1,0:T(8,128)(2,1)S(1)} %get-tuple-element.18), channel_id=1, source_target_pairs={{0,25},{1,24},{2,27},{3,26},{4,29},{5,28},{6,31},{7,30},{8,17},{9,... | collective-permute-start | bytes 49160 | tf_op jit(solution)/shard_map/ppermute | solution.py:241
  16.4 0.2 %collective-permute-start.6 = (bf16[32,256]{1,0:T(8,128)(2,1)S(1)}, bf16[32,256]{1,0:T(8,128)(2,1)S(1)}, u32[]{:S(2)}, u32[]{:S(2)}) collective-permute-start(bf16[32,256]{1,0:T(8,128)(2,1)S(1)} %get-tuple-element.19), channel_id=1, source_target_pairs={{0,9},{1,8},{2,11},{3,10},{4,13},{5,12},{6,15},{7,14},{8,1},{9,0},... | collective-permute-start | bytes 49160 | tf_op jit(solution)/shard_map/ppermute | solution.py:241
  16.6 0.3 %collective-permute-start.5 = (bf16[32,256]{1,0:T(8,128)(2,1)S(1)}, bf16[32,256]{1,0:T(8,128)(2,1)S(1)}, u32[]{:S(2)}, u32[]{:S(2)}) collective-permute-start(bf16[32,256]{1,0:T(8,128)(2,1)S(1)} %get-tuple-element.20), channel_id=1, source_target_pairs={{0,1},{1,0},{2,3},{3,2},{4,5},{5,4},{6,7},{7,6},{8,9},{9,8},{10,11... | collective-permute-start | bytes 49160 | tf_op jit(solution)/shard_map/ppermute | solution.py:241
  16.9 0.0 collective-permute-done.8.refs_3_
  16.9 3.3 %collective-permute-done.7.refs_2_ = bf16[32,256]{1,0:T(8,128)(2,1)S(1)} collective-permute-done((bf16[32,256]{1,0:T(8,128)(2,1)S(1)}, bf16[32,256]{1,0:T(8,128)(2,1)S(1)}, u32[]{:S(2)}, u32[]{:S(2)}) %collective-permute-start.7) | collective-permute-done | bytes 16416 | tf_op jit(solution)/shard_map/ppermute | solution.py:241
  20.2 0.0 collective-permute-done.6.refs_1_
  20.2 0.0 collective-permute-done.5.refs_0_
  20.2 0.0 copy-done
  20.2 0.0 copy-done.1
  20.3 0.9 %transform_planes.1 = f32[64,128]{1,0:T(8,128)} custom-call(bf16[32,256]{1,0:T(8,128)(2,1)S(1)} %collective-permute-done.5.refs_0_, bf16[32,256]{1,0:T(8,128)(2,1)S(1)} %collective-permute-done.6.refs_1_, bf16[32,256]{1,0:T(8,128)(2,1)S(1)} %collective-permute-done.7.refs_2_, bf16[32,256]{1,0:T(8,128)(2,1)S(1)} %collective-permute-done.8.refs_3_, ...), custom_call_target="tpu_custom_call" | custom-call | tf_op jit(solution)/shard_map/transform_planes/pallas_call | solution.py:340
  (3 shorter events, 0.1 us)
Async XLA Ops:
  2.7 1.7 %collective-permute-start = (bf16[16,32,256]{2,1,0:T(8,128)(2,1)S(1)}, bf16[16,32,256]{2,1,0:T(8,128)(2,1)S(1)}, u32[]{:S(2)}, u32[]{:S(2)}) collective-permute-start(bf16[16,32,256]{2,1,0:T(8,128)(2,1)S(1)} %get-tuple-element.12), channel_id=1, source_target_pairs={{0,1},{1,0},{2,3},{3,2},{4,5},{5,4},{6,7},{7,6},{8,9},{9,8},{10,11... | collective-permute-start | bytes 786440 | tf_op jit(solution)/shard_map/ppermute | solution.py:241
  3.2 17.0 %copy-start = (bf16[4,128,128]{2,1,0:T(8,128)(2,1)S(1)}, bf16[4,128,128]{2,1,0:T(8,128)(2,1)}, u32[]{:S(2)}) copy-start(bf16[4,128,128]{2,1,0:T(8,128)(2,1)} %constant.10.clone.refs_4_) | copy-start | bytes 393220
  3.2 17.1 %copy-start.1 = (bf16[2,64,32]{2,1,0:T(8,128)(2,1)S(1)}, bf16[2,64,32]{2,1,0:T(8,128)(2,1)}, u32[]{:S(2)}) copy-start(bf16[2,64,32]{2,1,0:T(8,128)(2,1)} %constant.11.clone.refs_5_) | copy-start | bytes 24580
  4.5 6.1 %collective-permute-start.1 = (bf16[4,32,256]{2,1,0:T(8,128)(2,1)S(1)}, bf16[4,32,256]{2,1,0:T(8,128)(2,1)S(1)}, u32[]{:S(2)}, u32[]{:S(2)}) collective-permute-start(bf16[4,32,256]{2,1,0:T(8,128)(2,1)S(1)} %get-tuple-element.13), channel_id=1, source_target_pairs={{0,7},{1,6},{2,5},{3,4},{4,3},{5,2},{6,1},{7,0},{8,15},{9,14},{10,... | collective-permute-start | bytes 196616 | tf_op jit(solution)/shard_map/ppermute | solution.py:241
  8.1 2.5 %collective-permute-start.4 = (bf16[4,32,256]{2,1,0:T(8,128)(2,1)S(1)}, bf16[4,32,256]{2,1,0:T(8,128)(2,1)S(1)}, u32[]{:S(2)}, u32[]{:S(2)}) collective-permute-start(bf16[4,32,256]{2,1,0:T(8,128)(2,1)S(1)} %get-tuple-element.14), channel_id=1, source_target_pairs={{0,1},{1,0},{2,3},{3,2},{4,5},{5,4},{6,7},{7,6},{8,9},{9,8},{10,11... | collective-permute-start | bytes 196616 | tf_op jit(solution)/shard_map/ppermute | solution.py:241
  8.5 4.1 %collective-permute-start.3 = (bf16[4,32,256]{2,1,0:T(8,128)(2,1)S(1)}, bf16[4,32,256]{2,1,0:T(8,128)(2,1)S(1)}, u32[]{:S(2)}, u32[]{:S(2)}) collective-permute-start(bf16[4,32,256]{2,1,0:T(8,128)(2,1)S(1)} %get-tuple-element.15), channel_id=1, source_target_pairs={{0,3},{1,2},{2,1},{3,0},{4,7},{5,6},{6,5},{7,4},{8,11},{9,10},{10,... | collective-permute-start | bytes 196616 | tf_op jit(solution)/shard_map/ppermute | solution.py:241
  8.7 3.9 %collective-permute-start.2 = (bf16[4,32,256]{2,1,0:T(8,128)(2,1)S(1)}, bf16[4,32,256]{2,1,0:T(8,128)(2,1)S(1)}, u32[]{:S(2)}, u32[]{:S(2)}) collective-permute-start(bf16[4,32,256]{2,1,0:T(8,128)(2,1)S(1)} %get-tuple-element.16), channel_id=1, source_target_pairs={{0,5},{1,4},{2,7},{3,6},{4,1},{5,0},{6,3},{7,2},{8,13},{9,12},{10,... | collective-permute-start | bytes 196616 | tf_op jit(solution)/shard_map/ppermute | solution.py:241
  12.7 4.2 %collective-permute-start.8 = (bf16[32,256]{1,0:T(8,128)(2,1)S(1)}, bf16[32,256]{1,0:T(8,128)(2,1)S(1)}, u32[]{:S(2)}, u32[]{:S(2)}) collective-permute-start(bf16[32,256]{1,0:T(8,128)(2,1)S(1)} %get-tuple-element.17), channel_id=1, source_target_pairs={{0,17},{1,16},{2,19},{3,18},{4,21},{5,20},{6,23},{7,22},{8,25},{9,... | collective-permute-start | bytes 49160 | tf_op jit(solution)/shard_map/ppermute | solution.py:241
  15.2 5.0 %collective-permute-start.7 = (bf16[32,256]{1,0:T(8,128)(2,1)S(1)}, bf16[32,256]{1,0:T(8,128)(2,1)S(1)}, u32[]{:S(2)}, u32[]{:S(2)}) collective-permute-start(bf16[32,256]{1,0:T(8,128)(2,1)S(1)} %get-tuple-element.18), channel_id=1, source_target_pairs={{0,25},{1,24},{2,27},{3,26},{4,29},{5,28},{6,31},{7,30},{8,17},{9,... | collective-permute-start | bytes 49160 | tf_op jit(solution)/shard_map/ppermute | solution.py:241
  16.4 3.8 %collective-permute-start.6 = (bf16[32,256]{1,0:T(8,128)(2,1)S(1)}, bf16[32,256]{1,0:T(8,128)(2,1)S(1)}, u32[]{:S(2)}, u32[]{:S(2)}) collective-permute-start(bf16[32,256]{1,0:T(8,128)(2,1)S(1)} %get-tuple-element.19), channel_id=1, source_target_pairs={{0,9},{1,8},{2,11},{3,10},{4,13},{5,12},{6,15},{7,14},{8,1},{9,0},... | collective-permute-start | bytes 49160 | tf_op jit(solution)/shard_map/ppermute | solution.py:241
  16.6 3.6 %collective-permute-start.5 = (bf16[32,256]{1,0:T(8,128)(2,1)S(1)}, bf16[32,256]{1,0:T(8,128)(2,1)S(1)}, u32[]{:S(2)}, u32[]{:S(2)}) collective-permute-start(bf16[32,256]{1,0:T(8,128)(2,1)S(1)} %get-tuple-element.20), channel_id=1, source_target_pairs={{0,1},{1,0},{2,3},{3,2},{4,5},{5,4},{6,7},{7,6},{8,9},{9,8},{10,11... | collective-permute-start | bytes 49160 | tf_op jit(solution)/shard_map/ppermute | solution.py:241

commit v4 on v3

--- a/solution.py
+++ b/solution.py
@@ -71,9 +71,12 @@
     return np.linalg.lstsq(basis, np.sin(2 * np.pi * f), rcond=None)[0].astype(np.float32)
 
 
-def device_bits():
-    slab, img = lax.axis_index("slab"), lax.axis_index("img")
-    return img // 2, slab % 2, slab // 2 % 2, slab // 4
+def slot_of(schedule, here, there):
+    slots = [[row[at] for row in schedule].index(there) for at in range(4)]
+    slot = jnp.int32(slots[0])
+    for at in range(1, 4):
+        slot = jnp.where(here == at, slots[at], slot)
+    return slot
 
 
 def quarter_sums(parts):
@@ -141,11 +144,13 @@
 
 
 def place(out_ref):
-    my_y, my_x, my_z, my_class = device_bits()
-
-    def put(y, cls, q, value):
-        index = ((q % 2) ^ my_x) * 8 + (y ^ my_y) * 4 + (cls ^ my_class) * 2 + ((q // 2) ^ my_z)
-        out_ref[index] = value
+    slab, img = lax.axis_index("slab"), lax.axis_index("img")
+    here = slab % 2 * 2 + img // 2
+    first = [slot_of(FIRST, here, there) for there in range(4)]
+    second = [slot_of(SECOND, slab // 2, there) for there in range(4)]
+
+    def put(y, cls, quarter, value):
+        out_ref[first[quarter % 2 * 2 + y] * 4 + second[cls * 2 + quarter // 2]] = value
 
     return put
 
@@ -230,15 +235,23 @@
 HBM = pl.BlockSpec(memory_space=pltpu.HBM)
 
 
-FIRST = (1, 1 + 2, 1 + 4, 1 + 2 + 4)
-SECOND = (1, 1 + 8, 1 + 16, 1 + 8 + 16)
-FIRST_ORDER = (3, 2, 1, 0)
-SECOND_ORDER = (0, 1, 3, 2)
-
-
-def passed(piece, flip):
-    flat = lax.axis_size("slab") * lax.axis_size("img")
-    return lax.ppermute(piece, ("slab", "img"), [(i, i ^ flip) for i in range(flat)])
+FIRST = ((1, 0, 2, 3), (2, 3, 1, 0), (3, 2, 0, 1), (0, 1, 3, 2))
+SECOND = ((1, 2, 0, 3), (2, 1, 3, 0), (3, 0, 2, 1), (0, 3, 1, 2))
+FIRST_LISTED = (0, 3, 2, 1)
+SECOND_LISTED = (3, 2, 1, 0)
+
+
+def pairs_of(stage, slot):
+    pairs = []
+    for source in range(32):
+        core, y, x, z = source & 1, source >> 1 & 1, source >> 2 & 1, source >> 3
+        if stage == 0:
+            to = FIRST[slot][2 * x + y]
+            x, y = to >> 1, to & 1
+        else:
+            z = SECOND[slot][z]
+        pairs.append((source, z << 3 | x << 2 | y << 1 | 1 - core))
+    return pairs
 
 
 def ctf_weights(defocus):
@@ -323,7 +336,8 @@
         pltpu.with_memory_space_constraint(v, pltpu.HBM)
         for v in (x, defocus[None], pose_bins[None], labels[None], jnp.asarray(turns_per_defocus()), table)
     ))
-    got = passed(other, 1)
+    axes = ("slab", "img")
+    got = lax.ppermute(other, axes, [(i, i ^ 1) for i in range(owners * groups)])
     own = pl.pallas_call(
         second_kernel,
         out_shape=piece_shape,
@@ -334,9 +348,9 @@
         name="transform_own",
     )(weighted, spread, near_table)
     total = (own.astype(f32) + got.astype(f32)).astype(bf16)
-    got = [passed(total[4 * group : 4 * group + 4], FIRST[group]) for group in FIRST_ORDER]
+    got = [lax.ppermute(total[4 * slot : 4 * slot + 4], axes, pairs_of(0, slot)) for slot in FIRST_LISTED]
     total = sum(g.astype(f32) for g in got).astype(bf16)
-    got = [passed(total[group], SECOND[group]) for group in SECOND_ORDER]
+    got = [lax.ppermute(total[slot], axes, pairs_of(1, slot)) for slot in SECOND_LISTED]
     out = pl.pallas_call(
         functools.partial(last_kernel, scale),
         out_shape=jax.ShapeDtypeStruct((2 * planes, LANES), f32),

time: 21.3 us -> 20.1 us (0.944)
  waiting for transfers between devices: 7.39 us -> 3.83 us
  starting transfers between devices: 9.16 us -> 11.5 us
    ppermute x9, waiting for transfers between devices: 7.39 us -> 3.83 us  [the longest x4 2.27 us: on_device(): lax.ppermute(total[4 * slot:4 * slot + 4], axes, pairs_of(0, slot))]
    ppermute x9, starting transfers between devices: 9.16 us -> 11.5 us  [the longest x4 5.71 us: on_device(): lax.ppermute(total[4 * slot:4 * slot + 4], axes, pairs_of(0, slot))]
where the time goes in v4:
time: 20.1 us; the launch traced here: 20 us
  starting transfers between devices  11.5 us (57%)
  Pallas kernels  4.39 us (22%)
  waiting for transfers between devices  3.83 us (19%)
    ppermute x4, starting transfers between devices, on_device(): lax.ppermute(total[4 * slot:4 * slot + 4], axes, pairs_of(0, slot))  5.71 us
    ppermute x4, starting transfers between devices, on_device(): lax.ppermute(total[slot], axes, pairs_of(1, slot))  5.28 us
    pallas_call x1, Pallas kernels, on_device(): pl.pallas_call(functools.partial(first_kernel, planes), out_shape=(piece_...  2.67 us
    ppermute x4, waiting for transfers between devices, on_device(): lax.ppermute(total[4 * slot:4 * slot + 4], axes, pairs_of(0, slot))  2.27 us
    ppermute x4, waiting for transfers between devices, on_device(): lax.ppermute(total[slot], axes, pairs_of(1, slot))  1.25 us
    pallas_call x1, Pallas kernels, on_device(): pl.pallas_call(functools.partial(last_kernel, scale), out_shape=jax.Shape...  0.89 us
    pallas_call x1, Pallas kernels, on_device(): pl.pallas_call(second_kernel, out_shape=piece_shape, in_specs=[VMEM] * 3,...  0.84 us
    ppermute x1, starting transfers between devices, on_device(): lax.ppermute(other, axes, [(i, i ^ 1) for i in range(owners * groups)])  0.52 us
  transfers between devices with their start and end apart: 9, of which 5 were waited for; matrix products, arithmetic and copies ran while one was open for 0% of the time, Pallas kernels for 4%

profile of v4, /device:TPU:0, one launch (start us, length us, event | category | flops | bytes accessed | tf_op | source)
XLA Modules:
  0.0 20.0 jit_solution(15333447527979289849)
XLA Ops:
  0.0 2.7 %weigh_and_transform_other.1 = (bf16[16,32,256]{2,1,0:T(8,128)(2,1)S(1)}, f32[4224,128]{1,0:T(8,128)S(1)}, bf16[256,128]{1,0:T(8,128)(2,1)S(1)}, bf16[4,512,256]{2,1,0:T(8,128)(2,1)S(1)}) custom-call(bf16[4096,128]{1,0:T(8,128)(2,1)} %bitcast.19, bf16[1,128]{1,0:T(2,128)(2,1)} %bitcast.20, s32[1,128]{1,0:T(1,128)} %bitcast.21, s32[1,128]{1,0:T(1,128)} %bitcast.22, ...), custom_call_target="tpu_custom_call" | custom-call | tf_op jit(solution)/shard_map/weigh_and_transform_other/pallas_call | solution.py:318
  2.7 0.5 %collective-permute-start = (bf16[16,32,256]{2,1,0:T(8,128)(2,1)S(1)}, bf16[16,32,256]{2,1,0:T(8,128)(2,1)S(1)}, u32[]{:S(2)}, u32[]{:S(2)}) collective-permute-start(bf16[16,32,256]{2,1,0:T(8,128)(2,1)S(1)} %get-tuple-element.12), channel_id=1, source_target_pairs={{0,1},{1,0},{2,3},{3,2},{4,5},{5,4},{6,7},{7,6},{8,9},{9,8},{10,11... | collective-permute-start | bytes 786440 | tf_op jit(solution)/shard_map/ppermute | solution.py:340
  3.2 0.0 copy-start
  3.2 0.0 copy-start.1
  3.2 0.8 %transform_own.1 = bf16[16,32,256]{2,1,0:T(8,128)(2,1)S(1)} custom-call(f32[4224,128]{1,0:T(8,128)S(1)} %get-tuple-element.9.w_ref, bf16[256,128]{1,0:T(8,128)(2,1)S(1)} %get-tuple-element.10.spread_ref, bf16[4,512,256]{2,1,0:T(8,128)(2,1)S(1)} %get-tuple-element.11.table_ref), custom_call_target="tpu_custom_call" | custom-call | tf_op jit(solution)/shard_map/transform_own/pallas_call | solution.py:341
  4.0 0.3 %collective-permute-done = bf16[16,32,256]{2,1,0:T(8,128)(2,1)S(1)} collective-permute-done((bf16[16,32,256]{2,1,0:T(8,128)(2,1)S(1)}, bf16[16,32,256]{2,1,0:T(8,128)(2,1)S(1)}, u32[]{:S(2)}, u32[]{:S(2)}) %collective-permute-start) | collective-permute-done | bytes 262176 | tf_op jit(solution)/shard_map/ppermute | solution.py:340
  4.4 0.1 add_convert_fusion
  4.5 2.7 %collective-permute-start.1 = (bf16[4,32,256]{2,1,0:T(8,128)(2,1)S(1)}, bf16[4,32,256]{2,1,0:T(8,128)(2,1)S(1)}, u32[]{:S(2)}, u32[]{:S(2)}) collective-permute-start(bf16[4,32,256]{2,1,0:T(8,128)(2,1)S(1)} %get-tuple-element.13), channel_id=1, source_target_pairs={{0,3},{1,2},{2,1},{3,0},{4,5},{5,4},{6,7},{7,6},{8,11},{9,10},{10,... | collective-permute-start | bytes 196616 | tf_op jit(solution)/shard_map/ppermute | solution.py:351
  7.2 0.3 %collective-permute-start.4 = (bf16[4,32,256]{2,1,0:T(8,128)(2,1)S(1)}, bf16[4,32,256]{2,1,0:T(8,128)(2,1)S(1)}, u32[]{:S(2)}, u32[]{:S(2)}) collective-permute-start(bf16[4,32,256]{2,1,0:T(8,128)(2,1)S(1)} %get-tuple-element.14), channel_id=1, source_target_pairs={{0,5},{1,4},{2,7},{3,6},{4,3},{5,2},{6,1},{7,0},{8,13},{9,12},{10,... | collective-permute-start | bytes 196616 | tf_op jit(solution)/shard_map/ppermute | solution.py:351
  7.5 2.3 %collective-permute-start.3 = (bf16[4,32,256]{2,1,0:T(8,128)(2,1)S(1)}, bf16[4,32,256]{2,1,0:T(8,128)(2,1)S(1)}, u32[]{:S(2)}, u32[]{:S(2)}) collective-permute-start(bf16[4,32,256]{2,1,0:T(8,128)(2,1)S(1)} %get-tuple-element.15), channel_id=1, source_target_pairs={{0,7},{1,6},{2,5},{3,4},{4,1},{5,0},{6,3},{7,2},{8,15},{9,14},{10,... | collective-permute-start | bytes 196616 | tf_op jit(solution)/shard_map/ppermute | solution.py:351
  9.8 0.4 %collective-permute-start.2 = (bf16[4,32,256]{2,1,0:T(8,128)(2,1)S(1)}, bf16[4,32,256]{2,1,0:T(8,128)(2,1)S(1)}, u32[]{:S(2)}, u32[]{:S(2)}) collective-permute-start(bf16[4,32,256]{2,1,0:T(8,128)(2,1)S(1)} %get-tuple-element.16), channel_id=1, source_target_pairs={{0,1},{1,0},{2,3},{3,2},{4,7},{5,6},{6,5},{7,4},{8,9},{9,8},{10,11... | collective-permute-start | bytes 196616 | tf_op jit(solution)/shard_map/ppermute | solution.py:351
  10.2 0.5 %collective-permute-done.1 = bf16[4,32,256]{2,1,0:T(8,128)(2,1)S(1)} collective-permute-done((bf16[4,32,256]{2,1,0:T(8,128)(2,1)S(1)}, bf16[4,32,256]{2,1,0:T(8,128)(2,1)S(1)}, u32[]{:S(2)}, u32[]{:S(2)}) %collective-permute-start.1) | collective-permute-done | bytes 65568 | tf_op jit(solution)/shard_map/ppermute | solution.py:351
  10.7 1.3 %collective-permute-done.4 = bf16[4,32,256]{2,1,0:T(8,128)(2,1)S(1)} collective-permute-done((bf16[4,32,256]{2,1,0:T(8,128)(2,1)S(1)}, bf16[4,32,256]{2,1,0:T(8,128)(2,1)S(1)}, u32[]{:S(2)}, u32[]{:S(2)}) %collective-permute-start.4) | collective-permute-done | bytes 65568 | tf_op jit(solution)/shard_map/ppermute | solution.py:351
  12.0 0.5 %collective-permute-done.3 = bf16[4,32,256]{2,1,0:T(8,128)(2,1)S(1)} collective-permute-done((bf16[4,32,256]{2,1,0:T(8,128)(2,1)S(1)}, bf16[4,32,256]{2,1,0:T(8,128)(2,1)S(1)}, u32[]{:S(2)}, u32[]{:S(2)}) %collective-permute-start.3) | collective-permute-done | bytes 65568 | tf_op jit(solution)/shard_map/ppermute | solution.py:351
  12.4 0.0 collective-permute-done.2
  12.5 1.5 %collective-permute-start.8 = (bf16[32,256]{1,0:T(8,128)(2,1)S(1)}, bf16[32,256]{1,0:T(8,128)(2,1)S(1)}, u32[]{:S(2)}, u32[]{:S(2)}) collective-permute-start(bf16[32,256]{1,0:T(8,128)(2,1)S(1)} %get-tuple-element.17), channel_id=1, source_target_pairs={{0,9},{1,8},{2,11},{3,10},{4,13},{5,12},{6,15},{7,14},{8,17},{9,16... | collective-permute-start | bytes 49160 | tf_op jit(solution)/shard_map/ppermute | solution.py:353
  14.1 1.1 %collective-permute-start.7 = (bf16[32,256]{1,0:T(8,128)(2,1)S(1)}, bf16[32,256]{1,0:T(8,128)(2,1)S(1)}, u32[]{:S(2)}, u32[]{:S(2)}) collective-permute-start(bf16[32,256]{1,0:T(8,128)(2,1)S(1)} %get-tuple-element.18), channel_id=1, source_target_pairs={{0,17},{1,16},{2,19},{3,18},{4,21},{5,20},{6,23},{7,22},{8,9},{9,8... | collective-permute-start | bytes 49160 | tf_op jit(solution)/shard_map/ppermute | solution.py:353
  15.2 2.4 %collective-permute-start.6 = (bf16[32,256]{1,0:T(8,128)(2,1)S(1)}, bf16[32,256]{1,0:T(8,128)(2,1)S(1)}, u32[]{:S(2)}, u32[]{:S(2)}) collective-permute-start(bf16[32,256]{1,0:T(8,128)(2,1)S(1)} %get-tuple-element.19), channel_id=1, source_target_pairs={{0,25},{1,24},{2,27},{3,26},{4,29},{5,28},{6,31},{7,30},{8,1},{9,0... | collective-permute-start | bytes 49160 | tf_op jit(solution)/shard_map/ppermute | solution.py:353
  17.6 0.2 collective-permute-start.5
  17.8 0.0 collective-permute-done.8.refs_3_
  17.8 1.2 %collective-permute-done.7.refs_2_ = bf16[32,256]{1,0:T(8,128)(2,1)S(1)} collective-permute-done((bf16[32,256]{1,0:T(8,128)(2,1)S(1)}, bf16[32,256]{1,0:T(8,128)(2,1)S(1)}, u32[]{:S(2)}, u32[]{:S(2)}) %collective-permute-start.7) | collective-permute-done | bytes 16416 | tf_op jit(solution)/shard_map/ppermute | solution.py:353
  19.0 0.0 collective-permute-done.6.refs_1_
  19.0 0.0 collective-permute-done.5.refs_0_
  19.0 0.0 copy-done
  19.1 0.0 copy-done.1
  19.1 0.9 %transform_planes.1 = f32[64,128]{1,0:T(8,128)} custom-call(bf16[32,256]{1,0:T(8,128)(2,1)S(1)} %collective-permute-done.5.refs_0_, bf16[32,256]{1,0:T(8,128)(2,1)S(1)} %collective-permute-done.6.refs_1_, bf16[32,256]{1,0:T(8,128)(2,1)S(1)} %collective-permute-done.7.refs_2_, bf16[32,256]{1,0:T(8,128)(2,1)S(1)} %collective-permute-done.8.refs_3_, ...), custom_call_target="tpu_custom_call" | custom-call | tf_op jit(solution)/shard_map/transform_planes/pallas_call | solution.py:354
  (3 shorter events, 0.1 us)
Async XLA Ops:
  2.7 1.7 %collective-permute-start = (bf16[16,32,256]{2,1,0:T(8,128)(2,1)S(1)}, bf16[16,32,256]{2,1,0:T(8,128)(2,1)S(1)}, u32[]{:S(2)}, u32[]{:S(2)}) collective-permute-start(bf16[16,32,256]{2,1,0:T(8,128)(2,1)S(1)} %get-tuple-element.12), channel_id=1, source_target_pairs={{0,1},{1,0},{2,3},{3,2},{4,5},{5,4},{6,7},{7,6},{8,9},{9,8},{10,11... | collective-permute-start | bytes 786440 | tf_op jit(solution)/shard_map/ppermute | solution.py:340
  3.2 15.9 %copy-start = (bf16[4,128,128]{2,1,0:T(8,128)(2,1)S(1)}, bf16[4,128,128]{2,1,0:T(8,128)(2,1)}, u32[]{:S(2)}) copy-start(bf16[4,128,128]{2,1,0:T(8,128)(2,1)} %constant.10.clone.refs_4_) | copy-start | bytes 393220
  3.2 15.9 %copy-start.1 = (bf16[2,64,32]{2,1,0:T(8,128)(2,1)S(1)}, bf16[2,64,32]{2,1,0:T(8,128)(2,1)}, u32[]{:S(2)}) copy-start(bf16[2,64,32]{2,1,0:T(8,128)(2,1)} %constant.11.clone.refs_5_) | copy-start | bytes 24580
  4.5 6.2 %collective-permute-start.1 = (bf16[4,32,256]{2,1,0:T(8,128)(2,1)S(1)}, bf16[4,32,256]{2,1,0:T(8,128)(2,1)S(1)}, u32[]{:S(2)}, u32[]{:S(2)}) collective-permute-start(bf16[4,32,256]{2,1,0:T(8,128)(2,1)S(1)} %get-tuple-element.13), channel_id=1, source_target_pairs={{0,3},{1,2},{2,1},{3,0},{4,5},{5,4},{6,7},{7,6},{8,11},{9,10},{10,... | collective-permute-start | bytes 196616 | tf_op jit(solution)/shard_map/ppermute | solution.py:351
  7.2 4.8 %collective-permute-start.4 = (bf16[4,32,256]{2,1,0:T(8,128)(2,1)S(1)}, bf16[4,32,256]{2,1,0:T(8,128)(2,1)S(1)}, u32[]{:S(2)}, u32[]{:S(2)}) collective-permute-start(bf16[4,32,256]{2,1,0:T(8,128)(2,1)S(1)} %get-tuple-element.14), channel_id=1, source_target_pairs={{0,5},{1,4},{2,7},{3,6},{4,3},{5,2},{6,1},{7,0},{8,13},{9,12},{10,... | collective-permute-start | bytes 196616 | tf_op jit(solution)/shard_map/ppermute | solution.py:351
  7.5 4.9 %collective-permute-start.3 = (bf16[4,32,256]{2,1,0:T(8,128)(2,1)S(1)}, bf16[4,32,256]{2,1,0:T(8,128)(2,1)S(1)}, u32[]{:S(2)}, u32[]{:S(2)}) collective-permute-start(bf16[4,32,256]{2,1,0:T(8,128)(2,1)S(1)} %get-tuple-element.15), channel_id=1, source_target_pairs={{0,7},{1,6},{2,5},{3,4},{4,1},{5,0},{6,3},{7,2},{8,15},{9,14},{10,... | collective-permute-start | bytes 196616 | tf_op jit(solution)/shard_map/ppermute | solution.py:351
  9.8 2.6 %collective-permute-start.2 = (bf16[4,32,256]{2,1,0:T(8,128)(2,1)S(1)}, bf16[4,32,256]{2,1,0:T(8,128)(2,1)S(1)}, u32[]{:S(2)}, u32[]{:S(2)}) collective-permute-start(bf16[4,32,256]{2,1,0:T(8,128)(2,1)S(1)} %get-tuple-element.16), channel_id=1, source_target_pairs={{0,1},{1,0},{2,3},{3,2},{4,7},{5,6},{6,5},{7,4},{8,9},{9,8},{10,11... | collective-permute-start | bytes 196616 | tf_op jit(solution)/shard_map/ppermute | solution.py:351
  12.5 5.3 %collective-permute-start.8 = (bf16[32,256]{1,0:T(8,128)(2,1)S(1)}, bf16[32,256]{1,0:T(8,128)(2,1)S(1)}, u32[]{:S(2)}, u32[]{:S(2)}) collective-permute-start(bf16[32,256]{1,0:T(8,128)(2,1)S(1)} %get-tuple-element.17), channel_id=1, source_target_pairs={{0,9},{1,8},{2,11},{3,10},{4,13},{5,12},{6,15},{7,14},{8,17},{9,16... | collective-permute-start | bytes 49160 | tf_op jit(solution)/shard_map/ppermute | solution.py:353
  14.1 5.0 %collective-permute-start.7 = (bf16[32,256]{1,0:T(8,128)(2,1)S(1)}, bf16[32,256]{1,0:T(8,128)(2,1)S(1)}, u32[]{:S(2)}, u32[]{:S(2)}) collective-permute-start(bf16[32,256]{1,0:T(8,128)(2,1)S(1)} %get-tuple-element.18), channel_id=1, source_target_pairs={{0,17},{1,16},{2,19},{3,18},{4,21},{5,20},{6,23},{7,22},{8,9},{9,8... | collective-permute-start | bytes 49160 | tf_op jit(solution)/shard_map/ppermute | solution.py:353
  15.2 3.8 %collective-permute-start.6 = (bf16[32,256]{1,0:T(8,128)(2,1)S(1)}, bf16[32,256]{1,0:T(8,128)(2,1)S(1)}, u32[]{:S(2)}, u32[]{:S(2)}) collective-permute-start(bf16[32,256]{1,0:T(8,128)(2,1)S(1)} %get-tuple-element.19), channel_id=1, source_target_pairs={{0,25},{1,24},{2,27},{3,26},{4,29},{5,28},{6,31},{7,30},{8,1},{9,0... | collective-permute-start | bytes 49160 | tf_op jit(solution)/shard_map/ppermute | solution.py:353
  17.6 1.4 %collective-permute-start.5 = (bf16[32,256]{1,0:T(8,128)(2,1)S(1)}, bf16[32,256]{1,0:T(8,128)(2,1)S(1)}, u32[]{:S(2)}, u32[]{:S(2)}) collective-permute-start(bf16[32,256]{1,0:T(8,128)(2,1)S(1)} %get-tuple-element.20), channel_id=1, source_target_pairs={{0,1},{1,0},{2,3},{3,2},{4,5},{5,4},{6,7},{7,6},{8,25},{9,24},{10,... | collective-permute-start | bytes 49160 | tf_op jit(solution)/shard_map/ppermute | solution.py:353

commit v5 on v4

--- a/solution.py
+++ b/solution.py
@@ -143,14 +143,19 @@
     return out.astype(bf16)
 
 
-def place(out_ref):
+def place(out_ref, core):
     slab, img = lax.axis_index("slab"), lax.axis_index("img")
-    here = slab % 2 * 2 + img // 2
-    first = [slot_of(FIRST, here, there) for there in range(4)]
-    second = [slot_of(SECOND, slab // 2, there) for there in range(4)]
+    here, plane = slab % 2 * 2 + img // 2, slab // 2
+    first = [
+        jnp.where(core == 0, slot_of(FIRST[0], here, there), slot_of(FIRST[1], here, there)) for there in range(4)
+    ]
+    second = {
+        schedule: [slot_of(schedule, plane, there) for there in range(4)] for schedule in dict.fromkeys(SECOND)
+    }
 
     def put(y, cls, quarter, value):
-        out_ref[first[quarter % 2 * 2 + y] * 4 + second[cls * 2 + quarter // 2]] = value
+        there = quarter % 2 * 2 + y
+        out_ref[first[there] * 4 + second[SECOND[there]][cls * 2 + quarter // 2]] = value
 
     return put
 
@@ -202,12 +207,12 @@
         parts[c].wait()
         lax.fori_loop(c * number // CHUNKS, (c + 1) * number // CHUNKS, weigh, 0, unroll=UNROLL)
     table.wait()
-    transform(w_ref, 1 - core, spread_ref[...], lambda q: table_ref[q], u_ref, v_ref, place(out_ref))
+    transform(w_ref, 1 - core, spread_ref[...], lambda q: table_ref[q], u_ref, v_ref, place(out_ref, 1 - core))
 
 
 def second_kernel(w_ref, spread_ref, table_ref, out_ref, u_ref, v_ref):
     core = lax.axis_index("img") % 2
-    transform(w_ref, core, spread_ref[...], lambda q: table_ref[q], u_ref, v_ref, place(out_ref))
+    transform(w_ref, core, spread_ref[...], lambda q: table_ref[q], u_ref, v_ref, place(out_ref, core))
 
 
 def last_kernel(scale, *refs):
@@ -235,8 +240,9 @@
 HBM = pl.BlockSpec(memory_space=pltpu.HBM)
 
 
-FIRST = ((1, 0, 2, 3), (2, 3, 1, 0), (3, 2, 0, 1), (0, 1, 3, 2))
-SECOND = ((1, 2, 0, 3), (2, 1, 3, 0), (3, 0, 2, 1), (0, 3, 1, 2))
+FIRST = (((1, 0, 2, 3), (2, 3, 1, 0), (3, 2, 0, 1), (0, 1, 3, 2)),) * 2
+USUAL = ((1, 2, 0, 3), (2, 1, 3, 0), (3, 0, 2, 1), (0, 3, 1, 2))
+SECOND = (((1, 3, 2, 0), (2, 1, 0, 3), (3, 0, 1, 2), (0, 2, 3, 1)), USUAL, USUAL, USUAL)
 FIRST_LISTED = (0, 3, 2, 1)
 SECOND_LISTED = (3, 2, 1, 0)
 
@@ -246,10 +252,10 @@
     for source in range(32):
         core, y, x, z = source & 1, source >> 1 & 1, source >> 2 & 1, source >> 3
         if stage == 0:
-            to = FIRST[slot][2 * x + y]
+            to = FIRST[core][slot][2 * x + y]
             x, y = to >> 1, to & 1
         else:
-            z = SECOND[slot][z]
+            z = SECOND[2 * x + y][slot][z]
         pairs.append((source, z << 3 | x << 2 | y << 1 | 1 - core))
     return pairs
 

time: 20.1 us -> 19.8 us (0.985)
  starting transfers between devices: 11.5 us -> 10.4 us
  waiting for transfers between devices: 3.83 us -> 4.53 us
    ppermute x4, starting transfers between devices: 5.28 us -> 4.15 us  [on_device(): lax.ppermute(total[slot], axes, pairs_of(1, slot))]
    ppermute x4, waiting for transfers between devices: 1.25 us -> 1.95 us  [on_device(): lax.ppermute(total[slot], axes, pairs_of(1, slot))]
  transfers between devices with their start and end apart: 9 -> 9, of which waited for: 5 -> 7; matrix products, arithmetic and copies ran while one was open for 0% -> 0% of each run, Pallas kernels for 4% -> 4%
where the time goes in v5:
time: 19.8 us; the launch traced here: 19.5 us
  starting transfers between devices  10.4 us (53%)
  waiting for transfers between devices  4.53 us (23%)
  Pallas kernels  4.39 us (22%)
    ppermute x4, starting transfers between devices, on_device(): lax.ppermute(total[4 * slot:4 * slot + 4], axes, pairs_of(0, slot))  5.71 us
    ppermute x4, starting transfers between devices, on_device(): lax.ppermute(total[slot], axes, pairs_of(1, slot))  4.15 us
    pallas_call x1, Pallas kernels, on_device(): pl.pallas_call(functools.partial(first_kernel, planes), out_shape=(piece_...  2.66 us
    ppermute x4, waiting for transfers between devices, on_device(): lax.ppermute(total[4 * slot:4 * slot + 4], axes, pairs_of(0, slot))  2.27 us
    ppermute x4, waiting for transfers between devices, on_device(): lax.ppermute(total[slot], axes, pairs_of(1, slot))  1.95 us
    pallas_call x1, Pallas kernels, on_device(): pl.pallas_call(functools.partial(last_kernel, scale), out_shape=jax.Shape...  0.89 us
    pallas_call x1, Pallas kernels, on_device(): pl.pallas_call(second_kernel, out_shape=piece_shape, in_specs=[VMEM] * 3,...  0.84 us
    ppermute x1, starting transfers between devices, on_device(): lax.ppermute(other, axes, [(i, i ^ 1) for i in range(owners * groups)])  0.52 us
  transfers between devices with their start and end apart: 9, of which 7 were waited for; matrix products, arithmetic and copies ran while one was open for 0% of the time, Pallas kernels for 4%

profile of v5, /device:TPU:0, one launch (start us, length us, event | category | flops | bytes accessed | tf_op | source)
XLA Modules:
  0.0 19.5 jit_solution(7636586090774131097)
XLA Ops:
  0.0 2.7 %weigh_and_transform_other.1 = (bf16[16,32,256]{2,1,0:T(8,128)(2,1)S(1)}, f32[4224,128]{1,0:T(8,128)S(1)}, bf16[256,128]{1,0:T(8,128)(2,1)S(1)}, bf16[4,512,256]{2,1,0:T(8,128)(2,1)S(1)}) custom-call(bf16[4096,128]{1,0:T(8,128)(2,1)} %bitcast.19, bf16[1,128]{1,0:T(2,128)(2,1)} %bitcast.20, s32[1,128]{1,0:T(1,128)} %bitcast.21, s32[1,128]{1,0:T(1,128)} %bitcast.22, ...), custom_call_target="tpu_custom_call" | custom-call | tf_op jit(solution)/shard_map/weigh_and_transform_other/pallas_call | solution.py:324
  2.7 0.5 %collective-permute-start = (bf16[16,32,256]{2,1,0:T(8,128)(2,1)S(1)}, bf16[16,32,256]{2,1,0:T(8,128)(2,1)S(1)}, u32[]{:S(2)}, u32[]{:S(2)}) collective-permute-start(bf16[16,32,256]{2,1,0:T(8,128)(2,1)S(1)} %get-tuple-element.12), channel_id=1, source_target_pairs={{0,1},{1,0},{2,3},{3,2},{4,5},{5,4},{6,7},{7,6},{8,9},{9,8},{10,11... | collective-permute-start | bytes 786440 | tf_op jit(solution)/shard_map/ppermute | solution.py:346
  3.2 0.0 copy-start
  3.2 0.0 copy-start.1
  3.2 0.8 %transform_own.1 = bf16[16,32,256]{2,1,0:T(8,128)(2,1)S(1)} custom-call(f32[4224,128]{1,0:T(8,128)S(1)} %get-tuple-element.9.w_ref, bf16[256,128]{1,0:T(8,128)(2,1)S(1)} %get-tuple-element.10.spread_ref, bf16[4,512,256]{2,1,0:T(8,128)(2,1)S(1)} %get-tuple-element.11.table_ref), custom_call_target="tpu_custom_call" | custom-call | tf_op jit(solution)/shard_map/transform_own/pallas_call | solution.py:347
  4.0 0.3 %collective-permute-done = bf16[16,32,256]{2,1,0:T(8,128)(2,1)S(1)} collective-permute-done((bf16[16,32,256]{2,1,0:T(8,128)(2,1)S(1)}, bf16[16,32,256]{2,1,0:T(8,128)(2,1)S(1)}, u32[]{:S(2)}, u32[]{:S(2)}) %collective-permute-start) | collective-permute-done | bytes 262176 | tf_op jit(solution)/shard_map/ppermute | solution.py:346
  4.4 0.1 add_convert_fusion
  4.5 2.7 %collective-permute-start.1 = (bf16[4,32,256]{2,1,0:T(8,128)(2,1)S(1)}, bf16[4,32,256]{2,1,0:T(8,128)(2,1)S(1)}, u32[]{:S(2)}, u32[]{:S(2)}) collective-permute-start(bf16[4,32,256]{2,1,0:T(8,128)(2,1)S(1)} %get-tuple-element.13), channel_id=1, source_target_pairs={{0,3},{1,2},{2,1},{3,0},{4,5},{5,4},{6,7},{7,6},{8,11},{9,10},{10,... | collective-permute-start | bytes 196616 | tf_op jit(solution)/shard_map/ppermute | solution.py:357
  7.2 0.3 %collective-permute-start.4 = (bf16[4,32,256]{2,1,0:T(8,128)(2,1)S(1)}, bf16[4,32,256]{2,1,0:T(8,128)(2,1)S(1)}, u32[]{:S(2)}, u32[]{:S(2)}) collective-permute-start(bf16[4,32,256]{2,1,0:T(8,128)(2,1)S(1)} %get-tuple-element.14), channel_id=1, source_target_pairs={{0,5},{1,4},{2,7},{3,6},{4,3},{5,2},{6,1},{7,0},{8,13},{9,12},{10,... | collective-permute-start | bytes 196616 | tf_op jit(solution)/shard_map/ppermute | solution.py:357
  7.5 2.3 %collective-permute-start.3 = (bf16[4,32,256]{2,1,0:T(8,128)(2,1)S(1)}, bf16[4,32,256]{2,1,0:T(8,128)(2,1)S(1)}, u32[]{:S(2)}, u32[]{:S(2)}) collective-permute-start(bf16[4,32,256]{2,1,0:T(8,128)(2,1)S(1)} %get-tuple-element.15), channel_id=1, source_target_pairs={{0,7},{1,6},{2,5},{3,4},{4,1},{5,0},{6,3},{7,2},{8,15},{9,14},{10,... | collective-permute-start | bytes 196616 | tf_op jit(solution)/shard_map/ppermute | solution.py:357
  9.8 0.4 %collective-permute-start.2 = (bf16[4,32,256]{2,1,0:T(8,128)(2,1)S(1)}, bf16[4,32,256]{2,1,0:T(8,128)(2,1)S(1)}, u32[]{:S(2)}, u32[]{:S(2)}) collective-permute-start(bf16[4,32,256]{2,1,0:T(8,128)(2,1)S(1)} %get-tuple-element.16), channel_id=1, source_target_pairs={{0,1},{1,0},{2,3},{3,2},{4,7},{5,6},{6,5},{7,4},{8,9},{9,8},{10,11... | collective-permute-start | bytes 196616 | tf_op jit(solution)/shard_map/ppermute | solution.py:357
  10.2 0.5 %collective-permute-done.1 = bf16[4,32,256]{2,1,0:T(8,128)(2,1)S(1)} collective-permute-done((bf16[4,32,256]{2,1,0:T(8,128)(2,1)S(1)}, bf16[4,32,256]{2,1,0:T(8,128)(2,1)S(1)}, u32[]{:S(2)}, u32[]{:S(2)}) %collective-permute-start.1) | collective-permute-done | bytes 65568 | tf_op jit(solution)/shard_map/ppermute | solution.py:357
  10.7 1.3 %collective-permute-done.4 = bf16[4,32,256]{2,1,0:T(8,128)(2,1)S(1)} collective-permute-done((bf16[4,32,256]{2,1,0:T(8,128)(2,1)S(1)}, bf16[4,32,256]{2,1,0:T(8,128)(2,1)S(1)}, u32[]{:S(2)}, u32[]{:S(2)}) %collective-permute-start.4) | collective-permute-done | bytes 65568 | tf_op jit(solution)/shard_map/ppermute | solution.py:357
  12.0 0.5 %collective-permute-done.3 = bf16[4,32,256]{2,1,0:T(8,128)(2,1)S(1)} collective-permute-done((bf16[4,32,256]{2,1,0:T(8,128)(2,1)S(1)}, bf16[4,32,256]{2,1,0:T(8,128)(2,1)S(1)}, u32[]{:S(2)}, u32[]{:S(2)}) %collective-permute-start.3) | collective-permute-done | bytes 65568 | tf_op jit(solution)/shard_map/ppermute | solution.py:357
  12.4 0.0 collective-permute-done.2
  12.5 1.5 %collective-permute-start.8 = (bf16[32,256]{1,0:T(8,128)(2,1)S(1)}, bf16[32,256]{1,0:T(8,128)(2,1)S(1)}, u32[]{:S(2)}, u32[]{:S(2)}) collective-permute-start(bf16[32,256]{1,0:T(8,128)(2,1)S(1)} %get-tuple-element.17), channel_id=1, source_target_pairs={{0,9},{1,8},{2,11},{3,10},{4,13},{5,12},{6,15},{7,14},{8,25},{9,24... | collective-permute-start | bytes 49160 | tf_op jit(solution)/shard_map/ppermute | solution.py:359
  14.1 1.2 %collective-permute-start.7 = (bf16[32,256]{1,0:T(8,128)(2,1)S(1)}, bf16[32,256]{1,0:T(8,128)(2,1)S(1)}, u32[]{:S(2)}, u32[]{:S(2)}) collective-permute-start(bf16[32,256]{1,0:T(8,128)(2,1)S(1)} %get-tuple-element.18), channel_id=1, source_target_pairs={{0,17},{1,16},{2,19},{3,18},{4,21},{5,20},{6,23},{7,22},{8,9},{9,8... | collective-permute-start | bytes 49160 | tf_op jit(solution)/shard_map/ppermute | solution.py:359
  15.3 1.2 %collective-permute-start.6 = (bf16[32,256]{1,0:T(8,128)(2,1)S(1)}, bf16[32,256]{1,0:T(8,128)(2,1)S(1)}, u32[]{:S(2)}, u32[]{:S(2)}) collective-permute-start(bf16[32,256]{1,0:T(8,128)(2,1)S(1)} %get-tuple-element.19), channel_id=1, source_target_pairs={{0,25},{1,24},{2,27},{3,26},{4,29},{5,28},{6,31},{7,30},{8,1},{9,0... | collective-permute-start | bytes 49160 | tf_op jit(solution)/shard_map/ppermute | solution.py:359
  16.4 0.2 %collective-permute-start.5 = (bf16[32,256]{1,0:T(8,128)(2,1)S(1)}, bf16[32,256]{1,0:T(8,128)(2,1)S(1)}, u32[]{:S(2)}, u32[]{:S(2)}) collective-permute-start(bf16[32,256]{1,0:T(8,128)(2,1)S(1)} %get-tuple-element.20), channel_id=1, source_target_pairs={{0,1},{1,0},{2,3},{3,2},{4,5},{5,4},{6,7},{7,6},{8,17},{9,16},{10,... | collective-permute-start | bytes 49160 | tf_op jit(solution)/shard_map/ppermute | solution.py:359
  16.7 0.9 %collective-permute-done.8.refs_3_ = bf16[32,256]{1,0:T(8,128)(2,1)S(1)} collective-permute-done((bf16[32,256]{1,0:T(8,128)(2,1)S(1)}, bf16[32,256]{1,0:T(8,128)(2,1)S(1)}, u32[]{:S(2)}, u32[]{:S(2)}) %collective-permute-start.8) | collective-permute-done | bytes 16416 | tf_op jit(solution)/shard_map/ppermute | solution.py:359
  17.5 0.7 %collective-permute-done.7.refs_2_ = bf16[32,256]{1,0:T(8,128)(2,1)S(1)} collective-permute-done((bf16[32,256]{1,0:T(8,128)(2,1)S(1)}, bf16[32,256]{1,0:T(8,128)(2,1)S(1)}, u32[]{:S(2)}, u32[]{:S(2)}) %collective-permute-start.7) | collective-permute-done | bytes 16416 | tf_op jit(solution)/shard_map/ppermute | solution.py:359
  18.2 0.4 %collective-permute-done.6.refs_1_ = bf16[32,256]{1,0:T(8,128)(2,1)S(1)} collective-permute-done((bf16[32,256]{1,0:T(8,128)(2,1)S(1)}, bf16[32,256]{1,0:T(8,128)(2,1)S(1)}, u32[]{:S(2)}, u32[]{:S(2)}) %collective-permute-start.6) | collective-permute-done | bytes 16416 | tf_op jit(solution)/shard_map/ppermute | solution.py:359
  18.6 0.0 collective-permute-done.5.refs_0_
  18.6 0.0 copy-done
  18.6 0.0 copy-done.1
  18.6 0.9 %transform_planes.1 = f32[64,128]{1,0:T(8,128)} custom-call(bf16[32,256]{1,0:T(8,128)(2,1)S(1)} %collective-permute-done.5.refs_0_, bf16[32,256]{1,0:T(8,128)(2,1)S(1)} %collective-permute-done.6.refs_1_, bf16[32,256]{1,0:T(8,128)(2,1)S(1)} %collective-permute-done.7.refs_2_, bf16[32,256]{1,0:T(8,128)(2,1)S(1)} %collective-permute-done.8.refs_3_, ...), custom_call_target="tpu_custom_call" | custom-call | tf_op jit(solution)/shard_map/transform_planes/pallas_call | solution.py:360
  (3 shorter events, 0.1 us)
Async XLA Ops:
  2.7 1.7 %collective-permute-start = (bf16[16,32,256]{2,1,0:T(8,128)(2,1)S(1)}, bf16[16,32,256]{2,1,0:T(8,128)(2,1)S(1)}, u32[]{:S(2)}, u32[]{:S(2)}) collective-permute-start(bf16[16,32,256]{2,1,0:T(8,128)(2,1)S(1)} %get-tuple-element.12), channel_id=1, source_target_pairs={{0,1},{1,0},{2,3},{3,2},{4,5},{5,4},{6,7},{7,6},{8,9},{9,8},{10,11... | collective-permute-start | bytes 786440 | tf_op jit(solution)/shard_map/ppermute | solution.py:346
  3.2 15.4 %copy-start = (bf16[4,128,128]{2,1,0:T(8,128)(2,1)S(1)}, bf16[4,128,128]{2,1,0:T(8,128)(2,1)}, u32[]{:S(2)}) copy-start(bf16[4,128,128]{2,1,0:T(8,128)(2,1)} %constant.10.clone.refs_4_) | copy-start | bytes 393220
  3.2 15.4 %copy-start.1 = (bf16[2,64,32]{2,1,0:T(8,128)(2,1)S(1)}, bf16[2,64,32]{2,1,0:T(8,128)(2,1)}, u32[]{:S(2)}) copy-start(bf16[2,64,32]{2,1,0:T(8,128)(2,1)} %constant.11.clone.refs_5_) | copy-start | bytes 24580
  4.5 6.2 %collective-permute-start.1 = (bf16[4,32,256]{2,1,0:T(8,128)(2,1)S(1)}, bf16[4,32,256]{2,1,0:T(8,128)(2,1)S(1)}, u32[]{:S(2)}, u32[]{:S(2)}) collective-permute-start(bf16[4,32,256]{2,1,0:T(8,128)(2,1)S(1)} %get-tuple-element.13), channel_id=1, source_target_pairs={{0,3},{1,2},{2,1},{3,0},{4,5},{5,4},{6,7},{7,6},{8,11},{9,10},{10,... | collective-permute-start | bytes 196616 | tf_op jit(solution)/shard_map/ppermute | solution.py:357
  7.2 4.8 %collective-permute-start.4 = (bf16[4,32,256]{2,1,0:T(8,128)(2,1)S(1)}, bf16[4,32,256]{2,1,0:T(8,128)(2,1)S(1)}, u32[]{:S(2)}, u32[]{:S(2)}) collective-permute-start(bf16[4,32,256]{2,1,0:T(8,128)(2,1)S(1)} %get-tuple-element.14), channel_id=1, source_target_pairs={{0,5},{1,4},{2,7},{3,6},{4,3},{5,2},{6,1},{7,0},{8,13},{9,12},{10,... | collective-permute-start | bytes 196616 | tf_op jit(solution)/shard_map/ppermute | solution.py:357
  7.5 4.9 %collective-permute-start.3 = (bf16[4,32,256]{2,1,0:T(8,128)(2,1)S(1)}, bf16[4,32,256]{2,1,0:T(8,128)(2,1)S(1)}, u32[]{:S(2)}, u32[]{:S(2)}) collective-permute-start(bf16[4,32,256]{2,1,0:T(8,128)(2,1)S(1)} %get-tuple-element.15), channel_id=1, source_target_pairs={{0,7},{1,6},{2,5},{3,4},{4,1},{5,0},{6,3},{7,2},{8,15},{9,14},{10,... | collective-permute-start | bytes 196616 | tf_op jit(solution)/shard_map/ppermute | solution.py:357
  9.8 2.6 %collective-permute-start.2 = (bf16[4,32,256]{2,1,0:T(8,128)(2,1)S(1)}, bf16[4,32,256]{2,1,0:T(8,128)(2,1)S(1)}, u32[]{:S(2)}, u32[]{:S(2)}) collective-permute-start(bf16[4,32,256]{2,1,0:T(8,128)(2,1)S(1)} %get-tuple-element.16), channel_id=1, source_target_pairs={{0,1},{1,0},{2,3},{3,2},{4,7},{5,6},{6,5},{7,4},{8,9},{9,8},{10,11... | collective-permute-start | bytes 196616 | tf_op jit(solution)/shard_map/ppermute | solution.py:357
  12.5 5.0 %collective-permute-start.8 = (bf16[32,256]{1,0:T(8,128)(2,1)S(1)}, bf16[32,256]{1,0:T(8,128)(2,1)S(1)}, u32[]{:S(2)}, u32[]{:S(2)}) collective-permute-start(bf16[32,256]{1,0:T(8,128)(2,1)S(1)} %get-tuple-element.17), channel_id=1, source_target_pairs={{0,9},{1,8},{2,11},{3,10},{4,13},{5,12},{6,15},{7,14},{8,25},{9,24... | collective-permute-start | bytes 49160 | tf_op jit(solution)/shard_map/ppermute | solution.py:359
  14.1 4.1 %collective-permute-start.7 = (bf16[32,256]{1,0:T(8,128)(2,1)S(1)}, bf16[32,256]{1,0:T(8,128)(2,1)S(1)}, u32[]{:S(2)}, u32[]{:S(2)}) collective-permute-start(bf16[32,256]{1,0:T(8,128)(2,1)S(1)} %get-tuple-element.18), channel_id=1, source_target_pairs={{0,17},{1,16},{2,19},{3,18},{4,21},{5,20},{6,23},{7,22},{8,9},{9,8... | collective-permute-start | bytes 49160 | tf_op jit(solution)/shard_map/ppermute | solution.py:359
  15.3 3.3 %collective-permute-start.6 = (bf16[32,256]{1,0:T(8,128)(2,1)S(1)}, bf16[32,256]{1,0:T(8,128)(2,1)S(1)}, u32[]{:S(2)}, u32[]{:S(2)}) collective-permute-start(bf16[32,256]{1,0:T(8,128)(2,1)S(1)} %get-tuple-element.19), channel_id=1, source_target_pairs={{0,25},{1,24},{2,27},{3,26},{4,29},{5,28},{6,31},{7,30},{8,1},{9,0... | collective-permute-start | bytes 49160 | tf_op jit(solution)/shard_map/ppermute | solution.py:359
  16.4 2.2 %collective-permute-start.5 = (bf16[32,256]{1,0:T(8,128)(2,1)S(1)}, bf16[32,256]{1,0:T(8,128)(2,1)S(1)}, u32[]{:S(2)}, u32[]{:S(2)}) collective-permute-start(bf16[32,256]{1,0:T(8,128)(2,1)S(1)} %get-tuple-element.20), channel_id=1, source_target_pairs={{0,1},{1,0},{2,3},{3,2},{4,5},{5,4},{6,7},{7,6},{8,17},{9,16},{10,... | collective-permute-start | bytes 49160 | tf_op jit(solution)/shard_map/ppermute | solution.py:359

commit v6 on v5

--- a/solution.py
+++ b/solution.py
@@ -42,19 +42,26 @@
     return table.astype(np.float32)
 
 
+def column_of(q):
+    group, lane = np.arange(LANES) // GROUP, np.arange(LANES) % GROUP
+    return 4 * (GROUP * ((group - q) % QUARTERS) + lane) + q
+
+
 def fourier_table():
+    out = np.zeros((QUARTERS, LANES, 2, LANES))
+    for q in range(QUARTERS):
+        wave = 2.0 * np.pi * ((np.arange(LANES)[:, None] * column_of(q)[None, :]) % NX) / NX
+        out[q, :, 0], out[q, :, 1] = np.cos(wave), np.sin(wave)
+    return out.reshape(QUARTERS, LANES, 2 * LANES).astype(jnp.bfloat16)
+
+
+def factor_table():
     taps = lanczos_taps(XBINS).astype(np.float64)
-    m = np.arange(LANES)
-    group, lane = np.arange(LANES) // GROUP, np.arange(LANES) % GROUP
-    out = np.zeros((QUARTERS, XBINS, LANES, 2, LANES))
+    out = np.zeros((XBINS, QUARTERS, 2, LANES))
     for q in range(QUARTERS):
-        column = 4 * (GROUP * ((group - q) % QUARTERS) + lane) + q
-        shift = 2.0 * np.pi * (((np.arange(TAPS) - 3)[:, None] * column[None, :]) % NX) / NX
-        wave = 2.0 * np.pi * ((m[:, None] * column[None, :]) % NX) / NX
-        for b in range(XBINS):
-            value = (taps[b][:, None] * np.exp(1j * shift)).sum(0)[None, :] * np.exp(1j * wave)
-            out[q, b, :, 0], out[q, b, :, 1] = value.real, value.imag
-    return out.reshape(QUARTERS, XBINS * LANES, 2 * LANES).astype(jnp.bfloat16)
+        shift = 2.0 * np.pi * (((np.arange(TAPS) - 3)[:, None] * column_of(q)[None, :]) % NX) / NX
+        out[:, q, 0], out[:, q, 1] = taps @ np.cos(shift), taps @ np.sin(shift)
+    return out.reshape(XBINS, 2 * NX).astype(np.float32)
 
 
 def order_table():
@@ -86,9 +93,8 @@
     return (ar + cr, ai + ci), (br - di, bi + dr), (ar - cr, ai - ci), (br + di, bi - dr)
 
 
-def transform(w_ref, ky_low, spread, table, u_ref, v_ref, put):
-    cz = CLASSES * PLANES
-    number = spread.shape[1]
+def transform(w_ref, ky_low, spread_ref, table_ref, factor_ref, u_ref, v_ref, put):
+    number = spread_ref.shape[1]
     for y in range(2):
 
         def column(r, p):
@@ -97,43 +103,41 @@
         sums = quarter_sums([(column(0, p), column(1, p)) for p in range(QUARTERS)])
         for q in range(QUARTERS):
             for r in range(2):
-                at = (r * QUARTERS + q) * LANES
-                u_ref[y, :, at : at + LANES] = sums[q][r].astype(bf16)
+                at = (r * 2 + y) * number
+                u_ref[q, at : at + number, :] = sums[q][r].astype(bf16)
+    for q in range(QUARTERS):
+        both = jnp.dot(u_ref[q], table_ref[q], preferred_element_type=f32)
+        real = both[: 2 * number, :LANES] - both[2 * number :, LANES:]
+        imag = both[: 2 * number, LANES:] + both[2 * number :, :LANES]
+        by_real, by_imag = (factor_ref[:, (2 * q + s) * LANES : (2 * q + s + 1) * LANES] for s in range(2))
+        for y in range(2):
+            rows = slice(y * number, (y + 1) * number)
+            at = (y * QUARTERS + q) * 2 * LANES
+            v_ref[:, at : at + LANES] = (real[rows] * by_real - imag[rows] * by_imag).astype(bf16)
+            v_ref[:, at + LANES : at + 2 * LANES] = (real[rows] * by_imag + imag[rows] * by_real).astype(bf16)
+    group = lax.broadcasted_iota(jnp.int32, (CLASSES * PLANES, 2 * LANES), 1) % LANES // GROUP
     for y in range(2):
-        part = jnp.dot(spread, u_ref[y], preferred_element_type=f32).astype(bf16)
-        for r in range(2):
-            for q in range(QUARTERS):
-                at, row = (r * QUARTERS + q) * LANES, (r * 2 + y) * cz
-                for b in range(XBINS):
-                    v_ref[q, row : row + cz, b * LANES : (b + 1) * LANES] = part[b * cz : (b + 1) * cz, at : at + LANES]
-    group = lax.broadcasted_iota(jnp.int32, (2 * cz, LANES), 1) // GROUP
-    real, imag = [], []
-    for q in range(QUARTERS):
-        both = jnp.dot(v_ref[q], table(q), preferred_element_type=f32)
-        real.append(both[: 2 * cz, :LANES] - both[2 * cz :, LANES:])
-        imag.append(both[: 2 * cz, LANES:] + both[2 * cz :, :LANES])
-    for quarter in range(QUARTERS):
-        chosen = []
-        for parts in (real, imag):
-            value = parts[(0 - quarter) % QUARTERS]
+        part = jnp.dot(
+            spread_ref[...], v_ref[:, y * 2 * NX : (y + 1) * 2 * NX], preferred_element_type=f32
+        )
+        parts = [part[:, q * 2 * LANES : (q + 1) * 2 * LANES] for q in range(QUARTERS)]
+        for quarter in range(QUARTERS):
+            value = parts[-quarter % QUARTERS]
             for j in range(1, QUARTERS):
                 value = jnp.where(group == j, parts[(j - quarter) % QUARTERS], value)
-            chosen.append(value.astype(bf16))
-        value = jnp.concatenate(chosen, axis=1)
-        for y in range(2):
+            value = value.astype(bf16)
             for cls in range(CLASSES):
-                at = (y * CLASSES + cls) * PLANES
-                put(y, cls, quarter, value[at : at + PLANES])
+                put(y, cls, quarter, value[cls * PLANES : (cls + 1) * PLANES])
 
 
 def spread_matrix(pose, label, planes, first_plane):
     per_pose = ZBINS * XBINS
     taps = lanczos_taps(ZBINS)
-    start, zbin, xbin = pose // per_pose, pose // XBINS % ZBINS, pose % XBINS
-    shape = (XBINS * CLASSES * PLANES, pose.shape[1])
+    start, zbin = pose // per_pose, pose // XBINS % ZBINS
+    shape = (CLASSES * PLANES, pose.shape[1])
     row = lax.broadcasted_iota(jnp.int32, shape, 0)
     tap = (first_plane + row % PLANES - start + planes) % planes
-    tap = jnp.where(row // PLANES == xbin * CLASSES + label, tap, -1)
+    tap = jnp.where(row // PLANES == label, tap, -1)
     out = jnp.zeros(shape, f32)
     for t in range(TAPS):
         weight = jnp.full(pose.shape, float(taps[0, t]), f32)
@@ -160,9 +164,9 @@
     return put
 
 
-def first_kernel(planes, x_hbm, focus_hbm, pose_hbm, label_hbm, turns_hbm, table_hbm,
-                 out_ref, w_ref, spread_ref, table_ref,
-                 x_ref, focus_ref, pose_ref, label_ref, turns_ref, wide_ref, u_ref, v_ref, sems):
+def first_kernel(planes, x_hbm, focus_hbm, pose_hbm, label_hbm, turns_hbm, bins_hbm, table_hbm,
+                 out_ref, w_ref, spread_ref, table_ref, factor_ref,
+                 x_ref, focus_ref, pose_ref, label_ref, turns_ref, bins_ref, wide_ref, u_ref, v_ref, sems):
     number = wide_ref.shape[0]
     chunk = x_ref.shape[0] // CHUNKS
 
@@ -174,19 +178,31 @@
     small = [
         copy(source, target, at)
         for at, (source, target) in enumerate(
-            ((focus_hbm, focus_ref), (turns_hbm, turns_ref), (pose_hbm, pose_ref), (label_hbm, label_ref))
+            (
+                (focus_hbm, focus_ref),
+                (turns_hbm, turns_ref),
+                (pose_hbm, pose_ref),
+                (label_hbm, label_ref),
+                (bins_hbm, bins_ref),
+            )
         )
     ]
     parts = [
-        copy(x_hbm.at[pl.ds(c * chunk, chunk)], x_ref.at[pl.ds(c * chunk, chunk)], 4 + c) for c in range(CHUNKS)
+        copy(x_hbm.at[pl.ds(c * chunk, chunk)], x_ref.at[pl.ds(c * chunk, chunk)], 5 + c) for c in range(CHUNKS)
     ]
-    table = copy(table_hbm, table_ref, 4 + CHUNKS)
+    table = copy(table_hbm, table_ref, 5 + CHUNKS)
     for made in small:
         made.wait()
     core = lax.axis_index("img") % 2
     coefficients = [float(v) for v in sine_coefficients()]
     wide_ref[...] = jnp.broadcast_to(focus_ref[...].astype(f32), (LANES, number)).T
     spread_ref[...] = spread_matrix(pose_ref[...], label_ref[...], planes, 0)
+    xbin = jnp.broadcast_to((pose_ref[...] % XBINS).astype(f32), (LANES, number)).T
+    for at in range(0, 2 * NX, LANES):
+        chosen = bins_ref[0:1, at : at + LANES]
+        for b in range(1, XBINS):
+            chosen = jnp.where(xbin == b, bins_ref[b : b + 1, at : at + LANES], chosen)
+        factor_ref[:, at : at + LANES] = chosen
     turns = turns_ref[...]
 
     def weigh(i, carry):
@@ -207,12 +223,12 @@
         parts[c].wait()
         lax.fori_loop(c * number // CHUNKS, (c + 1) * number // CHUNKS, weigh, 0, unroll=UNROLL)
     table.wait()
-    transform(w_ref, 1 - core, spread_ref[...], lambda q: table_ref[q], u_ref, v_ref, place(out_ref, 1 - core))
-
-
-def second_kernel(w_ref, spread_ref, table_ref, out_ref, u_ref, v_ref):
+    transform(w_ref, 1 - core, spread_ref, table_ref, factor_ref, u_ref, v_ref, place(out_ref, 1 - core))
+
+
+def second_kernel(w_ref, spread_ref, table_ref, factor_ref, out_ref, u_ref, v_ref):
     core = lax.axis_index("img") % 2
-    transform(w_ref, core, spread_ref[...], lambda q: table_ref[q], u_ref, v_ref, place(out_ref, core))
+    transform(w_ref, core, spread_ref, table_ref, factor_ref, u_ref, v_ref, place(out_ref, core))
 
 
 def last_kernel(scale, *refs):
@@ -274,25 +290,22 @@
     number = images.shape[0]
     planes = owners * 4
     weighted = (ctf_weights(defocus)[:, None] * images.astype(f32)).astype(bf16)
-    table = jnp.asarray(fourier_table()).reshape(QUARTERS, XBINS, LANES, 2, LANES)
-    order = jnp.asarray(order_table())
+    table = jnp.asarray(fourier_table()).reshape(QUARTERS, LANES, 2, LANES)
+    factors = jnp.asarray(factor_table()).reshape(XBINS, QUARTERS, 2, LANES)[pose_bins % XBINS]
+    by_real, by_imag = (jnp.moveaxis(factors[:, :, s], 0, 1)[:, :, None] for s in range(2))
     quarters = jnp.moveaxis(weighted.astype(f32).reshape(number, 2, KY, QUARTERS, LANES), 3, 0)
     sums = quarter_sums([(part[:, 0], part[:, 1]) for part in quarters])
     sums = jnp.stack([jnp.stack(pair) for pair in sums]).astype(bf16)
+    both = jnp.einsum("qrikm,qmsn->rsqikn", sums, table, preferred_element_type=f32)
+    real, imag = both[0, 0] - both[1, 1], both[0, 1] + both[1, 0]
+    turned = jnp.stack([real * by_real - imag * by_imag, real * by_imag + imag * by_real]).astype(bf16)
+    columns = np.argsort(np.concatenate([column_of(q) for q in range(QUARTERS)]))
+    turned = jnp.moveaxis(turned, 1, 3).reshape(2, number, KY, NX)[..., columns]
 
     def block(first_plane):
         spread = spread_matrix(pose_bins[None], labels[None], planes, first_plane)
-        spread = spread.reshape(XBINS, CLASSES * PLANES, number)
-        part = jnp.einsum("bci,qrikm->qrkcbm", spread, sums, preferred_element_type=f32).astype(bf16)
-        both = jnp.einsum("qrkcbm,qbmsn->rsqkcn", part, table, preferred_element_type=f32)
-        turned = jnp.stack([both[0, 0] - both[1, 1], both[0, 1] + both[1, 0]])
-        turned = turned.reshape(2, QUARTERS, KY, CLASSES, PLANES, QUARTERS, GROUP)
-        ordered = []
-        for quarter in range(QUARTERS):
-            groups_of = [turned[:, (j - quarter) % QUARTERS, ..., j, :] for j in range(QUARTERS)]
-            value = jnp.concatenate(groups_of, axis=-1).astype(bf16)
-            ordered.append(jnp.einsum("skczn,nw->kcwsz", value, order[quarter], preferred_element_type=f32))
-        return jnp.stack(ordered, axis=2).astype(bf16)
+        spread = spread.reshape(CLASSES, PLANES, number)
+        return jnp.einsum("czi,sikx->kcxsz", spread, turned, preferred_element_type=f32).astype(bf16)
 
     parts = lax.map(block, jnp.arange(planes // PLANES, dtype=jnp.int32) * PLANES)
     parts = jnp.moveaxis(parts, 0, -2).reshape(KY, CLASSES * NX, 2, planes).astype(f32)
@@ -313,46 +326,46 @@
     x = images.reshape(number, 2, KY, QUARTERS, LANES).transpose(0, 1, 3, 2, 4).reshape(number * 2 * ROWS, LANES)
     pieces = 2 * CLASSES * QUARTERS
     w_shape = jax.ShapeDtypeStruct((number * PITCH, LANES), f32)
-    spread_shape = jax.ShapeDtypeStruct((XBINS * CLASSES * PLANES, number), bf16)
+    spread_shape = jax.ShapeDtypeStruct((CLASSES * PLANES, number), bf16)
     piece_shape = jax.ShapeDtypeStruct((pieces, PLANES, 2 * LANES), bf16)
     table = jnp.asarray(fourier_table())
     table_shape = jax.ShapeDtypeStruct(table.shape, bf16)
-    work = [
-        pltpu.VMEM((2, number, 2 * NX), bf16),
-        pltpu.VMEM((QUARTERS, 4 * CLASSES * PLANES, XBINS * LANES), bf16),
-    ]
-    other, weighted, spread, near_table = pl.pallas_call(
+    bins = jnp.asarray(factor_table())
+    factor_shape = jax.ShapeDtypeStruct((number, 2 * NX), f32)
+    work = [pltpu.VMEM((QUARTERS, 4 * number, LANES), bf16), pltpu.VMEM((number, 4 * NX), bf16)]
+    other, *near = pl.pallas_call(
         functools.partial(first_kernel, planes),
-        out_shape=(piece_shape, w_shape, spread_shape, table_shape),
-        in_specs=[HBM] * 6,
-        out_specs=(VMEM,) * 4,
+        out_shape=(piece_shape, w_shape, spread_shape, table_shape, factor_shape),
+        in_specs=[HBM] * 7,
+        out_specs=(VMEM,) * 5,
         scratch_shapes=[
             pltpu.VMEM(x.shape, bf16),
             pltpu.VMEM((1, number), bf16),
             pltpu.VMEM((1, number), jnp.int32),
             pltpu.VMEM((1, number), jnp.int32),
             pltpu.VMEM((ROWS, LANES), f32),
+            pltpu.VMEM(bins.shape, f32),
             pltpu.VMEM((number, LANES), f32),
             *work,
-            pltpu.SemaphoreType.DMA((CHUNKS + 5,)),
+            pltpu.SemaphoreType.DMA((CHUNKS + 6,)),
         ],
         compiler_params=pltpu.CompilerParams(vmem_limit_bytes=32 << 20),
         name="weigh_and_transform_other",
     )(*(
         pltpu.with_memory_space_constraint(v, pltpu.HBM)
-        for v in (x, defocus[None], pose_bins[None], labels[None], jnp.asarray(turns_per_defocus()), table)
+        for v in (x, defocus[None], pose_bins[None], labels[None], jnp.asarray(turns_per_defocus()), bins, table)
     ))
     axes = ("slab", "img")
     got = lax.ppermute(other, axes, [(i, i ^ 1) for i in range(owners * groups)])
     own = pl.pallas_call(
         second_kernel,
         out_shape=piece_shape,
-        in_specs=[VMEM] * 3,
+        in_specs=[VMEM] * 4,
         out_specs=VMEM,
         scratch_shapes=work,
         compiler_params=pltpu.CompilerParams(vmem_limit_bytes=16 << 20),
         name="transform_own",
-    )(weighted, spread, near_table)
+    )(*near)
     total = (own.astype(f32) + got.astype(f32)).astype(bf16)
     got = [lax.ppermute(total[4 * slot : 4 * slot + 4], axes, pairs_of(0, slot)) for slot in FIRST_LISTED]
     total = sum(g.astype(f32) for g in got).astype(bf16)

time: 19.8 us -> 19.7 us (level)
  the two profiles are of different devices: /device:TPU:0 before, /device:TPU:3 now
where the time goes in v6:
time: 19.7 us; the launch traced here: 19.6 us
  starting transfers between devices  9.5 us (48%)
  waiting for transfers between devices  5.65 us (29%)
  Pallas kernels  4.21 us (21%)
    ppermute x4, starting transfers between devices, on_device(): lax.ppermute(total[slot], axes, pairs_of(1, slot))  5.29 us
    ppermute x4, waiting for transfers between devices, on_device(): lax.ppermute(total[4 * slot:4 * slot + 4], axes, pairs_of(0, slot))  3.98 us
    ppermute x4, starting transfers between devices, on_device(): lax.ppermute(total[4 * slot:4 * slot + 4], axes, pairs_of(0, slot))  3.47 us
    pallas_call x1, Pallas kernels, on_device(): pl.pallas_call(functools.partial(first_kernel, planes), out_shape=(piece_...  2.58 us
    ppermute x4, waiting for transfers between devices, on_device(): lax.ppermute(total[slot], axes, pairs_of(1, slot))  1.26 us
    pallas_call x1, Pallas kernels, on_device(): pl.pallas_call(functools.partial(last_kernel, scale), out_shape=jax.Shape...  0.89 us
    pallas_call x1, Pallas kernels, on_device(): pl.pallas_call(second_kernel, out_shape=piece_shape, in_specs=[VMEM] * 4,...  0.74 us
    ppermute x1, starting transfers between devices, on_device(): lax.ppermute(other, axes, [(i, i ^ 1) for i in range(owners * groups)])  0.74 us
  transfers between devices with their start and end apart: 9, of which 5 were waited for; matrix products, arithmetic and copies ran while one was open for 0% of the time, Pallas kernels for 4%

profile of v6, /device:TPU:3, one launch (start us, length us, event | category | flops | bytes accessed | tf_op | source)
XLA Modules:
  0.0 19.6 jit_solution(1594131670308281024)
XLA Ops:
  0.0 2.6 %weigh_and_transform_other.1 = (bf16[16,32,256]{2,1,0:T(8,128)(2,1)S(1)}, f32[4224,128]{1,0:T(8,128)S(1)}, bf16[64,128]{1,0:T(8,128)(2,1)S(1)}, bf16[4,128,256]{2,1,0:T(8,128)(2,1)S(1)}, f32[128,1024]{1,0:T(8,128)S(1)}) custom-call(bf16[4096,128]{1,0:T(8,128)(2,1)} %bitcast.19, bf16[1,128]{1,0:T(2,128)(2,1)} %bitcast.20, s32[1,128]{1,0:T(1,128)} %bitcast.21, ...), custom_call_target="tpu_custom_call" | custom-call | tf_op jit(solution)/shard_map/weigh_and_transform_other/pallas_call | solution.py:336
  2.6 0.7 %collective-permute-start = (bf16[16,32,256]{2,1,0:T(8,128)(2,1)S(1)}, bf16[16,32,256]{2,1,0:T(8,128)(2,1)S(1)}, u32[]{:S(2)}, u32[]{:S(2)}) collective-permute-start(bf16[16,32,256]{2,1,0:T(8,128)(2,1)S(1)} %get-tuple-element.14), channel_id=1, source_target_pairs={{0,1},{1,0},{2,3},{3,2},{4,5},{5,4},{6,7},{7,6},{8,9},{9,8},{10,11... | collective-permute-start | bytes 786440 | tf_op jit(solution)/shard_map/ppermute | solution.py:359
  3.3 0.0 copy-start
  3.3 0.0 copy-start.1
  3.3 0.7 %transform_own.1 = bf16[16,32,256]{2,1,0:T(8,128)(2,1)S(1)} custom-call(f32[4224,128]{1,0:T(8,128)S(1)} %get-tuple-element.10.w_ref, bf16[64,128]{1,0:T(8,128)(2,1)S(1)} %get-tuple-element.11.spread_ref, bf16[4,128,256]{2,1,0:T(8,128)(2,1)S(1)} %get-tuple-element.12.table_ref, f32[128,1024]{1,0:T(8,128)S(1)} %get-tuple-element.13.factor_ref), custom_call_target="tpu_custom_call" | custom-call | tf_op jit(solution)/shard_map/transform_own/pallas_call | solution.py:360
  4.1 0.4 %collective-permute-done = bf16[16,32,256]{2,1,0:T(8,128)(2,1)S(1)} collective-permute-done((bf16[16,32,256]{2,1,0:T(8,128)(2,1)S(1)}, bf16[16,32,256]{2,1,0:T(8,128)(2,1)S(1)}, u32[]{:S(2)}, u32[]{:S(2)}) %collective-permute-start) | collective-permute-done | bytes 262176 | tf_op jit(solution)/shard_map/ppermute | solution.py:359
  4.5 0.1 add_convert_fusion
  4.6 0.4 %collective-permute-start.1 = (bf16[4,32,256]{2,1,0:T(8,128)(2,1)S(1)}, bf16[4,32,256]{2,1,0:T(8,128)(2,1)S(1)}, u32[]{:S(2)}, u32[]{:S(2)}) collective-permute-start(bf16[4,32,256]{2,1,0:T(8,128)(2,1)S(1)} %get-tuple-element.15), channel_id=1, source_target_pairs={{0,3},{1,2},{2,1},{3,0},{4,5},{5,4},{6,7},{7,6},{8,11},{9,10},{10,... | collective-permute-start | bytes 196616 | tf_op jit(solution)/shard_map/ppermute | solution.py:370
  5.0 1.2 %collective-permute-start.4 = (bf16[4,32,256]{2,1,0:T(8,128)(2,1)S(1)}, bf16[4,32,256]{2,1,0:T(8,128)(2,1)S(1)}, u32[]{:S(2)}, u32[]{:S(2)}) collective-permute-start(bf16[4,32,256]{2,1,0:T(8,128)(2,1)S(1)} %get-tuple-element.16), channel_id=1, source_target_pairs={{0,5},{1,4},{2,7},{3,6},{4,3},{5,2},{6,1},{7,0},{8,13},{9,12},{10,... | collective-permute-start | bytes 196616 | tf_op jit(solution)/shard_map/ppermute | solution.py:370
  6.2 0.6 %collective-permute-start.3 = (bf16[4,32,256]{2,1,0:T(8,128)(2,1)S(1)}, bf16[4,32,256]{2,1,0:T(8,128)(2,1)S(1)}, u32[]{:S(2)}, u32[]{:S(2)}) collective-permute-start(bf16[4,32,256]{2,1,0:T(8,128)(2,1)S(1)} %get-tuple-element.17), channel_id=1, source_target_pairs={{0,7},{1,6},{2,5},{3,4},{4,1},{5,0},{6,3},{7,2},{8,15},{9,14},{10,... | collective-permute-start | bytes 196616 | tf_op jit(solution)/shard_map/ppermute | solution.py:370
  6.8 1.3 %collective-permute-start.2 = (bf16[4,32,256]{2,1,0:T(8,128)(2,1)S(1)}, bf16[4,32,256]{2,1,0:T(8,128)(2,1)S(1)}, u32[]{:S(2)}, u32[]{:S(2)}) collective-permute-start(bf16[4,32,256]{2,1,0:T(8,128)(2,1)S(1)} %get-tuple-element.18), channel_id=1, source_target_pairs={{0,1},{1,0},{2,3},{3,2},{4,7},{5,6},{6,5},{7,4},{8,9},{9,8},{10,11... | collective-permute-start | bytes 196616 | tf_op jit(solution)/shard_map/ppermute | solution.py:370
  8.1 0.0 collective-permute-done.1
  8.1 0.8 %collective-permute-done.4 = bf16[4,32,256]{2,1,0:T(8,128)(2,1)S(1)} collective-permute-done((bf16[4,32,256]{2,1,0:T(8,128)(2,1)S(1)}, bf16[4,32,256]{2,1,0:T(8,128)(2,1)S(1)}, u32[]{:S(2)}, u32[]{:S(2)}) %collective-permute-start.4) | collective-permute-done | bytes 65568 | tf_op jit(solution)/shard_map/ppermute | solution.py:370
  8.9 2.4 %collective-permute-done.3 = bf16[4,32,256]{2,1,0:T(8,128)(2,1)S(1)} collective-permute-done((bf16[4,32,256]{2,1,0:T(8,128)(2,1)S(1)}, bf16[4,32,256]{2,1,0:T(8,128)(2,1)S(1)}, u32[]{:S(2)}, u32[]{:S(2)}) %collective-permute-start.3) | collective-permute-done | bytes 65568 | tf_op jit(solution)/shard_map/ppermute | solution.py:370
  11.3 0.7 %collective-permute-done.2 = bf16[4,32,256]{2,1,0:T(8,128)(2,1)S(1)} collective-permute-done((bf16[4,32,256]{2,1,0:T(8,128)(2,1)S(1)}, bf16[4,32,256]{2,1,0:T(8,128)(2,1)S(1)}, u32[]{:S(2)}, u32[]{:S(2)}) %collective-permute-start.2) | collective-permute-done | bytes 65568 | tf_op jit(solution)/shard_map/ppermute | solution.py:370
  12.1 1.5 %collective-permute-start.8 = (bf16[32,256]{1,0:T(8,128)(2,1)S(1)}, bf16[32,256]{1,0:T(8,128)(2,1)S(1)}, u32[]{:S(2)}, u32[]{:S(2)}) collective-permute-start(bf16[32,256]{1,0:T(8,128)(2,1)S(1)} %get-tuple-element.19), channel_id=1, source_target_pairs={{0,9},{1,8},{2,11},{3,10},{4,13},{5,12},{6,15},{7,14},{8,25},{9,24... | collective-permute-start | bytes 49160 | tf_op jit(solution)/shard_map/ppermute | solution.py:372
  13.6 1.2 %collective-permute-start.7 = (bf16[32,256]{1,0:T(8,128)(2,1)S(1)}, bf16[32,256]{1,0:T(8,128)(2,1)S(1)}, u32[]{:S(2)}, u32[]{:S(2)}) collective-permute-start(bf16[32,256]{1,0:T(8,128)(2,1)S(1)} %get-tuple-element.20), channel_id=1, source_target_pairs={{0,17},{1,16},{2,19},{3,18},{4,21},{5,20},{6,23},{7,22},{8,9},{9,8... | collective-permute-start | bytes 49160 | tf_op jit(solution)/shard_map/ppermute | solution.py:372
  14.8 2.3 %collective-permute-start.6 = (bf16[32,256]{1,0:T(8,128)(2,1)S(1)}, bf16[32,256]{1,0:T(8,128)(2,1)S(1)}, u32[]{:S(2)}, u32[]{:S(2)}) collective-permute-start(bf16[32,256]{1,0:T(8,128)(2,1)S(1)} %get-tuple-element.21), channel_id=1, source_target_pairs={{0,25},{1,24},{2,27},{3,26},{4,29},{5,28},{6,31},{7,30},{8,1},{9,0... | collective-permute-start | bytes 49160 | tf_op jit(solution)/shard_map/ppermute | solution.py:372
  17.1 0.3 %collective-permute-start.5 = (bf16[32,256]{1,0:T(8,128)(2,1)S(1)}, bf16[32,256]{1,0:T(8,128)(2,1)S(1)}, u32[]{:S(2)}, u32[]{:S(2)}) collective-permute-start(bf16[32,256]{1,0:T(8,128)(2,1)S(1)} %get-tuple-element.22), channel_id=1, source_target_pairs={{0,1},{1,0},{2,3},{3,2},{4,5},{5,4},{6,7},{7,6},{8,17},{9,16},{10,... | collective-permute-start | bytes 49160 | tf_op jit(solution)/shard_map/ppermute | solution.py:372
  17.4 0.0 collective-permute-done.8.refs_3_
  17.4 1.2 %collective-permute-done.7.refs_2_ = bf16[32,256]{1,0:T(8,128)(2,1)S(1)} collective-permute-done((bf16[32,256]{1,0:T(8,128)(2,1)S(1)}, bf16[32,256]{1,0:T(8,128)(2,1)S(1)}, u32[]{:S(2)}, u32[]{:S(2)}) %collective-permute-start.7) | collective-permute-done | bytes 16416 | tf_op jit(solution)/shard_map/ppermute | solution.py:372
  18.7 0.0 collective-permute-done.6.refs_1_
  18.7 0.0 collective-permute-done.5.refs_0_
  18.7 0.0 copy-done
  18.7 0.0 copy-done.1
  18.7 0.9 %transform_planes.1 = f32[64,128]{1,0:T(8,128)} custom-call(bf16[32,256]{1,0:T(8,128)(2,1)S(1)} %collective-permute-done.5.refs_0_, bf16[32,256]{1,0:T(8,128)(2,1)S(1)} %collective-permute-done.6.refs_1_, bf16[32,256]{1,0:T(8,128)(2,1)S(1)} %collective-permute-done.7.refs_2_, bf16[32,256]{1,0:T(8,128)(2,1)S(1)} %collective-permute-done.8.refs_3_, ...), custom_call_target="tpu_custom_call" | custom-call | tf_op jit(solution)/shard_map/transform_planes/pallas_call | solution.py:373
  (3 shorter events, 0.1 us)
Async XLA Ops:
  2.6 1.9 %collective-permute-start = (bf16[16,32,256]{2,1,0:T(8,128)(2,1)S(1)}, bf16[16,32,256]{2,1,0:T(8,128)(2,1)S(1)}, u32[]{:S(2)}, u32[]{:S(2)}) collective-permute-start(bf16[16,32,256]{2,1,0:T(8,128)(2,1)S(1)} %get-tuple-element.14), channel_id=1, source_target_pairs={{0,1},{1,0},{2,3},{3,2},{4,5},{5,4},{6,7},{7,6},{8,9},{9,8},{10,11... | collective-permute-start | bytes 786440 | tf_op jit(solution)/shard_map/ppermute | solution.py:359
  3.3 15.3 %copy-start = (bf16[4,128,128]{2,1,0:T(8,128)(2,1)S(1)}, bf16[4,128,128]{2,1,0:T(8,128)(2,1)}, u32[]{:S(2)}) copy-start(bf16[4,128,128]{2,1,0:T(8,128)(2,1)} %constant.13.clone.refs_4_) | copy-start | bytes 393220
  3.3 15.3 %copy-start.1 = (bf16[2,64,32]{2,1,0:T(8,128)(2,1)S(1)}, bf16[2,64,32]{2,1,0:T(8,128)(2,1)}, u32[]{:S(2)}) copy-start(bf16[2,64,32]{2,1,0:T(8,128)(2,1)} %constant.14.clone.refs_5_) | copy-start | bytes 24580
  4.6 3.5 %collective-permute-start.1 = (bf16[4,32,256]{2,1,0:T(8,128)(2,1)S(1)}, bf16[4,32,256]{2,1,0:T(8,128)(2,1)S(1)}, u32[]{:S(2)}, u32[]{:S(2)}) collective-permute-start(bf16[4,32,256]{2,1,0:T(8,128)(2,1)S(1)} %get-tuple-element.15), channel_id=1, source_target_pairs={{0,3},{1,2},{2,1},{3,0},{4,5},{5,4},{6,7},{7,6},{8,11},{9,10},{10,... | collective-permute-start | bytes 196616 | tf_op jit(solution)/shard_map/ppermute | solution.py:370
  5.0 3.9 %collective-permute-start.4 = (bf16[4,32,256]{2,1,0:T(8,128)(2,1)S(1)}, bf16[4,32,256]{2,1,0:T(8,128)(2,1)S(1)}, u32[]{:S(2)}, u32[]{:S(2)}) collective-permute-start(bf16[4,32,256]{2,1,0:T(8,128)(2,1)S(1)} %get-tuple-element.16), channel_id=1, source_target_pairs={{0,5},{1,4},{2,7},{3,6},{4,3},{5,2},{6,1},{7,0},{8,13},{9,12},{10,... | collective-permute-start | bytes 196616 | tf_op jit(solution)/shard_map/ppermute | solution.py:370
  6.2 5.1 %collective-permute-start.3 = (bf16[4,32,256]{2,1,0:T(8,128)(2,1)S(1)}, bf16[4,32,256]{2,1,0:T(8,128)(2,1)S(1)}, u32[]{:S(2)}, u32[]{:S(2)}) collective-permute-start(bf16[4,32,256]{2,1,0:T(8,128)(2,1)S(1)} %get-tuple-element.17), channel_id=1, source_target_pairs={{0,7},{1,6},{2,5},{3,4},{4,1},{5,0},{6,3},{7,2},{8,15},{9,14},{10,... | collective-permute-start | bytes 196616 | tf_op jit(solution)/shard_map/ppermute | solution.py:370
  6.8 5.3 %collective-permute-start.2 = (bf16[4,32,256]{2,1,0:T(8,128)(2,1)S(1)}, bf16[4,32,256]{2,1,0:T(8,128)(2,1)S(1)}, u32[]{:S(2)}, u32[]{:S(2)}) collective-permute-start(bf16[4,32,256]{2,1,0:T(8,128)(2,1)S(1)} %get-tuple-element.18), channel_id=1, source_target_pairs={{0,1},{1,0},{2,3},{3,2},{4,7},{5,6},{6,5},{7,4},{8,9},{9,8},{10,11... | collective-permute-start | bytes 196616 | tf_op jit(solution)/shard_map/ppermute | solution.py:370
  12.1 5.3 %collective-permute-start.8 = (bf16[32,256]{1,0:T(8,128)(2,1)S(1)}, bf16[32,256]{1,0:T(8,128)(2,1)S(1)}, u32[]{:S(2)}, u32[]{:S(2)}) collective-permute-start(bf16[32,256]{1,0:T(8,128)(2,1)S(1)} %get-tuple-element.19), channel_id=1, source_target_pairs={{0,9},{1,8},{2,11},{3,10},{4,13},{5,12},{6,15},{7,14},{8,25},{9,24... | collective-permute-start | bytes 49160 | tf_op jit(solution)/shard_map/ppermute | solution.py:372
  13.6 5.1 %collective-permute-start.7 = (bf16[32,256]{1,0:T(8,128)(2,1)S(1)}, bf16[32,256]{1,0:T(8,128)(2,1)S(1)}, u32[]{:S(2)}, u32[]{:S(2)}) collective-permute-start(bf16[32,256]{1,0:T(8,128)(2,1)S(1)} %get-tuple-element.20), channel_id=1, source_target_pairs={{0,17},{1,16},{2,19},{3,18},{4,21},{5,20},{6,23},{7,22},{8,9},{9,8... | collective-permute-start | bytes 49160 | tf_op jit(solution)/shard_map/ppermute | solution.py:372
  14.8 3.8 %collective-permute-start.6 = (bf16[32,256]{1,0:T(8,128)(2,1)S(1)}, bf16[32,256]{1,0:T(8,128)(2,1)S(1)}, u32[]{:S(2)}, u32[]{:S(2)}) collective-permute-start(bf16[32,256]{1,0:T(8,128)(2,1)S(1)} %get-tuple-element.21), channel_id=1, source_target_pairs={{0,25},{1,24},{2,27},{3,26},{4,29},{5,28},{6,31},{7,30},{8,1},{9,0... | collective-permute-start | bytes 49160 | tf_op jit(solution)/shard_map/ppermute | solution.py:372
  17.1 1.5 %collective-permute-start.5 = (bf16[32,256]{1,0:T(8,128)(2,1)S(1)}, bf16[32,256]{1,0:T(8,128)(2,1)S(1)}, u32[]{:S(2)}, u32[]{:S(2)}) collective-permute-start(bf16[32,256]{1,0:T(8,128)(2,1)S(1)} %get-tuple-element.22), channel_id=1, source_target_pairs={{0,1},{1,0},{2,3},{3,2},{4,5},{5,4},{6,7},{7,6},{8,17},{9,16},{10,... | collective-permute-start | bytes 49160 | tf_op jit(solution)/shard_map/ppermute | solution.py:372

commit v7 on v6

--- a/solution.py
+++ b/solution.py
@@ -17,10 +17,10 @@
 TAPS = 8
 LANES = 128
 QUARTERS = NX // LANES
-GROUP = LANES // QUARTERS
 PLANES = 32
 CHUNKS = 4
-UNROLL = 8
+UNROLL = 16
+PARTS = 4
 ROWS = QUARTERS * KY
 PITCH = 2 * ROWS + 1
 bf16, f32 = jnp.bfloat16, jnp.float32
@@ -43,8 +43,9 @@
 
 
 def column_of(q):
-    group, lane = np.arange(LANES) // GROUP, np.arange(LANES) % GROUP
-    return 4 * (GROUP * ((group - q) % QUARTERS) + lane) + q
+    place = np.arange(LANES)
+    quarter = (place - q) % QUARTERS
+    return 4 * (LANES // QUARTERS * quarter + (place - q - quarter) % LANES // 4) + q
 
 
 def fourier_table():
@@ -55,8 +56,8 @@
     return out.reshape(QUARTERS, LANES, 2 * LANES).astype(jnp.bfloat16)
 
 
-def factor_table():
-    taps = lanczos_taps(XBINS).astype(np.float64)
+def factor_table(scale):
+    taps = scale * lanczos_taps(XBINS).astype(np.float64)
     out = np.zeros((XBINS, QUARTERS, 2, LANES))
     for q in range(QUARTERS):
         shift = 2.0 * np.pi * (((np.arange(TAPS) - 3)[:, None] * column_of(q)[None, :]) % NX) / NX
@@ -64,12 +65,11 @@
     return out.reshape(XBINS, 2 * NX).astype(np.float32)
 
 
-def order_table():
-    out = np.zeros((QUARTERS, LANES, LANES), np.float32)
-    group, lane = np.arange(LANES) // GROUP, np.arange(LANES) % GROUP
-    for quarter in range(QUARTERS):
-        out[quarter, np.arange(LANES), 4 * lane + (group - quarter) % QUARTERS] = 1.0
-    return out.astype(jnp.bfloat16)
+def z_table(planes):
+    z = np.arange(planes)
+    angle = 2.0 * np.pi * ((z[:, None] * z[None, :]) % planes) / planes
+    cos, sin = np.cos(angle), np.sin(angle)
+    return np.stack([np.concatenate([cos, sin]), np.concatenate([-sin, cos])])
 
 
 def sine_coefficients(terms=5):
@@ -93,41 +93,43 @@
     return (ar + cr, ai + ci), (br - di, bi + dr), (ar - cr, ai - ci), (br + di, bi - dr)
 
 
-def transform(w_ref, ky_low, spread_ref, table_ref, factor_ref, u_ref, v_ref, put):
-    number = spread_ref.shape[1]
+def transform(w_ref, ky_low, spread_ref, table_ref, factor_ref, v_ref, put):
+    number = spread_ref.shape[1] // 2
+    count = number // PARTS
+    for at in range(0, number, count):
+        sums = []
+        for y in range(2):
+
+            def column(r, p):
+                return w_ref[pl.ds(at * PITCH + r * ROWS + p * KY + 2 * y + ky_low, count, stride=PITCH), :]
+
+            sums.append(quarter_sums([(column(0, p), column(1, p)) for p in range(QUARTERS)]))
+        for q in range(QUARTERS):
+            rows = jnp.concatenate([sums[y][q][r] for r in range(2) for y in range(2)], axis=0).astype(bf16)
+            both = jnp.dot(rows, table_ref[q], preferred_element_type=f32)
+            real = both[: 2 * count, :LANES] - both[2 * count :, LANES:]
+            imag = both[: 2 * count, LANES:] + both[2 * count :, :LANES]
+            by_real, by_imag = (
+                factor_ref[at : at + count, (2 * q + s) * LANES : (2 * q + s + 1) * LANES] for s in range(2)
+            )
+            for y in range(2):
+                part = slice(y * count, (y + 1) * count)
+                to = slice((y * QUARTERS + q) * LANES, (y * QUARTERS + q + 1) * LANES)
+                v_ref[at : at + count, to] = (real[part] * by_real - imag[part] * by_imag).astype(bf16)
+                v_ref[number + at : number + at + count, to] = (
+                    real[part] * by_imag + imag[part] * by_real
+                ).astype(bf16)
+    group = lax.broadcasted_iota(jnp.int32, (CLASSES * 2 * PLANES, LANES), 1) % QUARTERS
     for y in range(2):
-
-        def column(r, p):
-            return w_ref[pl.ds(r * ROWS + p * KY + 2 * y + ky_low, number, stride=PITCH), :]
-
-        sums = quarter_sums([(column(0, p), column(1, p)) for p in range(QUARTERS)])
-        for q in range(QUARTERS):
-            for r in range(2):
-                at = (r * 2 + y) * number
-                u_ref[q, at : at + number, :] = sums[q][r].astype(bf16)
-    for q in range(QUARTERS):
-        both = jnp.dot(u_ref[q], table_ref[q], preferred_element_type=f32)
-        real = both[: 2 * number, :LANES] - both[2 * number :, LANES:]
-        imag = both[: 2 * number, LANES:] + both[2 * number :, :LANES]
-        by_real, by_imag = (factor_ref[:, (2 * q + s) * LANES : (2 * q + s + 1) * LANES] for s in range(2))
-        for y in range(2):
-            rows = slice(y * number, (y + 1) * number)
-            at = (y * QUARTERS + q) * 2 * LANES
-            v_ref[:, at : at + LANES] = (real[rows] * by_real - imag[rows] * by_imag).astype(bf16)
-            v_ref[:, at + LANES : at + 2 * LANES] = (real[rows] * by_imag + imag[rows] * by_real).astype(bf16)
-    group = lax.broadcasted_iota(jnp.int32, (CLASSES * PLANES, 2 * LANES), 1) % LANES // GROUP
-    for y in range(2):
-        part = jnp.dot(
-            spread_ref[...], v_ref[:, y * 2 * NX : (y + 1) * 2 * NX], preferred_element_type=f32
-        )
-        parts = [part[:, q * 2 * LANES : (q + 1) * 2 * LANES] for q in range(QUARTERS)]
+        part = jnp.dot(spread_ref[...], v_ref[:, y * NX : (y + 1) * NX], preferred_element_type=f32)
+        parts = [part[:, q * LANES : (q + 1) * LANES] for q in range(QUARTERS)]
         for quarter in range(QUARTERS):
             value = parts[-quarter % QUARTERS]
             for j in range(1, QUARTERS):
                 value = jnp.where(group == j, parts[(j - quarter) % QUARTERS], value)
             value = value.astype(bf16)
             for cls in range(CLASSES):
-                put(y, cls, quarter, value[cls * PLANES : (cls + 1) * PLANES])
+                put(y, cls, quarter, value[cls * 2 * PLANES : (cls + 1) * 2 * PLANES])
 
 
 def spread_matrix(pose, label, planes, first_plane):
@@ -164,9 +166,9 @@
     return put
 
 
-def first_kernel(planes, x_hbm, focus_hbm, pose_hbm, label_hbm, turns_hbm, bins_hbm, table_hbm,
+def first_kernel(planes, x_hbm, focus_hbm, pose_hbm, label_hbm, turns_hbm, bins_hbm, along_z_hbm, table_hbm,
                  out_ref, w_ref, spread_ref, table_ref, factor_ref,
-                 x_ref, focus_ref, pose_ref, label_ref, turns_ref, bins_ref, wide_ref, u_ref, v_ref, sems):
+                 x_ref, focus_ref, pose_ref, label_ref, turns_ref, bins_ref, along_z_ref, wide_ref, v_ref, sems):
     number = wide_ref.shape[0]
     chunk = x_ref.shape[0] // CHUNKS
 
@@ -184,19 +186,20 @@
                 (pose_hbm, pose_ref),
                 (label_hbm, label_ref),
                 (bins_hbm, bins_ref),
+                (along_z_hbm, along_z_ref),
             )
         )
     ]
     parts = [
-        copy(x_hbm.at[pl.ds(c * chunk, chunk)], x_ref.at[pl.ds(c * chunk, chunk)], 5 + c) for c in range(CHUNKS)
+        copy(x_hbm.at[pl.ds(c * chunk, chunk)], x_ref.at[pl.ds(c * chunk, chunk)], 6 + c) for c in range(CHUNKS)
     ]
-    table = copy(table_hbm, table_ref, 5 + CHUNKS)
+    table = copy(table_hbm, table_ref, 6 + CHUNKS)
     for made in small:
         made.wait()
     core = lax.axis_index("img") % 2
     coefficients = [float(v) for v in sine_coefficients()]
     wide_ref[...] = jnp.broadcast_to(focus_ref[...].astype(f32), (LANES, number)).T
-    spread_ref[...] = spread_matrix(pose_ref[...], label_ref[...], planes, 0)
+    planar = spread_matrix(pose_ref[...], label_ref[...], planes, 0)
     xbin = jnp.broadcast_to((pose_ref[...] % XBINS).astype(f32), (LANES, number)).T
     for at in range(0, 2 * NX, LANES):
         chosen = bins_ref[0:1, at : at + LANES]
@@ -223,32 +226,22 @@
         parts[c].wait()
         lax.fori_loop(c * number // CHUNKS, (c + 1) * number // CHUNKS, weigh, 0, unroll=UNROLL)
     table.wait()
-    transform(w_ref, 1 - core, spread_ref, table_ref, factor_ref, u_ref, v_ref, place(out_ref, 1 - core))
-
-
-def second_kernel(w_ref, spread_ref, table_ref, factor_ref, out_ref, u_ref, v_ref):
+    for s in range(2):
+        spread = jnp.dot(along_z_ref[s], planar, preferred_element_type=f32).astype(bf16)
+        spread_ref[:, s * number : (s + 1) * number] = spread
+    transform(w_ref, 1 - core, spread_ref, table_ref, factor_ref, v_ref, place(out_ref, 1 - core))
+
+
+def second_kernel(w_ref, spread_ref, table_ref, factor_ref, out_ref, v_ref):
     core = lax.axis_index("img") % 2
-    transform(w_ref, core, spread_ref, table_ref, factor_ref, u_ref, v_ref, place(out_ref, core))
-
-
-def last_kernel(scale, *refs):
-    *got_refs, order_ref, table_ref, out_ref = refs
+    transform(w_ref, core, spread_ref, table_ref, factor_ref, v_ref, place(out_ref, core))
+
+
+def last_kernel(*refs):
+    *got_refs, out_ref = refs
+    quarter = lax.axis_index("slab") % QUARTERS
     total = sum(got_ref[...].astype(f32) for got_ref in got_refs)
-    total = total.astype(bf16)
-    order = order_ref[lax.axis_index("slab") % QUARTERS]
-    turned = 0.0
-    for s in range(2):
-        part = total[:, s * LANES : (s + 1) * LANES]
-        part = jnp.dot(part, order, preferred_element_type=f32).astype(bf16)
-        turned += jnp.dot(table_ref[s], part, preferred_element_type=f32)
-    out_ref[...] = turned * scale
-
-
-def z_table(planes):
-    z = np.arange(planes)
-    angle = 2.0 * np.pi * ((z[:, None] * z[None, :]) % planes) / planes
-    cos, sin = np.cos(angle), np.sin(angle)
-    return np.stack([np.concatenate([cos, sin]), np.concatenate([-sin, cos])]).astype(jnp.bfloat16)
+    out_ref[...] = pltpu.roll(total, (LANES - quarter) % LANES, 1)
 
 
 VMEM = pl.BlockSpec(memory_space=pltpu.VMEM)
@@ -291,7 +284,8 @@
     planes = owners * 4
     weighted = (ctf_weights(defocus)[:, None] * images.astype(f32)).astype(bf16)
     table = jnp.asarray(fourier_table()).reshape(QUARTERS, LANES, 2, LANES)
-    factors = jnp.asarray(factor_table()).reshape(XBINS, QUARTERS, 2, LANES)[pose_bins % XBINS]
+    scale = 2.5 / math.sqrt(number * owners * groups * NX)
+    factors = jnp.asarray(factor_table(scale)).reshape(XBINS, QUARTERS, 2, LANES)[pose_bins % XBINS]
     by_real, by_imag = (jnp.moveaxis(factors[:, :, s], 0, 1)[:, :, None] for s in range(2))
     quarters = jnp.moveaxis(weighted.astype(f32).reshape(number, 2, KY, QUARTERS, LANES), 3, 0)
     sums = quarter_sums([(part[:, 0], part[:, 1]) for part in quarters])
@@ -312,8 +306,7 @@
     total = lax.psum_scatter(parts, "img", scatter_dimension=0, tiled=True)
     total = lax.psum_scatter(total, "slab", scatter_dimension=1, tiled=True)
     table = jnp.asarray(z_table(planes).astype(np.float32)).reshape(2, 2, planes, planes)
-    scale = 2.5 / math.sqrt(number * owners * groups * NX)
-    return scale * jnp.einsum("yqsz,stwz->yqtw", total, table, precision=lax.Precision.HIGHEST)
+    return jnp.einsum("yqsz,stwz->yqtw", total, table, precision=lax.Precision.HIGHEST)
 
 
 def on_device(images, pose_bins, labels, defocus):
@@ -326,17 +319,18 @@
     x = images.reshape(number, 2, KY, QUARTERS, LANES).transpose(0, 1, 3, 2, 4).reshape(number * 2 * ROWS, LANES)
     pieces = 2 * CLASSES * QUARTERS
     w_shape = jax.ShapeDtypeStruct((number * PITCH, LANES), f32)
-    spread_shape = jax.ShapeDtypeStruct((CLASSES * PLANES, number), bf16)
-    piece_shape = jax.ShapeDtypeStruct((pieces, PLANES, 2 * LANES), bf16)
+    spread_shape = jax.ShapeDtypeStruct((CLASSES * 2 * PLANES, 2 * number), bf16)
+    piece_shape = jax.ShapeDtypeStruct((pieces, 2 * PLANES, LANES), bf16)
     table = jnp.asarray(fourier_table())
     table_shape = jax.ShapeDtypeStruct(table.shape, bf16)
-    bins = jnp.asarray(factor_table())
+    bins = jnp.asarray(factor_table(scale))
+    along_z = jnp.asarray(np.stack([np.kron(np.eye(CLASSES), part) for part in z_table(planes)]).astype(jnp.bfloat16))
     factor_shape = jax.ShapeDtypeStruct((number, 2 * NX), f32)
-    work = [pltpu.VMEM((QUARTERS, 4 * number, LANES), bf16), pltpu.VMEM((number, 4 * NX), bf16)]
+    work = [pltpu.VMEM((2 * number, 2 * NX), bf16)]
     other, *near = pl.pallas_call(
         functools.partial(first_kernel, planes),
         out_shape=(piece_shape, w_shape, spread_shape, table_shape, factor_shape),
-        in_specs=[HBM] * 7,
+        in_specs=[HBM] * 8,
         out_specs=(VMEM,) * 5,
         scratch_shapes=[
             pltpu.VMEM(x.shape, bf16),
@@ -345,15 +339,16 @@
             pltpu.VMEM((1, number), jnp.int32),
             pltpu.VMEM((ROWS, LANES), f32),
             pltpu.VMEM(bins.shape, f32),
+            pltpu.VMEM(along_z.shape, bf16),
             pltpu.VMEM((number, LANES), f32),
             *work,
-            pltpu.SemaphoreType.DMA((CHUNKS + 6,)),
+            pltpu.SemaphoreType.DMA((CHUNKS + 7,)),
         ],
         compiler_params=pltpu.CompilerParams(vmem_limit_bytes=32 << 20),
         name="weigh_and_transform_other",
     )(*(
         pltpu.with_memory_space_constraint(v, pltpu.HBM)
-        for v in (x, defocus[None], pose_bins[None], labels[None], jnp.asarray(turns_per_defocus()), bins, table)
+        for v in (x, defocus[None], pose_bins[None], labels[None], jnp.asarray(turns_per_defocus()), bins, along_z, table)
     ))
     axes = ("slab", "img")
     got = lax.ppermute(other, axes, [(i, i ^ 1) for i in range(owners * groups)])
@@ -371,13 +366,13 @@
     total = sum(g.astype(f32) for g in got).astype(bf16)
     got = [lax.ppermute(total[slot], axes, pairs_of(1, slot)) for slot in SECOND_LISTED]
     out = pl.pallas_call(
-        functools.partial(last_kernel, scale),
+        last_kernel,
         out_shape=jax.ShapeDtypeStruct((2 * planes, LANES), f32),
-        in_specs=[VMEM] * 6,
+        in_specs=[VMEM] * 4,
         out_specs=VMEM,
         compiler_params=pltpu.CompilerParams(vmem_limit_bytes=16 << 20),
-        name="transform_planes",
-    )(*got, jnp.asarray(order_table()), jnp.asarray(z_table(planes)))
+        name="add_last",
+    )(*got)
     return out.reshape(1, 2, planes, LANES).transpose(0, 3, 1, 2)
 
 

time: 19.7 us -> 19.5 us (0.990)
  the two profiles are of different devices: /device:TPU:3 before, /device:TPU:0 now
where the time goes in v7:
time: 19.5 us; the launch traced here: 19.2 us
  starting transfers between devices  10.4 us (53%)
  waiting for transfers between devices  4.69 us (24%)
  Pallas kernels  3.93 us (20%)
    ppermute x4, starting transfers between devices, on_device(): lax.ppermute(total[4 * slot:4 * slot + 4], axes, pairs_of(0, slot))  5.71 us
    ppermute x4, starting transfers between devices, on_device(): lax.ppermute(total[slot], axes, pairs_of(1, slot))  4.15 us
    pallas_call x1, Pallas kernels, on_device(): pl.pallas_call(functools.partial(first_kernel, planes), out_shape=(piece_...  2.55 us
    ppermute x4, waiting for transfers between devices, on_device(): lax.ppermute(total[4 * slot:4 * slot + 4], axes, pairs_of(0, slot))  2.27 us
    ppermute x4, waiting for transfers between devices, on_device(): lax.ppermute(total[slot], axes, pairs_of(1, slot))  1.94 us
    pallas_call x1, Pallas kernels, on_device(): pl.pallas_call(last_kernel, out_shape=jax.ShapeDtypeStruct((2 * planes, L...  0.7 us
    pallas_call x1, Pallas kernels, on_device(): pl.pallas_call(second_kernel, out_shape=piece_shape, in_specs=[VMEM] * 4,...  0.67 us
    ppermute x1, starting transfers between devices, on_device(): lax.ppermute(other, axes, [(i, i ^ 1) for i in range(owners * groups)])  0.52 us
  transfers between devices with their start and end apart: 9, of which 7 were waited for; matrix products, arithmetic and copies ran while one was open for 0% of the time, Pallas kernels for 4%

profile of v7, /device:TPU:0, one launch (start us, length us, event | category | flops | bytes accessed | tf_op | source)
XLA Modules:
  0.0 19.2 jit_solution(11919798208841519777)
XLA Ops:
  0.0 2.6 %weigh_and_transform_other.1 = (bf16[16,64,128]{2,1,0:T(8,128)(2,1)S(1)}, f32[4224,128]{1,0:T(8,128)S(1)}, bf16[128,256]{1,0:T(8,128)(2,1)S(1)}, bf16[4,128,256]{2,1,0:T(8,128)(2,1)S(1)}, f32[128,1024]{1,0:T(8,128)S(1)}) custom-call(bf16[4096,128]{1,0:T(8,128)(2,1)} %bitcast.19, bf16[1,128]{1,0:T(2,128)(2,1)} %bitcast.20, s32[1,128]{1,0:T(1,128)} %bitcast.21, ...), custom_call_target="tpu_custom_call" | custom-call | tf_op jit(solution)/shard_map/weigh_and_transform_other/pallas_call | solution.py:330
  2.6 0.5 %collective-permute-start = (bf16[16,64,128]{2,1,0:T(8,128)(2,1)S(1)}, bf16[16,64,128]{2,1,0:T(8,128)(2,1)S(1)}, u32[]{:S(2)}, u32[]{:S(2)}) collective-permute-start(bf16[16,64,128]{2,1,0:T(8,128)(2,1)S(1)} %get-tuple-element.14), channel_id=1, source_target_pairs={{0,1},{1,0},{2,3},{3,2},{4,5},{5,4},{6,7},{7,6},{8,9},{9,8},{10,11... | collective-permute-start | bytes 786440 | tf_op jit(solution)/shard_map/ppermute | solution.py:354
  3.1 0.7 %transform_own.1 = bf16[16,64,128]{2,1,0:T(8,128)(2,1)S(1)} custom-call(f32[4224,128]{1,0:T(8,128)S(1)} %get-tuple-element.10.w_ref, bf16[128,256]{1,0:T(8,128)(2,1)S(1)} %get-tuple-element.11.spread_ref, bf16[4,128,256]{2,1,0:T(8,128)(2,1)S(1)} %get-tuple-element.12.table_ref, f32[128,1024]{1,0:T(8,128)S(1)} %get-tuple-element.13.factor_ref), custom_call_target="tpu_custom_call" | custom-call | tf_op jit(solution)/shard_map/transform_own/pallas_call | solution.py:355
  3.8 0.5 %collective-permute-done = bf16[16,64,128]{2,1,0:T(8,128)(2,1)S(1)} collective-permute-done((bf16[16,64,128]{2,1,0:T(8,128)(2,1)S(1)}, bf16[16,64,128]{2,1,0:T(8,128)(2,1)S(1)}, u32[]{:S(2)}, u32[]{:S(2)}) %collective-permute-start) | collective-permute-done | bytes 262176 | tf_op jit(solution)/shard_map/ppermute | solution.py:354
  4.2 0.1 add_convert_fusion
  4.3 2.7 %collective-permute-start.1 = (bf16[4,64,128]{2,1,0:T(8,128)(2,1)S(1)}, bf16[4,64,128]{2,1,0:T(8,128)(2,1)S(1)}, u32[]{:S(2)}, u32[]{:S(2)}) collective-permute-start(bf16[4,64,128]{2,1,0:T(8,128)(2,1)S(1)} %get-tuple-element.15), channel_id=1, source_target_pairs={{0,3},{1,2},{2,1},{3,0},{4,5},{5,4},{6,7},{7,6},{8,11},{9,10},{10,... | collective-permute-start | bytes 196616 | tf_op jit(solution)/shard_map/ppermute | solution.py:365
  7.0 0.3 %collective-permute-start.4 = (bf16[4,64,128]{2,1,0:T(8,128)(2,1)S(1)}, bf16[4,64,128]{2,1,0:T(8,128)(2,1)S(1)}, u32[]{:S(2)}, u32[]{:S(2)}) collective-permute-start(bf16[4,64,128]{2,1,0:T(8,128)(2,1)S(1)} %get-tuple-element.16), channel_id=1, source_target_pairs={{0,5},{1,4},{2,7},{3,6},{4,3},{5,2},{6,1},{7,0},{8,13},{9,12},{10,... | collective-permute-start | bytes 196616 | tf_op jit(solution)/shard_map/ppermute | solution.py:365
  7.4 2.3 %collective-permute-start.3 = (bf16[4,64,128]{2,1,0:T(8,128)(2,1)S(1)}, bf16[4,64,128]{2,1,0:T(8,128)(2,1)S(1)}, u32[]{:S(2)}, u32[]{:S(2)}) collective-permute-start(bf16[4,64,128]{2,1,0:T(8,128)(2,1)S(1)} %get-tuple-element.17), channel_id=1, source_target_pairs={{0,7},{1,6},{2,5},{3,4},{4,1},{5,0},{6,3},{7,2},{8,15},{9,14},{10,... | collective-permute-start | bytes 196616 | tf_op jit(solution)/shard_map/ppermute | solution.py:365
  9.7 0.4 %collective-permute-start.2 = (bf16[4,64,128]{2,1,0:T(8,128)(2,1)S(1)}, bf16[4,64,128]{2,1,0:T(8,128)(2,1)S(1)}, u32[]{:S(2)}, u32[]{:S(2)}) collective-permute-start(bf16[4,64,128]{2,1,0:T(8,128)(2,1)S(1)} %get-tuple-element.18), channel_id=1, source_target_pairs={{0,1},{1,0},{2,3},{3,2},{4,7},{5,6},{6,5},{7,4},{8,9},{9,8},{10,11... | collective-permute-start | bytes 196616 | tf_op jit(solution)/shard_map/ppermute | solution.py:365
  10.1 0.5 %collective-permute-done.1 = bf16[4,64,128]{2,1,0:T(8,128)(2,1)S(1)} collective-permute-done((bf16[4,64,128]{2,1,0:T(8,128)(2,1)S(1)}, bf16[4,64,128]{2,1,0:T(8,128)(2,1)S(1)}, u32[]{:S(2)}, u32[]{:S(2)}) %collective-permute-start.1) | collective-permute-done | bytes 65568 | tf_op jit(solution)/shard_map/ppermute | solution.py:365
  10.6 1.3 %collective-permute-done.4 = bf16[4,64,128]{2,1,0:T(8,128)(2,1)S(1)} collective-permute-done((bf16[4,64,128]{2,1,0:T(8,128)(2,1)S(1)}, bf16[4,64,128]{2,1,0:T(8,128)(2,1)S(1)}, u32[]{:S(2)}, u32[]{:S(2)}) %collective-permute-start.4) | collective-permute-done | bytes 65568 | tf_op jit(solution)/shard_map/ppermute | solution.py:365
  11.9 0.5 %collective-permute-done.3 = bf16[4,64,128]{2,1,0:T(8,128)(2,1)S(1)} collective-permute-done((bf16[4,64,128]{2,1,0:T(8,128)(2,1)S(1)}, bf16[4,64,128]{2,1,0:T(8,128)(2,1)S(1)}, u32[]{:S(2)}, u32[]{:S(2)}) %collective-permute-start.3) | collective-permute-done | bytes 65568 | tf_op jit(solution)/shard_map/ppermute | solution.py:365
  12.3 0.0 collective-permute-done.2
  12.4 1.6 %collective-permute-start.8 = (bf16[64,128]{1,0:T(8,128)(2,1)S(1)}, bf16[64,128]{1,0:T(8,128)(2,1)S(1)}, u32[]{:S(2)}, u32[]{:S(2)}) collective-permute-start(bf16[64,128]{1,0:T(8,128)(2,1)S(1)} %get-tuple-element.19), channel_id=1, source_target_pairs={{0,9},{1,8},{2,11},{3,10},{4,13},{5,12},{6,15},{7,14},{8,25},{9,24... | collective-permute-start | bytes 49160 | tf_op jit(solution)/shard_map/ppermute | solution.py:367
  13.9 1.2 %collective-permute-start.7 = (bf16[64,128]{1,0:T(8,128)(2,1)S(1)}, bf16[64,128]{1,0:T(8,128)(2,1)S(1)}, u32[]{:S(2)}, u32[]{:S(2)}) collective-permute-start(bf16[64,128]{1,0:T(8,128)(2,1)S(1)} %get-tuple-element.20), channel_id=1, source_target_pairs={{0,17},{1,16},{2,19},{3,18},{4,21},{5,20},{6,23},{7,22},{8,9},{9,8... | collective-permute-start | bytes 49160 | tf_op jit(solution)/shard_map/ppermute | solution.py:367
  15.1 1.2 %collective-permute-start.6 = (bf16[64,128]{1,0:T(8,128)(2,1)S(1)}, bf16[64,128]{1,0:T(8,128)(2,1)S(1)}, u32[]{:S(2)}, u32[]{:S(2)}) collective-permute-start(bf16[64,128]{1,0:T(8,128)(2,1)S(1)} %get-tuple-element.21), channel_id=1, source_target_pairs={{0,25},{1,24},{2,27},{3,26},{4,29},{5,28},{6,31},{7,30},{8,1},{9,0... | collective-permute-start | bytes 49160 | tf_op jit(solution)/shard_map/ppermute | solution.py:367
  16.3 0.2 %collective-permute-start.5 = (bf16[64,128]{1,0:T(8,128)(2,1)S(1)}, bf16[64,128]{1,0:T(8,128)(2,1)S(1)}, u32[]{:S(2)}, u32[]{:S(2)}) collective-permute-start(bf16[64,128]{1,0:T(8,128)(2,1)S(1)} %get-tuple-element.22), channel_id=1, source_target_pairs={{0,1},{1,0},{2,3},{3,2},{4,5},{5,4},{6,7},{7,6},{8,17},{9,16},{10,... | collective-permute-start | bytes 49160 | tf_op jit(solution)/shard_map/ppermute | solution.py:367
  16.5 0.9 %collective-permute-done.8.refs_3_ = bf16[64,128]{1,0:T(8,128)(2,1)S(1)} collective-permute-done((bf16[64,128]{1,0:T(8,128)(2,1)S(1)}, bf16[64,128]{1,0:T(8,128)(2,1)S(1)}, u32[]{:S(2)}, u32[]{:S(2)}) %collective-permute-start.8) | collective-permute-done | bytes 16416 | tf_op jit(solution)/shard_map/ppermute | solution.py:367
  17.4 0.7 %collective-permute-done.7.refs_2_ = bf16[64,128]{1,0:T(8,128)(2,1)S(1)} collective-permute-done((bf16[64,128]{1,0:T(8,128)(2,1)S(1)}, bf16[64,128]{1,0:T(8,128)(2,1)S(1)}, u32[]{:S(2)}, u32[]{:S(2)}) %collective-permute-start.7) | collective-permute-done | bytes 16416 | tf_op jit(solution)/shard_map/ppermute | solution.py:367
  18.1 0.4 %collective-permute-done.6.refs_1_ = bf16[64,128]{1,0:T(8,128)(2,1)S(1)} collective-permute-done((bf16[64,128]{1,0:T(8,128)(2,1)S(1)}, bf16[64,128]{1,0:T(8,128)(2,1)S(1)}, u32[]{:S(2)}, u32[]{:S(2)}) %collective-permute-start.6) | collective-permute-done | bytes 16416 | tf_op jit(solution)/shard_map/ppermute | solution.py:367
  18.5 0.0 collective-permute-done.5.refs_0_
  18.5 0.7 %add_last.1 = f32[64,128]{1,0:T(8,128)} custom-call(bf16[64,128]{1,0:T(8,128)(2,1)S(1)} %collective-permute-done.5.refs_0_, bf16[64,128]{1,0:T(8,128)(2,1)S(1)} %collective-permute-done.6.refs_1_, bf16[64,128]{1,0:T(8,128)(2,1)S(1)} %collective-permute-done.7.refs_2_, bf16[64,128]{1,0:T(8,128)(2,1)S(1)} %collective-permute-done.8.refs_3_), custom_call_target="tpu_custom_call" | custom-call | tf_op jit(solution)/shard_map/add_last/pallas_call | solution.py:368
  (3 shorter events, 0.1 us)
Async XLA Ops:
  2.6 1.7 %collective-permute-start = (bf16[16,64,128]{2,1,0:T(8,128)(2,1)S(1)}, bf16[16,64,128]{2,1,0:T(8,128)(2,1)S(1)}, u32[]{:S(2)}, u32[]{:S(2)}) collective-permute-start(bf16[16,64,128]{2,1,0:T(8,128)(2,1)S(1)} %get-tuple-element.14), channel_id=1, source_target_pairs={{0,1},{1,0},{2,3},{3,2},{4,5},{5,4},{6,7},{7,6},{8,9},{9,8},{10,11... | collective-permute-start | bytes 786440 | tf_op jit(solution)/shard_map/ppermute | solution.py:354
  4.3 6.2 %collective-permute-start.1 = (bf16[4,64,128]{2,1,0:T(8,128)(2,1)S(1)}, bf16[4,64,128]{2,1,0:T(8,128)(2,1)S(1)}, u32[]{:S(2)}, u32[]{:S(2)}) collective-permute-start(bf16[4,64,128]{2,1,0:T(8,128)(2,1)S(1)} %get-tuple-element.15), channel_id=1, source_target_pairs={{0,3},{1,2},{2,1},{3,0},{4,5},{5,4},{6,7},{7,6},{8,11},{9,10},{10,... | collective-permute-start | bytes 196616 | tf_op jit(solution)/shard_map/ppermute | solution.py:365
  7.0 4.8 %collective-permute-start.4 = (bf16[4,64,128]{2,1,0:T(8,128)(2,1)S(1)}, bf16[4,64,128]{2,1,0:T(8,128)(2,1)S(1)}, u32[]{:S(2)}, u32[]{:S(2)}) collective-permute-start(bf16[4,64,128]{2,1,0:T(8,128)(2,1)S(1)} %get-tuple-element.16), channel_id=1, source_target_pairs={{0,5},{1,4},{2,7},{3,6},{4,3},{5,2},{6,1},{7,0},{8,13},{9,12},{10,... | collective-permute-start | bytes 196616 | tf_op jit(solution)/shard_map/ppermute | solution.py:365
  7.4 4.9 %collective-permute-start.3 = (bf16[4,64,128]{2,1,0:T(8,128)(2,1)S(1)}, bf16[4,64,128]{2,1,0:T(8,128)(2,1)S(1)}, u32[]{:S(2)}, u32[]{:S(2)}) collective-permute-start(bf16[4,64,128]{2,1,0:T(8,128)(2,1)S(1)} %get-tuple-element.17), channel_id=1, source_target_pairs={{0,7},{1,6},{2,5},{3,4},{4,1},{5,0},{6,3},{7,2},{8,15},{9,14},{10,... | collective-permute-start | bytes 196616 | tf_op jit(solution)/shard_map/ppermute | solution.py:365
  9.7 2.6 %collective-permute-start.2 = (bf16[4,64,128]{2,1,0:T(8,128)(2,1)S(1)}, bf16[4,64,128]{2,1,0:T(8,128)(2,1)S(1)}, u32[]{:S(2)}, u32[]{:S(2)}) collective-permute-start(bf16[4,64,128]{2,1,0:T(8,128)(2,1)S(1)} %get-tuple-element.18), channel_id=1, source_target_pairs={{0,1},{1,0},{2,3},{3,2},{4,7},{5,6},{6,5},{7,4},{8,9},{9,8},{10,11... | collective-permute-start | bytes 196616 | tf_op jit(solution)/shard_map/ppermute | solution.py:365
  12.4 5.0 %collective-permute-start.8 = (bf16[64,128]{1,0:T(8,128)(2,1)S(1)}, bf16[64,128]{1,0:T(8,128)(2,1)S(1)}, u32[]{:S(2)}, u32[]{:S(2)}) collective-permute-start(bf16[64,128]{1,0:T(8,128)(2,1)S(1)} %get-tuple-element.19), channel_id=1, source_target_pairs={{0,9},{1,8},{2,11},{3,10},{4,13},{5,12},{6,15},{7,14},{8,25},{9,24... | collective-permute-start | bytes 49160 | tf_op jit(solution)/shard_map/ppermute | solution.py:367
  13.9 4.1 %collective-permute-start.7 = (bf16[64,128]{1,0:T(8,128)(2,1)S(1)}, bf16[64,128]{1,0:T(8,128)(2,1)S(1)}, u32[]{:S(2)}, u32[]{:S(2)}) collective-permute-start(bf16[64,128]{1,0:T(8,128)(2,1)S(1)} %get-tuple-element.20), channel_id=1, source_target_pairs={{0,17},{1,16},{2,19},{3,18},{4,21},{5,20},{6,23},{7,22},{8,9},{9,8... | collective-permute-start | bytes 49160 | tf_op jit(solution)/shard_map/ppermute | solution.py:367
  15.1 3.3 %collective-permute-start.6 = (bf16[64,128]{1,0:T(8,128)(2,1)S(1)}, bf16[64,128]{1,0:T(8,128)(2,1)S(1)}, u32[]{:S(2)}, u32[]{:S(2)}) collective-permute-start(bf16[64,128]{1,0:T(8,128)(2,1)S(1)} %get-tuple-element.21), channel_id=1, source_target_pairs={{0,25},{1,24},{2,27},{3,26},{4,29},{5,28},{6,31},{7,30},{8,1},{9,0... | collective-permute-start | bytes 49160 | tf_op jit(solution)/shard_map/ppermute | solution.py:367
  16.3 2.2 %collective-permute-start.5 = (bf16[64,128]{1,0:T(8,128)(2,1)S(1)}, bf16[64,128]{1,0:T(8,128)(2,1)S(1)}, u32[]{:S(2)}, u32[]{:S(2)}) collective-permute-start(bf16[64,128]{1,0:T(8,128)(2,1)S(1)} %get-tuple-element.22), channel_id=1, source_target_pairs={{0,1},{1,0},{2,3},{3,2},{4,5},{5,4},{6,7},{7,6},{8,17},{9,16},{10,... | collective-permute-start | bytes 49160 | tf_op jit(solution)/shard_map/ppermute | solution.py:367

commit v8 on v7

--- a/solution.py
+++ b/solution.py
@@ -93,7 +93,7 @@
     return (ar + cr, ai + ci), (br - di, bi + dr), (ar - cr, ai - ci), (br + di, bi - dr)
 
 
-def transform(w_ref, ky_low, spread_ref, table_ref, factor_ref, v_ref, put):
+def transform(w_ref, half, ky_low, spread_ref, table_ref, factor_ref, v_ref, put):
     number = spread_ref.shape[1] // 2
     count = number // PARTS
     for at in range(0, number, count):
@@ -101,7 +101,8 @@
         for y in range(2):
 
             def column(r, p):
-                return w_ref[pl.ds(at * PITCH + r * ROWS + p * KY + 2 * y + ky_low, count, stride=PITCH), :]
+                row = p * KY + ky_low if p < 2 else jnp.where(half, (p - 2) * KY + 1 - ky_low, p * KY + ky_low)
+                return w_ref[pl.ds(at * PITCH + r * ROWS + 2 * y + row, count, stride=PITCH), :]
 
             sums.append(quarter_sums([(column(0, p), column(1, p)) for p in range(QUARTERS)]))
         for q in range(QUARTERS):
@@ -166,9 +167,52 @@
     return put
 
 
+def contrast(turns, focus):
+    coefficients = [float(v) for v in sine_coefficients()]
+    angle = turns * focus + 0.1 / (2 * math.pi)
+    f = angle - jnp.round(angle)
+    square = f * f
+    poly = coefficients[-1] * square + coefficients[-2]
+    for coefficient in coefficients[-3::-1]:
+        poly = poly * square + coefficient
+    return poly * f
+
+
+def weigher(turns_ref, wide_ref, x_ref, w_ref):
+    turns = turns_ref[...]
+
+    def weigh(i, carry):
+        ctf = contrast(turns, wide_ref[pl.ds(i, 1), :])
+        rows = x_ref[pl.ds(pl.multiple_of(i * 2 * ROWS, 2 * ROWS), 2 * ROWS), :].astype(f32)
+        w_ref[pl.ds(i * PITCH, ROWS), :] = ctf * rows[:ROWS]
+        w_ref[pl.ds(i * PITCH + ROWS, ROWS), :] = ctf * rows[ROWS:]
+        return carry
+
+    return weigh
+
+
+def half_weigher(ky_low, turns_ref, wide_ref, x_ref, w_ref):
+    stays = lax.broadcasted_iota(jnp.int32, (8, LANES), 0) % 2 == ky_low
+    shift = 1 if ky_low == 0 else 7
+
+    def wanted(first, second):
+        return jnp.where(stays, first, pltpu.roll(second, shift, 0))
+
+    turns = wanted(turns_ref[0:8, :], turns_ref[8:16, :])
+
+    def weigh(i, carry):
+        ctf = contrast(turns, wide_ref[pl.ds(i, 1), :])
+        rows = x_ref[pl.ds(pl.multiple_of(i * 2 * ROWS, 2 * ROWS), 2 * ROWS), :].astype(f32)
+        w_ref[pl.ds(i * PITCH, 8), :] = ctf * wanted(rows[0:8], rows[8:16])
+        w_ref[pl.ds(i * PITCH + ROWS, 8), :] = ctf * wanted(rows[16:24], rows[24:32])
+        return carry
+
+    return weigh
+
+
 def first_kernel(planes, x_hbm, focus_hbm, pose_hbm, label_hbm, turns_hbm, bins_hbm, along_z_hbm, table_hbm,
-                 out_ref, w_ref, spread_ref, table_ref, factor_ref,
-                 x_ref, focus_ref, pose_ref, label_ref, turns_ref, bins_ref, along_z_ref, wide_ref, v_ref, sems):
+                 out_ref, w_ref, x_ref, wide_ref, turns_ref, spread_ref, table_ref, factor_ref,
+                 focus_ref, pose_ref, label_ref, bins_ref, along_z_ref, v_ref, sems):
     number = wide_ref.shape[0]
     chunk = x_ref.shape[0] // CHUNKS
 
@@ -197,7 +241,6 @@
     for made in small:
         made.wait()
     core = lax.axis_index("img") % 2
-    coefficients = [float(v) for v in sine_coefficients()]
     wide_ref[...] = jnp.broadcast_to(focus_ref[...].astype(f32), (LANES, number)).T
     planar = spread_matrix(pose_ref[...], label_ref[...], planes, 0)
     xbin = jnp.broadcast_to((pose_ref[...] % XBINS).astype(f32), (LANES, number)).T
@@ -206,35 +249,35 @@
         for b in range(1, XBINS):
             chosen = jnp.where(xbin == b, bins_ref[b : b + 1, at : at + LANES], chosen)
         factor_ref[:, at : at + LANES] = chosen
-    turns = turns_ref[...]
-
-    def weigh(i, carry):
-        angle = turns * wide_ref[pl.ds(i, 1), :] + 0.1 / (2 * math.pi)
-        f = angle - jnp.round(angle)
-        square = f * f
-        poly = jnp.full(f.shape, coefficients[-1], f32)
-        for coefficient in coefficients[-2::-1]:
-            poly = poly * square + coefficient
-        ctf = poly * f
-        at = pl.multiple_of(i * 2 * ROWS, 2 * ROWS)
-        rows = x_ref[pl.ds(at, 2 * ROWS), :].astype(f32)
-        w_ref[pl.ds(i * PITCH, ROWS), :] = ctf * rows[:ROWS]
-        w_ref[pl.ds(i * PITCH + ROWS, ROWS), :] = ctf * rows[ROWS:]
-        return carry
-
+    full, half = weigher(turns_ref, wide_ref, x_ref, w_ref), half_weigher(1, turns_ref, wide_ref, x_ref, w_ref)
     for c in range(CHUNKS):
         parts[c].wait()
-        lax.fori_loop(c * number // CHUNKS, (c + 1) * number // CHUNKS, weigh, 0, unroll=UNROLL)
+        first, last = c * number // CHUNKS, (c + 1) * number // CHUNKS
+
+        @pl.when(core == 0)
+        def _():
+            lax.fori_loop(first, last, half, 0, unroll=UNROLL)
+
+        @pl.when(core == 1)
+        def _():
+            lax.fori_loop(first, last, full, 0, unroll=UNROLL)
+
     table.wait()
     for s in range(2):
         spread = jnp.dot(along_z_ref[s], planar, preferred_element_type=f32).astype(bf16)
         spread_ref[:, s * number : (s + 1) * number] = spread
-    transform(w_ref, 1 - core, spread_ref, table_ref, factor_ref, v_ref, place(out_ref, 1 - core))
-
-
-def second_kernel(w_ref, spread_ref, table_ref, factor_ref, out_ref, v_ref):
+    transform(w_ref, core == 0, 1 - core, spread_ref, table_ref, factor_ref, v_ref, place(out_ref, 1 - core))
+
+
+def second_kernel(w_in, x_ref, wide_ref, turns_ref, spread_ref, table_ref, factor_ref, out_ref, w_ref, v_ref):
     core = lax.axis_index("img") % 2
-    transform(w_ref, core, spread_ref, table_ref, factor_ref, v_ref, place(out_ref, core))
+
+    @pl.when(core == 0)
+    def _():
+        half = half_weigher(0, turns_ref, wide_ref, x_ref, w_ref)
+        lax.fori_loop(0, wide_ref.shape[0], half, 0, unroll=UNROLL)
+
+    transform(w_ref, core == 0, core, spread_ref, table_ref, factor_ref, v_ref, place(out_ref, core))
 
 
 def last_kernel(*refs):
@@ -318,7 +361,8 @@
     scale = 2.5 / math.sqrt(number * owners * groups * NX)
     x = images.reshape(number, 2, KY, QUARTERS, LANES).transpose(0, 1, 3, 2, 4).reshape(number * 2 * ROWS, LANES)
     pieces = 2 * CLASSES * QUARTERS
-    w_shape = jax.ShapeDtypeStruct((number * PITCH, LANES), f32)
+    w_shape = jax.ShapeDtypeStruct((number * PITCH + 40, LANES), f32)
+    turns = jnp.asarray(turns_per_defocus())
     spread_shape = jax.ShapeDtypeStruct((CLASSES * 2 * PLANES, 2 * number), bf16)
     piece_shape = jax.ShapeDtypeStruct((pieces, 2 * PLANES, LANES), bf16)
     table = jnp.asarray(fourier_table())
@@ -329,18 +373,24 @@
     work = [pltpu.VMEM((2 * number, 2 * NX), bf16)]
     other, *near = pl.pallas_call(
         functools.partial(first_kernel, planes),
-        out_shape=(piece_shape, w_shape, spread_shape, table_shape, factor_shape),
+        out_shape=(
+            piece_shape,
+            w_shape,
+            jax.ShapeDtypeStruct(x.shape, bf16),
+            jax.ShapeDtypeStruct((number, LANES), f32),
+            jax.ShapeDtypeStruct(turns.shape, f32),
+            spread_shape,
+            table_shape,
+            factor_shape,
+        ),
         in_specs=[HBM] * 8,
-        out_specs=(VMEM,) * 5,
+        out_specs=(VMEM,) * 8,
         scratch_shapes=[
-            pltpu.VMEM(x.shape, bf16),
             pltpu.VMEM((1, number), bf16),
             pltpu.VMEM((1, number), jnp.int32),
             pltpu.VMEM((1, number), jnp.int32),
-            pltpu.VMEM((ROWS, LANES), f32),
             pltpu.VMEM(bins.shape, f32),
             pltpu.VMEM(along_z.shape, bf16),
-            pltpu.VMEM((number, LANES), f32),
             *work,
             pltpu.SemaphoreType.DMA((CHUNKS + 7,)),
         ],
@@ -348,15 +398,16 @@
         name="weigh_and_transform_other",
     )(*(
         pltpu.with_memory_space_constraint(v, pltpu.HBM)
-        for v in (x, defocus[None], pose_bins[None], labels[None], jnp.asarray(turns_per_defocus()), bins, along_z, table)
+        for v in (x, defocus[None], pose_bins[None], labels[None], turns, bins, along_z, table)
     ))
     axes = ("slab", "img")
     got = lax.ppermute(other, axes, [(i, i ^ 1) for i in range(owners * groups)])
-    own = pl.pallas_call(
+    own, _ = pl.pallas_call(
         second_kernel,
-        out_shape=piece_shape,
-        in_specs=[VMEM] * 4,
-        out_specs=VMEM,
+        out_shape=(piece_shape, w_shape),
+        in_specs=[VMEM] * 7,
+        out_specs=(VMEM, VMEM),
+        input_output_aliases={0: 1},
         scratch_shapes=work,
         compiler_params=pltpu.CompilerParams(vmem_limit_bytes=16 << 20),
         name="transform_own",

time: 19.5 us -> 19.3 us (0.990)
  waiting for transfers between devices: 4.69 us -> 4.21 us
  Pallas kernels: 3.93 us -> 4.25 us
    pallas_call x1, Pallas kernels: 0.67 us -> 1.17 us  [on_device(): pl.pallas_call(second_kernel, out_shape=(piece_shape, w_shape), in_specs=...]
    ppermute x1, waiting for transfers between devices: 0.48 us -> 0.01 us  [on_device(): lax.ppermute(other, axes, [(i, i ^ 1) for i in range(owners * groups)])]
    ppermute x4, starting transfers between devices: 5.71 us -> 5.47 us  [on_device(): lax.ppermute(total[4 * slot:4 * slot + 4], axes, pairs_of(0, slot))]
    ppermute x1, starting transfers between devices: 0.52 us -> 0.73 us  [on_device(): lax.ppermute(other, axes, [(i, i ^ 1) for i in range(owners * groups)])]
  transfers between devices with their start and end apart: 9 -> 9, of which waited for: 7 -> 6; matrix products, arithmetic and copies ran while one was open for 0% -> 0% of each run, Pallas kernels for 4% -> 6%
where the time goes in v8:
time: 19.3 us; the launch traced here: 19 us
  starting transfers between devices  10.3 us (53%)
  Pallas kernels  4.25 us (22%)
  waiting for transfers between devices  4.21 us (22%)
    ppermute x4, starting transfers between devices, on_device(): lax.ppermute(total[4 * slot:4 * slot + 4], axes, pairs_of(0, slot))  5.47 us
    ppermute x4, starting transfers between devices, on_device(): lax.ppermute(total[slot], axes, pairs_of(1, slot))  4.15 us
    pallas_call x1, Pallas kernels, on_device(): pl.pallas_call(functools.partial(first_kernel, planes), out_shape=(piece_...  2.37 us
    ppermute x4, waiting for transfers between devices, on_device(): lax.ppermute(total[4 * slot:4 * slot + 4], axes, pairs_of(0, slot))  2.27 us
    ppermute x4, waiting for transfers between devices, on_device(): lax.ppermute(total[slot], axes, pairs_of(1, slot))  1.94 us
    pallas_call x1, Pallas kernels, on_device(): pl.pallas_call(second_kernel, out_shape=(piece_shape, w_shape), in_specs=...  1.17 us
    ppermute x1, starting transfers between devices, on_device(): lax.ppermute(other, axes, [(i, i ^ 1) for i in range(owners * groups)])  0.73 us
    pallas_call x1, Pallas kernels, on_device(): pl.pallas_call(last_kernel, out_shape=jax.ShapeDtypeStruct((2 * planes, L...  0.7 us
  transfers between devices with their start and end apart: 9, of which 6 were waited for; matrix products, arithmetic and copies ran while one was open for 0% of the time, Pallas kernels for 6%

profile of v8, /device:TPU:0, one launch (start us, length us, event | category | flops | bytes accessed | tf_op | source)
XLA Modules:
  0.0 19.0 jit_solution(13415396213998948799)
XLA Ops:
  0.0 2.4 %weigh_and_transform_other.1 = (bf16[16,64,128]{2,1,0:T(8,128)(2,1)S(1)}, f32[4264,128]{1,0:T(8,128)S(1)}, bf16[4096,128]{1,0:T(8,128)(2,1)S(1)}, f32[128,128]{1...) custom-call(bf16[4096,128]{1,0:T(8,128)(2,1)} %bitcast.19, ...), custom_call_target="tpu_custom_call" | custom-call | tf_op jit(solution)/shard_map/weigh_and_transform_other/pallas_call | solution.py:374
  2.4 0.7 %collective-permute-start = (bf16[16,64,128]{2,1,0:T(8,128)(2,1)S(1)}, bf16[16,64,128]{2,1,0:T(8,128)(2,1)S(1)}, u32[]{:S(2)}, u32[]{:S(2)}) collective-permute-start(bf16[16,64,128]{2,1,0:T(8,128)(2,1)S(1)} %get-tuple-element.22), channel_id=1, source_target_pairs={{0,1},{1,0},{2,3},{3,2},{4,5},{5,4},{6,7},{7,6},{8,9},{9,8},{10,11... | collective-permute-start | bytes 786440 | tf_op jit(solution)/shard_map/ppermute | solution.py:404
  3.1 1.2 %transform_own.1 = (bf16[16,64,128]{2,1,0:T(8,128)(2,1)S(1)}, f32[4264,128]{1,0:T(8,128)S(1)}) custom-call(f32[4264,128]{1,0:T(8,128)S(1)} %get-tuple-element.14.w_in, bf16[4096,128]{1,0:T(8,128)(2,1)S(1)} %get-tuple-element.15.x_ref, f32[128,128]{1,0:T(8,128)S(1)} %get-tuple-element.16.wide_ref, ...), custom_call_target="tpu_custom_call", output_to_operand_aliasing={{1}: (0, {})} | custom-call | tf_op jit(solution)/shard_map/transform_own/pallas_call | solution.py:405
  4.3 0.0 collective-permute-done
  4.3 0.1 add_convert_fusion
  4.4 2.4 %collective-permute-start.1 = (bf16[4,64,128]{2,1,0:T(8,128)(2,1)S(1)}, bf16[4,64,128]{2,1,0:T(8,128)(2,1)S(1)}, u32[]{:S(2)}, u32[]{:S(2)}) collective-permute-start(bf16[4,64,128]{2,1,0:T(8,128)(2,1)S(1)} %get-tuple-element.23), channel_id=1, source_target_pairs={{0,3},{1,2},{2,1},{3,0},{4,5},{5,4},{6,7},{7,6},{8,11},{9,10},{10,... | collective-permute-start | bytes 196616 | tf_op jit(solution)/shard_map/ppermute | solution.py:416
  6.9 0.3 %collective-permute-start.4 = (bf16[4,64,128]{2,1,0:T(8,128)(2,1)S(1)}, bf16[4,64,128]{2,1,0:T(8,128)(2,1)S(1)}, u32[]{:S(2)}, u32[]{:S(2)}) collective-permute-start(bf16[4,64,128]{2,1,0:T(8,128)(2,1)S(1)} %get-tuple-element.24), channel_id=1, source_target_pairs={{0,5},{1,4},{2,7},{3,6},{4,3},{5,2},{6,1},{7,0},{8,13},{9,12},{10,... | collective-permute-start | bytes 196616 | tf_op jit(solution)/shard_map/ppermute | solution.py:416
  7.2 2.3 %collective-permute-start.3 = (bf16[4,64,128]{2,1,0:T(8,128)(2,1)S(1)}, bf16[4,64,128]{2,1,0:T(8,128)(2,1)S(1)}, u32[]{:S(2)}, u32[]{:S(2)}) collective-permute-start(bf16[4,64,128]{2,1,0:T(8,128)(2,1)S(1)} %get-tuple-element.25), channel_id=1, source_target_pairs={{0,7},{1,6},{2,5},{3,4},{4,1},{5,0},{6,3},{7,2},{8,15},{9,14},{10,... | collective-permute-start | bytes 196616 | tf_op jit(solution)/shard_map/ppermute | solution.py:416
  9.5 0.4 %collective-permute-start.2 = (bf16[4,64,128]{2,1,0:T(8,128)(2,1)S(1)}, bf16[4,64,128]{2,1,0:T(8,128)(2,1)S(1)}, u32[]{:S(2)}, u32[]{:S(2)}) collective-permute-start(bf16[4,64,128]{2,1,0:T(8,128)(2,1)S(1)} %get-tuple-element.26), channel_id=1, source_target_pairs={{0,1},{1,0},{2,3},{3,2},{4,7},{5,6},{6,5},{7,4},{8,9},{9,8},{10,11... | collective-permute-start | bytes 196616 | tf_op jit(solution)/shard_map/ppermute | solution.py:416
  9.9 0.5 %collective-permute-done.1 = bf16[4,64,128]{2,1,0:T(8,128)(2,1)S(1)} collective-permute-done((bf16[4,64,128]{2,1,0:T(8,128)(2,1)S(1)}, bf16[4,64,128]{2,1,0:T(8,128)(2,1)S(1)}, u32[]{:S(2)}, u32[]{:S(2)}) %collective-permute-start.1) | collective-permute-done | bytes 65568 | tf_op jit(solution)/shard_map/ppermute | solution.py:416
  10.4 1.3 %collective-permute-done.4 = bf16[4,64,128]{2,1,0:T(8,128)(2,1)S(1)} collective-permute-done((bf16[4,64,128]{2,1,0:T(8,128)(2,1)S(1)}, bf16[4,64,128]{2,1,0:T(8,128)(2,1)S(1)}, u32[]{:S(2)}, u32[]{:S(2)}) %collective-permute-start.4) | collective-permute-done | bytes 65568 | tf_op jit(solution)/shard_map/ppermute | solution.py:416
  11.7 0.5 %collective-permute-done.3 = bf16[4,64,128]{2,1,0:T(8,128)(2,1)S(1)} collective-permute-done((bf16[4,64,128]{2,1,0:T(8,128)(2,1)S(1)}, bf16[4,64,128]{2,1,0:T(8,128)(2,1)S(1)}, u32[]{:S(2)}, u32[]{:S(2)}) %collective-permute-start.3) | collective-permute-done | bytes 65568 | tf_op jit(solution)/shard_map/ppermute | solution.py:416
  12.1 0.0 collective-permute-done.2
  12.2 1.6 %collective-permute-start.8 = (bf16[64,128]{1,0:T(8,128)(2,1)S(1)}, bf16[64,128]{1,0:T(8,128)(2,1)S(1)}, u32[]{:S(2)}, u32[]{:S(2)}) collective-permute-start(bf16[64,128]{1,0:T(8,128)(2,1)S(1)} %get-tuple-element.27), channel_id=1, source_target_pairs={{0,9},{1,8},{2,11},{3,10},{4,13},{5,12},{6,15},{7,14},{8,25},{9,24... | collective-permute-start | bytes 49160 | tf_op jit(solution)/shard_map/ppermute | solution.py:418
  13.8 1.2 %collective-permute-start.7 = (bf16[64,128]{1,0:T(8,128)(2,1)S(1)}, bf16[64,128]{1,0:T(8,128)(2,1)S(1)}, u32[]{:S(2)}, u32[]{:S(2)}) collective-permute-start(bf16[64,128]{1,0:T(8,128)(2,1)S(1)} %get-tuple-element.28), channel_id=1, source_target_pairs={{0,17},{1,16},{2,19},{3,18},{4,21},{5,20},{6,23},{7,22},{8,9},{9,8... | collective-permute-start | bytes 49160 | tf_op jit(solution)/shard_map/ppermute | solution.py:418
  15.0 1.2 %collective-permute-start.6 = (bf16[64,128]{1,0:T(8,128)(2,1)S(1)}, bf16[64,128]{1,0:T(8,128)(2,1)S(1)}, u32[]{:S(2)}, u32[]{:S(2)}) collective-permute-start(bf16[64,128]{1,0:T(8,128)(2,1)S(1)} %get-tuple-element.29), channel_id=1, source_target_pairs={{0,25},{1,24},{2,27},{3,26},{4,29},{5,28},{6,31},{7,30},{8,1},{9,0... | collective-permute-start | bytes 49160 | tf_op jit(solution)/shard_map/ppermute | solution.py:418
  16.1 0.2 %collective-permute-start.5 = (bf16[64,128]{1,0:T(8,128)(2,1)S(1)}, bf16[64,128]{1,0:T(8,128)(2,1)S(1)}, u32[]{:S(2)}, u32[]{:S(2)}) collective-permute-start(bf16[64,128]{1,0:T(8,128)(2,1)S(1)} %get-tuple-element.30), channel_id=1, source_target_pairs={{0,1},{1,0},{2,3},{3,2},{4,5},{5,4},{6,7},{7,6},{8,17},{9,16},{10,... | collective-permute-start | bytes 49160 | tf_op jit(solution)/shard_map/ppermute | solution.py:418
  16.4 0.9 %collective-permute-done.8.refs_3_ = bf16[64,128]{1,0:T(8,128)(2,1)S(1)} collective-permute-done((bf16[64,128]{1,0:T(8,128)(2,1)S(1)}, bf16[64,128]{1,0:T(8,128)(2,1)S(1)}, u32[]{:S(2)}, u32[]{:S(2)}) %collective-permute-start.8) | collective-permute-done | bytes 16416 | tf_op jit(solution)/shard_map/ppermute | solution.py:418
  17.2 0.7 %collective-permute-done.7.refs_2_ = bf16[64,128]{1,0:T(8,128)(2,1)S(1)} collective-permute-done((bf16[64,128]{1,0:T(8,128)(2,1)S(1)}, bf16[64,128]{1,0:T(8,128)(2,1)S(1)}, u32[]{:S(2)}, u32[]{:S(2)}) %collective-permute-start.7) | collective-permute-done | bytes 16416 | tf_op jit(solution)/shard_map/ppermute | solution.py:418
  17.9 0.4 %collective-permute-done.6.refs_1_ = bf16[64,128]{1,0:T(8,128)(2,1)S(1)} collective-permute-done((bf16[64,128]{1,0:T(8,128)(2,1)S(1)}, bf16[64,128]{1,0:T(8,128)(2,1)S(1)}, u32[]{:S(2)}, u32[]{:S(2)}) %collective-permute-start.6) | collective-permute-done | bytes 16416 | tf_op jit(solution)/shard_map/ppermute | solution.py:418
  18.3 0.0 collective-permute-done.5.refs_0_
  18.3 0.7 %add_last.1 = f32[64,128]{1,0:T(8,128)} custom-call(bf16[64,128]{1,0:T(8,128)(2,1)S(1)} %collective-permute-done.5.refs_0_, bf16[64,128]{1,0:T(8,128)(2,1)S(1)} %collective-permute-done.6.refs_1_, bf16[64,128]{1,0:T(8,128)(2,1)S(1)} %collective-permute-done.7.refs_2_, bf16[64,128]{1,0:T(8,128)(2,1)S(1)} %collective-permute-done.8.refs_3_), custom_call_target="tpu_custom_call" | custom-call | tf_op jit(solution)/shard_map/add_last/pallas_call | solution.py:419
  (3 shorter events, 0.1 us)
Async XLA Ops:
  2.4 1.9 %collective-permute-start = (bf16[16,64,128]{2,1,0:T(8,128)(2,1)S(1)}, bf16[16,64,128]{2,1,0:T(8,128)(2,1)S(1)}, u32[]{:S(2)}, u32[]{:S(2)}) collective-permute-start(bf16[16,64,128]{2,1,0:T(8,128)(2,1)S(1)} %get-tuple-element.22), channel_id=1, source_target_pairs={{0,1},{1,0},{2,3},{3,2},{4,5},{5,4},{6,7},{7,6},{8,9},{9,8},{10,11... | collective-permute-start | bytes 786440 | tf_op jit(solution)/shard_map/ppermute | solution.py:404
  4.4 6.0 %collective-permute-start.1 = (bf16[4,64,128]{2,1,0:T(8,128)(2,1)S(1)}, bf16[4,64,128]{2,1,0:T(8,128)(2,1)S(1)}, u32[]{:S(2)}, u32[]{:S(2)}) collective-permute-start(bf16[4,64,128]{2,1,0:T(8,128)(2,1)S(1)} %get-tuple-element.23), channel_id=1, source_target_pairs={{0,3},{1,2},{2,1},{3,0},{4,5},{5,4},{6,7},{7,6},{8,11},{9,10},{10,... | collective-permute-start | bytes 196616 | tf_op jit(solution)/shard_map/ppermute | solution.py:416
  6.9 4.8 %collective-permute-start.4 = (bf16[4,64,128]{2,1,0:T(8,128)(2,1)S(1)}, bf16[4,64,128]{2,1,0:T(8,128)(2,1)S(1)}, u32[]{:S(2)}, u32[]{:S(2)}) collective-permute-start(bf16[4,64,128]{2,1,0:T(8,128)(2,1)S(1)} %get-tuple-element.24), channel_id=1, source_target_pairs={{0,5},{1,4},{2,7},{3,6},{4,3},{5,2},{6,1},{7,0},{8,13},{9,12},{10,... | collective-permute-start | bytes 196616 | tf_op jit(solution)/shard_map/ppermute | solution.py:416
  7.2 4.9 %collective-permute-start.3 = (bf16[4,64,128]{2,1,0:T(8,128)(2,1)S(1)}, bf16[4,64,128]{2,1,0:T(8,128)(2,1)S(1)}, u32[]{:S(2)}, u32[]{:S(2)}) collective-permute-start(bf16[4,64,128]{2,1,0:T(8,128)(2,1)S(1)} %get-tuple-element.25), channel_id=1, source_target_pairs={{0,7},{1,6},{2,5},{3,4},{4,1},{5,0},{6,3},{7,2},{8,15},{9,14},{10,... | collective-permute-start | bytes 196616 | tf_op jit(solution)/shard_map/ppermute | solution.py:416
  9.5 2.6 %collective-permute-start.2 = (bf16[4,64,128]{2,1,0:T(8,128)(2,1)S(1)}, bf16[4,64,128]{2,1,0:T(8,128)(2,1)S(1)}, u32[]{:S(2)}, u32[]{:S(2)}) collective-permute-start(bf16[4,64,128]{2,1,0:T(8,128)(2,1)S(1)} %get-tuple-element.26), channel_id=1, source_target_pairs={{0,1},{1,0},{2,3},{3,2},{4,7},{5,6},{6,5},{7,4},{8,9},{9,8},{10,11... | collective-permute-start | bytes 196616 | tf_op jit(solution)/shard_map/ppermute | solution.py:416
  12.2 5.0 %collective-permute-start.8 = (bf16[64,128]{1,0:T(8,128)(2,1)S(1)}, bf16[64,128]{1,0:T(8,128)(2,1)S(1)}, u32[]{:S(2)}, u32[]{:S(2)}) collective-permute-start(bf16[64,128]{1,0:T(8,128)(2,1)S(1)} %get-tuple-element.27), channel_id=1, source_target_pairs={{0,9},{1,8},{2,11},{3,10},{4,13},{5,12},{6,15},{7,14},{8,25},{9,24... | collective-permute-start | bytes 49160 | tf_op jit(solution)/shard_map/ppermute | solution.py:418
  13.8 4.1 %collective-permute-start.7 = (bf16[64,128]{1,0:T(8,128)(2,1)S(1)}, bf16[64,128]{1,0:T(8,128)(2,1)S(1)}, u32[]{:S(2)}, u32[]{:S(2)}) collective-permute-start(bf16[64,128]{1,0:T(8,128)(2,1)S(1)} %get-tuple-element.28), channel_id=1, source_target_pairs={{0,17},{1,16},{2,19},{3,18},{4,21},{5,20},{6,23},{7,22},{8,9},{9,8... | collective-permute-start | bytes 49160 | tf_op jit(solution)/shard_map/ppermute | solution.py:418
  15.0 3.3 %collective-permute-start.6 = (bf16[64,128]{1,0:T(8,128)(2,1)S(1)}, bf16[64,128]{1,0:T(8,128)(2,1)S(1)}, u32[]{:S(2)}, u32[]{:S(2)}) collective-permute-start(bf16[64,128]{1,0:T(8,128)(2,1)S(1)} %get-tuple-element.29), channel_id=1, source_target_pairs={{0,25},{1,24},{2,27},{3,26},{4,29},{5,28},{6,31},{7,30},{8,1},{9,0... | collective-permute-start | bytes 49160 | tf_op jit(solution)/shard_map/ppermute | solution.py:418
  16.1 2.2 %collective-permute-start.5 = (bf16[64,128]{1,0:T(8,128)(2,1)S(1)}, bf16[64,128]{1,0:T(8,128)(2,1)S(1)}, u32[]{:S(2)}, u32[]{:S(2)}) collective-permute-start(bf16[64,128]{1,0:T(8,128)(2,1)S(1)} %get-tuple-element.30), channel_id=1, source_target_pairs={{0,1},{1,0},{2,3},{3,2},{4,5},{5,4},{6,7},{7,6},{8,17},{9,16},{10,... | collective-permute-start | bytes 49160 | tf_op jit(solution)/shard_map/ppermute | solution.py:418

commit v9 on v8

--- a/solution.py
+++ b/solution.py
@@ -292,7 +292,10 @@
 HBM = pl.BlockSpec(memory_space=pltpu.HBM)
 
 
-FIRST = (((1, 0, 2, 3), (2, 3, 1, 0), (3, 2, 0, 1), (0, 1, 3, 2)),) * 2
+FIRST = (
+    ((2, 1, 0, 3), (1, 2, 3, 0), (3, 0, 2, 1), (0, 3, 1, 2)),
+    ((1, 0, 2, 3), (2, 3, 1, 0), (3, 1, 0, 2), (0, 2, 3, 1)),
+)
 USUAL = ((1, 2, 0, 3), (2, 1, 3, 0), (3, 0, 2, 1), (0, 3, 1, 2))
 SECOND = (((1, 3, 2, 0), (2, 1, 0, 3), (3, 0, 1, 2), (0, 2, 3, 1)), USUAL, USUAL, USUAL)
 FIRST_LISTED = (0, 3, 2, 1)

time: 19.3 us -> 19.2 us (level)
  waiting for transfers between devices: 4.21 us -> 3.6 us
  starting transfers between devices: 10.3 us -> 10.9 us
    ppermute x4, starting transfers between devices: 4.15 us -> 4.71 us  [on_device(): lax.ppermute(total[slot], axes, pairs_of(1, slot))]
    ppermute x4, waiting for transfers between devices: 2.27 us -> 1.8 us  [on_device(): lax.ppermute(total[4 * slot:4 * slot + 4], axes, pairs_of(0, slot))]
  transfers between devices with their start and end apart: 9 -> 9, of which waited for: 6 -> 4; matrix products, arithmetic and copies ran while one was open for 0% -> 0% of each run, Pallas kernels for 6% -> 6%
where the time goes in v9:
time: 19.2 us; the launch traced here: 19 us
  starting transfers between devices  10.9 us (57%)
  Pallas kernels  4.25 us (22%)
  waiting for transfers between devices  3.6 us (19%)
    ppermute x4, starting transfers between devices, on_device(): lax.ppermute(total[4 * slot:4 * slot + 4], axes, pairs_of(0, slot))  5.48 us
    ppermute x4, starting transfers between devices, on_device(): lax.ppermute(total[slot], axes, pairs_of(1, slot))  4.71 us
    pallas_call x1, Pallas kernels, on_device(): pl.pallas_call(functools.partial(first_kernel, planes), out_shape=(piece_...  2.37 us
    ppermute x4, waiting for transfers between devices, on_device(): lax.ppermute(total[slot], axes, pairs_of(1, slot))  1.8 us
    ppermute x4, waiting for transfers between devices, on_device(): lax.ppermute(total[4 * slot:4 * slot + 4], axes, pairs_of(0, slot))  1.8 us
    pallas_call x1, Pallas kernels, on_device(): pl.pallas_call(second_kernel, out_shape=(piece_shape, w_shape), in_specs=...  1.17 us
    ppermute x1, starting transfers between devices, on_device(): lax.ppermute(other, axes, [(i, i ^ 1) for i in range(owners * groups)])  0.73 us
    pallas_call x1, Pallas kernels, on_device(): pl.pallas_call(last_kernel, out_shape=jax.ShapeDtypeStruct((2 * planes, L...  0.7 us
  transfers between devices with their start and end apart: 9, of which 4 were waited for; matrix products, arithmetic and copies ran while one was open for 0% of the time, Pallas kernels for 6%

profile of v9, /device:TPU:0, one launch (start us, length us, event | category | flops | bytes accessed | tf_op | source)
XLA Modules:
  0.0 19.0 jit_solution(13223393706001866517)
XLA Ops:
  0.0 2.4 %weigh_and_transform_other.1 = (bf16[16,64,128]{2,1,0:T(8,128)(2,1)S(1)}, f32[4264,128]{1,0:T(8,128)S(1)}, bf16[4096,128]{1,0:T(8,128)(2,1)S(1)}, f32[128,128]{1...) custom-call(bf16[4096,128]{1,0:T(8,128)(2,1)} %bitcast.19, ...), custom_call_target="tpu_custom_call" | custom-call | tf_op jit(solution)/shard_map/weigh_and_transform_other/pallas_call | solution.py:377
  2.4 0.7 %collective-permute-start = (bf16[16,64,128]{2,1,0:T(8,128)(2,1)S(1)}, bf16[16,64,128]{2,1,0:T(8,128)(2,1)S(1)}, u32[]{:S(2)}, u32[]{:S(2)}) collective-permute-start(bf16[16,64,128]{2,1,0:T(8,128)(2,1)S(1)} %get-tuple-element.22), channel_id=1, source_target_pairs={{0,1},{1,0},{2,3},{3,2},{4,5},{5,4},{6,7},{7,6},{8,9},{9,8},{10,11... | collective-permute-start | bytes 786440 | tf_op jit(solution)/shard_map/ppermute | solution.py:407
  3.1 1.2 %transform_own.1 = (bf16[16,64,128]{2,1,0:T(8,128)(2,1)S(1)}, f32[4264,128]{1,0:T(8,128)S(1)}) custom-call(f32[4264,128]{1,0:T(8,128)S(1)} %get-tuple-element.14.w_in, bf16[4096,128]{1,0:T(8,128)(2,1)S(1)} %get-tuple-element.15.x_ref, f32[128,128]{1,0:T(8,128)S(1)} %get-tuple-element.16.wide_ref, ...), custom_call_target="tpu_custom_call", output_to_operand_aliasing={{1}: (0, {})} | custom-call | tf_op jit(solution)/shard_map/transform_own/pallas_call | solution.py:408
  4.3 0.0 collective-permute-done
  4.3 0.1 add_convert_fusion
  4.4 2.4 %collective-permute-start.1 = (bf16[4,64,128]{2,1,0:T(8,128)(2,1)S(1)}, bf16[4,64,128]{2,1,0:T(8,128)(2,1)S(1)}, u32[]{:S(2)}, u32[]{:S(2)}) collective-permute-start(bf16[4,64,128]{2,1,0:T(8,128)(2,1)S(1)} %get-tuple-element.23), channel_id=1, source_target_pairs={{0,5},{1,2},{2,3},{3,0},{4,1},{5,4},{6,7},{7,6},{8,13},{9,10},{10,... | collective-permute-start | bytes 196616 | tf_op jit(solution)/shard_map/ppermute | solution.py:419
  6.8 0.1 collective-permute-start.4
  6.9 2.6 %collective-permute-start.3 = (bf16[4,64,128]{2,1,0:T(8,128)(2,1)S(1)}, bf16[4,64,128]{2,1,0:T(8,128)(2,1)S(1)}, u32[]{:S(2)}, u32[]{:S(2)}) collective-permute-start(bf16[4,64,128]{2,1,0:T(8,128)(2,1)S(1)} %get-tuple-element.25), channel_id=1, source_target_pairs={{0,7},{1,6},{2,1},{3,2},{4,5},{5,0},{6,3},{7,4},{8,15},{9,14},{10,... | collective-permute-start | bytes 196616 | tf_op jit(solution)/shard_map/ppermute | solution.py:419
  9.5 0.4 %collective-permute-start.2 = (bf16[4,64,128]{2,1,0:T(8,128)(2,1)S(1)}, bf16[4,64,128]{2,1,0:T(8,128)(2,1)S(1)}, u32[]{:S(2)}, u32[]{:S(2)}) collective-permute-start(bf16[4,64,128]{2,1,0:T(8,128)(2,1)S(1)} %get-tuple-element.26), channel_id=1, source_target_pairs={{0,1},{1,0},{2,7},{3,4},{4,3},{5,6},{6,5},{7,2},{8,9},{9,8},{10,15... | collective-permute-start | bytes 196616 | tf_op jit(solution)/shard_map/ppermute | solution.py:419
  9.9 0.0 collective-permute-done.1
  9.9 1.8 %collective-permute-done.4 = bf16[4,64,128]{2,1,0:T(8,128)(2,1)S(1)} collective-permute-done((bf16[4,64,128]{2,1,0:T(8,128)(2,1)S(1)}, bf16[4,64,128]{2,1,0:T(8,128)(2,1)S(1)}, u32[]{:S(2)}, u32[]{:S(2)}) %collective-permute-start.4) | collective-permute-done | bytes 65568 | tf_op jit(solution)/shard_map/ppermute | solution.py:419
  11.7 0.0 collective-permute-done.3
  11.7 0.0 collective-permute-done.2
  11.8 2.1 %collective-permute-start.8 = (bf16[64,128]{1,0:T(8,128)(2,1)S(1)}, bf16[64,128]{1,0:T(8,128)(2,1)S(1)}, u32[]{:S(2)}, u32[]{:S(2)}) collective-permute-start(bf16[64,128]{1,0:T(8,128)(2,1)S(1)} %get-tuple-element.27), channel_id=1, source_target_pairs={{0,9},{1,8},{2,11},{3,10},{4,13},{5,12},{6,15},{7,14},{8,25},{9,24... | collective-permute-start | bytes 49160 | tf_op jit(solution)/shard_map/ppermute | solution.py:421
  13.9 1.1 %collective-permute-start.7 = (bf16[64,128]{1,0:T(8,128)(2,1)S(1)}, bf16[64,128]{1,0:T(8,128)(2,1)S(1)}, u32[]{:S(2)}, u32[]{:S(2)}) collective-permute-start(bf16[64,128]{1,0:T(8,128)(2,1)S(1)} %get-tuple-element.28), channel_id=1, source_target_pairs={{0,17},{1,16},{2,19},{3,18},{4,21},{5,20},{6,23},{7,22},{8,9},{9,8... | collective-permute-start | bytes 49160 | tf_op jit(solution)/shard_map/ppermute | solution.py:421
  14.9 1.2 %collective-permute-start.6 = (bf16[64,128]{1,0:T(8,128)(2,1)S(1)}, bf16[64,128]{1,0:T(8,128)(2,1)S(1)}, u32[]{:S(2)}, u32[]{:S(2)}) collective-permute-start(bf16[64,128]{1,0:T(8,128)(2,1)S(1)} %get-tuple-element.29), channel_id=1, source_target_pairs={{0,25},{1,24},{2,27},{3,26},{4,29},{5,28},{6,31},{7,30},{8,1},{9,0... | collective-permute-start | bytes 49160 | tf_op jit(solution)/shard_map/ppermute | solution.py:421
  16.1 0.3 %collective-permute-start.5 = (bf16[64,128]{1,0:T(8,128)(2,1)S(1)}, bf16[64,128]{1,0:T(8,128)(2,1)S(1)}, u32[]{:S(2)}, u32[]{:S(2)}) collective-permute-start(bf16[64,128]{1,0:T(8,128)(2,1)S(1)} %get-tuple-element.30), channel_id=1, source_target_pairs={{0,1},{1,0},{2,3},{3,2},{4,5},{5,4},{6,7},{7,6},{8,17},{9,16},{10,... | collective-permute-start | bytes 49160 | tf_op jit(solution)/shard_map/ppermute | solution.py:421
  16.5 0.8 %collective-permute-done.8.refs_3_ = bf16[64,128]{1,0:T(8,128)(2,1)S(1)} collective-permute-done((bf16[64,128]{1,0:T(8,128)(2,1)S(1)}, bf16[64,128]{1,0:T(8,128)(2,1)S(1)}, u32[]{:S(2)}, u32[]{:S(2)}) %collective-permute-start.8) | collective-permute-done | bytes 16416 | tf_op jit(solution)/shard_map/ppermute | solution.py:421
  17.3 0.8 %collective-permute-done.7.refs_2_ = bf16[64,128]{1,0:T(8,128)(2,1)S(1)} collective-permute-done((bf16[64,128]{1,0:T(8,128)(2,1)S(1)}, bf16[64,128]{1,0:T(8,128)(2,1)S(1)}, u32[]{:S(2)}, u32[]{:S(2)}) %collective-permute-start.7) | collective-permute-done | bytes 16416 | tf_op jit(solution)/shard_map/ppermute | solution.py:421
  18.1 0.2 collective-permute-done.6.refs_1_
  18.3 0.0 collective-permute-done.5.refs_0_
  18.3 0.7 %add_last.1 = f32[64,128]{1,0:T(8,128)} custom-call(bf16[64,128]{1,0:T(8,128)(2,1)S(1)} %collective-permute-done.5.refs_0_, bf16[64,128]{1,0:T(8,128)(2,1)S(1)} %collective-permute-done.6.refs_1_, bf16[64,128]{1,0:T(8,128)(2,1)S(1)} %collective-permute-done.7.refs_2_, bf16[64,128]{1,0:T(8,128)(2,1)S(1)} %collective-permute-done.8.refs_3_), custom_call_target="tpu_custom_call" | custom-call | tf_op jit(solution)/shard_map/add_last/pallas_call | solution.py:422
  (3 shorter events, 0.1 us)
Async XLA Ops:
  2.4 1.9 %collective-permute-start = (bf16[16,64,128]{2,1,0:T(8,128)(2,1)S(1)}, bf16[16,64,128]{2,1,0:T(8,128)(2,1)S(1)}, u32[]{:S(2)}, u32[]{:S(2)}) collective-permute-start(bf16[16,64,128]{2,1,0:T(8,128)(2,1)S(1)} %get-tuple-element.22), channel_id=1, source_target_pairs={{0,1},{1,0},{2,3},{3,2},{4,5},{5,4},{6,7},{7,6},{8,9},{9,8},{10,11... | collective-permute-start | bytes 786440 | tf_op jit(solution)/shard_map/ppermute | solution.py:407
  4.4 5.5 %collective-permute-start.1 = (bf16[4,64,128]{2,1,0:T(8,128)(2,1)S(1)}, bf16[4,64,128]{2,1,0:T(8,128)(2,1)S(1)}, u32[]{:S(2)}, u32[]{:S(2)}) collective-permute-start(bf16[4,64,128]{2,1,0:T(8,128)(2,1)S(1)} %get-tuple-element.23), channel_id=1, source_target_pairs={{0,5},{1,2},{2,3},{3,0},{4,1},{5,4},{6,7},{7,6},{8,13},{9,10},{10,... | collective-permute-start | bytes 196616 | tf_op jit(solution)/shard_map/ppermute | solution.py:419
  6.8 4.8 %collective-permute-start.4 = (bf16[4,64,128]{2,1,0:T(8,128)(2,1)S(1)}, bf16[4,64,128]{2,1,0:T(8,128)(2,1)S(1)}, u32[]{:S(2)}, u32[]{:S(2)}) collective-permute-start(bf16[4,64,128]{2,1,0:T(8,128)(2,1)S(1)} %get-tuple-element.24), channel_id=1, source_target_pairs={{0,3},{1,4},{2,5},{3,6},{4,7},{5,2},{6,1},{7,0},{8,11},{9,12},{10,... | collective-permute-start | bytes 196616 | tf_op jit(solution)/shard_map/ppermute | solution.py:419
  6.9 4.8 %collective-permute-start.3 = (bf16[4,64,128]{2,1,0:T(8,128)(2,1)S(1)}, bf16[4,64,128]{2,1,0:T(8,128)(2,1)S(1)}, u32[]{:S(2)}, u32[]{:S(2)}) collective-permute-start(bf16[4,64,128]{2,1,0:T(8,128)(2,1)S(1)} %get-tuple-element.25), channel_id=1, source_target_pairs={{0,7},{1,6},{2,1},{3,2},{4,5},{5,0},{6,3},{7,4},{8,15},{9,14},{10,... | collective-permute-start | bytes 196616 | tf_op jit(solution)/shard_map/ppermute | solution.py:419
  9.5 2.2 %collective-permute-start.2 = (bf16[4,64,128]{2,1,0:T(8,128)(2,1)S(1)}, bf16[4,64,128]{2,1,0:T(8,128)(2,1)S(1)}, u32[]{:S(2)}, u32[]{:S(2)}) collective-permute-start(bf16[4,64,128]{2,1,0:T(8,128)(2,1)S(1)} %get-tuple-element.26), channel_id=1, source_target_pairs={{0,1},{1,0},{2,7},{3,4},{4,3},{5,6},{6,5},{7,2},{8,9},{9,8},{10,15... | collective-permute-start | bytes 196616 | tf_op jit(solution)/shard_map/ppermute | solution.py:419
  11.8 5.6 %collective-permute-start.8 = (bf16[64,128]{1,0:T(8,128)(2,1)S(1)}, bf16[64,128]{1,0:T(8,128)(2,1)S(1)}, u32[]{:S(2)}, u32[]{:S(2)}) collective-permute-start(bf16[64,128]{1,0:T(8,128)(2,1)S(1)} %get-tuple-element.27), channel_id=1, source_target_pairs={{0,9},{1,8},{2,11},{3,10},{4,13},{5,12},{6,15},{7,14},{8,25},{9,24... | collective-permute-start | bytes 49160 | tf_op jit(solution)/shard_map/ppermute | solution.py:421
  13.9 4.2 %collective-permute-start.7 = (bf16[64,128]{1,0:T(8,128)(2,1)S(1)}, bf16[64,128]{1,0:T(8,128)(2,1)S(1)}, u32[]{:S(2)}, u32[]{:S(2)}) collective-permute-start(bf16[64,128]{1,0:T(8,128)(2,1)S(1)} %get-tuple-element.28), channel_id=1, source_target_pairs={{0,17},{1,16},{2,19},{3,18},{4,21},{5,20},{6,23},{7,22},{8,9},{9,8... | collective-permute-start | bytes 49160 | tf_op jit(solution)/shard_map/ppermute | solution.py:421
  14.9 3.3 %collective-permute-start.6 = (bf16[64,128]{1,0:T(8,128)(2,1)S(1)}, bf16[64,128]{1,0:T(8,128)(2,1)S(1)}, u32[]{:S(2)}, u32[]{:S(2)}) collective-permute-start(bf16[64,128]{1,0:T(8,128)(2,1)S(1)} %get-tuple-element.29), channel_id=1, source_target_pairs={{0,25},{1,24},{2,27},{3,26},{4,29},{5,28},{6,31},{7,30},{8,1},{9,0... | collective-permute-start | bytes 49160 | tf_op jit(solution)/shard_map/ppermute | solution.py:421
  16.1 2.1 %collective-permute-start.5 = (bf16[64,128]{1,0:T(8,128)(2,1)S(1)}, bf16[64,128]{1,0:T(8,128)(2,1)S(1)}, u32[]{:S(2)}, u32[]{:S(2)}) collective-permute-start(bf16[64,128]{1,0:T(8,128)(2,1)S(1)} %get-tuple-element.30), channel_id=1, source_target_pairs={{0,1},{1,0},{2,3},{3,2},{4,5},{5,4},{6,7},{7,6},{8,17},{9,16},{10,... | collective-permute-start | bytes 49160 | tf_op jit(solution)/shard_map/ppermute | solution.py:421

commit v10 on v9

--- a/solution.py
+++ b/solution.py
@@ -19,7 +19,7 @@
 QUARTERS = NX // LANES
 PLANES = 32
 CHUNKS = 4
-UNROLL = 16
+UNROLL = 32
 PARTS = 4
 ROWS = QUARTERS * KY
 PITCH = 2 * ROWS + 1
@@ -128,6 +128,8 @@
             value = parts[-quarter % QUARTERS]
             for j in range(1, QUARTERS):
                 value = jnp.where(group == j, parts[(j - quarter) % QUARTERS], value)
+            if quarter:
+                value = pltpu.roll(value, LANES - quarter, 1)
             value = value.astype(bf16)
             for cls in range(CLASSES):
                 put(y, cls, quarter, value[cls * 2 * PLANES : (cls + 1) * 2 * PLANES])
@@ -282,9 +284,7 @@
 
 def last_kernel(*refs):
     *got_refs, out_ref = refs
-    quarter = lax.axis_index("slab") % QUARTERS
-    total = sum(got_ref[...].astype(f32) for got_ref in got_refs)
-    out_ref[...] = pltpu.roll(total, (LANES - quarter) % LANES, 1)
+    out_ref[...] = sum(got_ref[...].astype(f32) for got_ref in got_refs)
 
 
 VMEM = pl.BlockSpec(memory_space=pltpu.VMEM)

time: 19.2 us -> 19.2 us (level)
  no operation moved by 1% of the time
where the time goes in v10:
time: 19.2 us; the launch traced here: 18.9 us
  starting transfers between devices  10.9 us (57%)
  Pallas kernels  4.25 us (22%)
  waiting for transfers between devices  3.6 us (19%)
    ppermute x4, starting transfers between devices, on_device(): lax.ppermute(total[4 * slot:4 * slot + 4], axes, pairs_of(0, slot))  5.44 us
    ppermute x4, starting transfers between devices, on_device(): lax.ppermute(total[slot], axes, pairs_of(1, slot))  4.71 us
    pallas_call x1, Pallas kernels, on_device(): pl.pallas_call(functools.partial(first_kernel, planes), out_shape=(piece_...  2.4 us
    ppermute x4, waiting for transfers between devices, on_device(): lax.ppermute(total[slot], axes, pairs_of(1, slot))  1.8 us
    ppermute x4, waiting for transfers between devices, on_device(): lax.ppermute(total[4 * slot:4 * slot + 4], axes, pairs_of(0, slot))  1.8 us
    pallas_call x1, Pallas kernels, on_device(): pl.pallas_call(second_kernel, out_shape=(piece_shape, w_shape), in_specs=...  1.22 us
    ppermute x1, starting transfers between devices, on_device(): lax.ppermute(other, axes, [(i, i ^ 1) for i in range(owners * groups)])  0.72 us
    pallas_call x1, Pallas kernels, on_device(): pl.pallas_call(last_kernel, out_shape=jax.ShapeDtypeStruct((2 * planes, L...  0.63 us
  transfers between devices with their start and end apart: 9, of which 4 were waited for; matrix products, arithmetic and copies ran while one was open for 0% of the time, Pallas kernels for 6%

profile of v10, /device:TPU:0, one launch (start us, length us, event | category | flops | bytes accessed | tf_op | source)
XLA Modules:
  0.0 18.9 jit_solution(9514819214769717956)
XLA Ops:
  0.0 2.4 %weigh_and_transform_other.1 = (bf16[16,64,128]{2,1,0:T(8,128)(2,1)S(1)}, f32[4264,128]{1,0:T(8,128)S(1)}, bf16[4096,128]{1,0:T(8,128)(2,1)S(1)}, f32[128,128]{1...) custom-call(bf16[4096,128]{1,0:T(8,128)(2,1)} %bitcast.19, ...), custom_call_target="tpu_custom_call" | custom-call | tf_op jit(solution)/shard_map/weigh_and_transform_other/pallas_call | solution.py:377
  2.4 0.7 %collective-permute-start = (bf16[16,64,128]{2,1,0:T(8,128)(2,1)S(1)}, bf16[16,64,128]{2,1,0:T(8,128)(2,1)S(1)}, u32[]{:S(2)}, u32[]{:S(2)}) collective-permute-start(bf16[16,64,128]{2,1,0:T(8,128)(2,1)S(1)} %get-tuple-element.22), channel_id=1, source_target_pairs={{0,1},{1,0},{2,3},{3,2},{4,5},{5,4},{6,7},{7,6},{8,9},{9,8},{10,11... | collective-permute-start | bytes 786440 | tf_op jit(solution)/shard_map/ppermute | solution.py:407
  3.1 1.2 %transform_own.1 = (bf16[16,64,128]{2,1,0:T(8,128)(2,1)S(1)}, f32[4264,128]{1,0:T(8,128)S(1)}) custom-call(f32[4264,128]{1,0:T(8,128)S(1)} %get-tuple-element.14.w_in, bf16[4096,128]{1,0:T(8,128)(2,1)S(1)} %get-tuple-element.15.x_ref, f32[128,128]{1,0:T(8,128)S(1)} %get-tuple-element.16.wide_ref, ...), custom_call_target="tpu_custom_call", output_to_operand_aliasing={{1}: (0, {})} | custom-call | tf_op jit(solution)/shard_map/transform_own/pallas_call | solution.py:408
  4.4 0.0 collective-permute-done
  4.4 0.1 add_convert_fusion
  4.5 2.4 %collective-permute-start.1 = (bf16[4,64,128]{2,1,0:T(8,128)(2,1)S(1)}, bf16[4,64,128]{2,1,0:T(8,128)(2,1)S(1)}, u32[]{:S(2)}, u32[]{:S(2)}) collective-permute-start(bf16[4,64,128]{2,1,0:T(8,128)(2,1)S(1)} %get-tuple-element.23), channel_id=1, source_target_pairs={{0,5},{1,2},{2,3},{3,0},{4,1},{5,4},{6,7},{7,6},{8,13},{9,10},{10,... | collective-permute-start | bytes 196616 | tf_op jit(solution)/shard_map/ppermute | solution.py:419
  6.8 0.1 collective-permute-start.4
  6.9 2.6 %collective-permute-start.3 = (bf16[4,64,128]{2,1,0:T(8,128)(2,1)S(1)}, bf16[4,64,128]{2,1,0:T(8,128)(2,1)S(1)}, u32[]{:S(2)}, u32[]{:S(2)}) collective-permute-start(bf16[4,64,128]{2,1,0:T(8,128)(2,1)S(1)} %get-tuple-element.25), channel_id=1, source_target_pairs={{0,7},{1,6},{2,1},{3,2},{4,5},{5,0},{6,3},{7,4},{8,15},{9,14},{10,... | collective-permute-start | bytes 196616 | tf_op jit(solution)/shard_map/ppermute | solution.py:419
  9.5 0.4 %collective-permute-start.2 = (bf16[4,64,128]{2,1,0:T(8,128)(2,1)S(1)}, bf16[4,64,128]{2,1,0:T(8,128)(2,1)S(1)}, u32[]{:S(2)}, u32[]{:S(2)}) collective-permute-start(bf16[4,64,128]{2,1,0:T(8,128)(2,1)S(1)} %get-tuple-element.26), channel_id=1, source_target_pairs={{0,1},{1,0},{2,7},{3,4},{4,3},{5,6},{6,5},{7,2},{8,9},{9,8},{10,15... | collective-permute-start | bytes 196616 | tf_op jit(solution)/shard_map/ppermute | solution.py:419
  9.9 0.0 collective-permute-done.1
  9.9 1.8 %collective-permute-done.4 = bf16[4,64,128]{2,1,0:T(8,128)(2,1)S(1)} collective-permute-done((bf16[4,64,128]{2,1,0:T(8,128)(2,1)S(1)}, bf16[4,64,128]{2,1,0:T(8,128)(2,1)S(1)}, u32[]{:S(2)}, u32[]{:S(2)}) %collective-permute-start.4) | collective-permute-done | bytes 65568 | tf_op jit(solution)/shard_map/ppermute | solution.py:419
  11.7 0.0 collective-permute-done.3
  11.7 0.0 collective-permute-done.2
  11.8 2.1 %collective-permute-start.8 = (bf16[64,128]{1,0:T(8,128)(2,1)S(1)}, bf16[64,128]{1,0:T(8,128)(2,1)S(1)}, u32[]{:S(2)}, u32[]{:S(2)}) collective-permute-start(bf16[64,128]{1,0:T(8,128)(2,1)S(1)} %get-tuple-element.27), channel_id=1, source_target_pairs={{0,9},{1,8},{2,11},{3,10},{4,13},{5,12},{6,15},{7,14},{8,25},{9,24... | collective-permute-start | bytes 49160 | tf_op jit(solution)/shard_map/ppermute | solution.py:421
  13.9 1.1 %collective-permute-start.7 = (bf16[64,128]{1,0:T(8,128)(2,1)S(1)}, bf16[64,128]{1,0:T(8,128)(2,1)S(1)}, u32[]{:S(2)}, u32[]{:S(2)}) collective-permute-start(bf16[64,128]{1,0:T(8,128)(2,1)S(1)} %get-tuple-element.28), channel_id=1, source_target_pairs={{0,17},{1,16},{2,19},{3,18},{4,21},{5,20},{6,23},{7,22},{8,9},{9,8... | collective-permute-start | bytes 49160 | tf_op jit(solution)/shard_map/ppermute | solution.py:421
  15.0 1.2 %collective-permute-start.6 = (bf16[64,128]{1,0:T(8,128)(2,1)S(1)}, bf16[64,128]{1,0:T(8,128)(2,1)S(1)}, u32[]{:S(2)}, u32[]{:S(2)}) collective-permute-start(bf16[64,128]{1,0:T(8,128)(2,1)S(1)} %get-tuple-element.29), channel_id=1, source_target_pairs={{0,25},{1,24},{2,27},{3,26},{4,29},{5,28},{6,31},{7,30},{8,1},{9,0... | collective-permute-start | bytes 49160 | tf_op jit(solution)/shard_map/ppermute | solution.py:421
  16.2 0.3 %collective-permute-start.5 = (bf16[64,128]{1,0:T(8,128)(2,1)S(1)}, bf16[64,128]{1,0:T(8,128)(2,1)S(1)}, u32[]{:S(2)}, u32[]{:S(2)}) collective-permute-start(bf16[64,128]{1,0:T(8,128)(2,1)S(1)} %get-tuple-element.30), channel_id=1, source_target_pairs={{0,1},{1,0},{2,3},{3,2},{4,5},{5,4},{6,7},{7,6},{8,17},{9,16},{10,... | collective-permute-start | bytes 49160 | tf_op jit(solution)/shard_map/ppermute | solution.py:421
  16.5 0.8 %collective-permute-done.8.refs_3_ = bf16[64,128]{1,0:T(8,128)(2,1)S(1)} collective-permute-done((bf16[64,128]{1,0:T(8,128)(2,1)S(1)}, bf16[64,128]{1,0:T(8,128)(2,1)S(1)}, u32[]{:S(2)}, u32[]{:S(2)}) %collective-permute-start.8) | collective-permute-done | bytes 16416 | tf_op jit(solution)/shard_map/ppermute | solution.py:421
  17.3 0.8 %collective-permute-done.7.refs_2_ = bf16[64,128]{1,0:T(8,128)(2,1)S(1)} collective-permute-done((bf16[64,128]{1,0:T(8,128)(2,1)S(1)}, bf16[64,128]{1,0:T(8,128)(2,1)S(1)}, u32[]{:S(2)}, u32[]{:S(2)}) %collective-permute-start.7) | collective-permute-done | bytes 16416 | tf_op jit(solution)/shard_map/ppermute | solution.py:421
  18.1 0.2 collective-permute-done.6.refs_1_
  18.3 0.0 collective-permute-done.5.refs_0_
  18.3 0.6 %add_last.1 = f32[64,128]{1,0:T(8,128)} custom-call(bf16[64,128]{1,0:T(8,128)(2,1)S(1)} %collective-permute-done.5.refs_0_, bf16[64,128]{1,0:T(8,128)(2,1)S(1)} %collective-permute-done.6.refs_1_, bf16[64,128]{1,0:T(8,128)(2,1)S(1)} %collective-permute-done.7.refs_2_, bf16[64,128]{1,0:T(8,128)(2,1)S(1)} %collective-permute-done.8.refs_3_), custom_call_target="tpu_custom_call" | custom-call | tf_op jit(solution)/shard_map/add_last/pallas_call | solution.py:422
  (3 shorter events, 0.1 us)
Async XLA Ops:
  2.4 2.0 %collective-permute-start = (bf16[16,64,128]{2,1,0:T(8,128)(2,1)S(1)}, bf16[16,64,128]{2,1,0:T(8,128)(2,1)S(1)}, u32[]{:S(2)}, u32[]{:S(2)}) collective-permute-start(bf16[16,64,128]{2,1,0:T(8,128)(2,1)S(1)} %get-tuple-element.22), channel_id=1, source_target_pairs={{0,1},{1,0},{2,3},{3,2},{4,5},{5,4},{6,7},{7,6},{8,9},{9,8},{10,11... | collective-permute-start | bytes 786440 | tf_op jit(solution)/shard_map/ppermute | solution.py:407
  4.5 5.4 %collective-permute-start.1 = (bf16[4,64,128]{2,1,0:T(8,128)(2,1)S(1)}, bf16[4,64,128]{2,1,0:T(8,128)(2,1)S(1)}, u32[]{:S(2)}, u32[]{:S(2)}) collective-permute-start(bf16[4,64,128]{2,1,0:T(8,128)(2,1)S(1)} %get-tuple-element.23), channel_id=1, source_target_pairs={{0,5},{1,2},{2,3},{3,0},{4,1},{5,4},{6,7},{7,6},{8,13},{9,10},{10,... | collective-permute-start | bytes 196616 | tf_op jit(solution)/shard_map/ppermute | solution.py:419
  6.8 4.8 %collective-permute-start.4 = (bf16[4,64,128]{2,1,0:T(8,128)(2,1)S(1)}, bf16[4,64,128]{2,1,0:T(8,128)(2,1)S(1)}, u32[]{:S(2)}, u32[]{:S(2)}) collective-permute-start(bf16[4,64,128]{2,1,0:T(8,128)(2,1)S(1)} %get-tuple-element.24), channel_id=1, source_target_pairs={{0,3},{1,4},{2,5},{3,6},{4,7},{5,2},{6,1},{7,0},{8,11},{9,12},{10,... | collective-permute-start | bytes 196616 | tf_op jit(solution)/shard_map/ppermute | solution.py:419
  6.9 4.8 %collective-permute-start.3 = (bf16[4,64,128]{2,1,0:T(8,128)(2,1)S(1)}, bf16[4,64,128]{2,1,0:T(8,128)(2,1)S(1)}, u32[]{:S(2)}, u32[]{:S(2)}) collective-permute-start(bf16[4,64,128]{2,1,0:T(8,128)(2,1)S(1)} %get-tuple-element.25), channel_id=1, source_target_pairs={{0,7},{1,6},{2,1},{3,2},{4,5},{5,0},{6,3},{7,4},{8,15},{9,14},{10,... | collective-permute-start | bytes 196616 | tf_op jit(solution)/shard_map/ppermute | solution.py:419
  9.5 2.2 %collective-permute-start.2 = (bf16[4,64,128]{2,1,0:T(8,128)(2,1)S(1)}, bf16[4,64,128]{2,1,0:T(8,128)(2,1)S(1)}, u32[]{:S(2)}, u32[]{:S(2)}) collective-permute-start(bf16[4,64,128]{2,1,0:T(8,128)(2,1)S(1)} %get-tuple-element.26), channel_id=1, source_target_pairs={{0,1},{1,0},{2,7},{3,4},{4,3},{5,6},{6,5},{7,2},{8,9},{9,8},{10,15... | collective-permute-start | bytes 196616 | tf_op jit(solution)/shard_map/ppermute | solution.py:419
  11.8 5.6 %collective-permute-start.8 = (bf16[64,128]{1,0:T(8,128)(2,1)S(1)}, bf16[64,128]{1,0:T(8,128)(2,1)S(1)}, u32[]{:S(2)}, u32[]{:S(2)}) collective-permute-start(bf16[64,128]{1,0:T(8,128)(2,1)S(1)} %get-tuple-element.27), channel_id=1, source_target_pairs={{0,9},{1,8},{2,11},{3,10},{4,13},{5,12},{6,15},{7,14},{8,25},{9,24... | collective-permute-start | bytes 49160 | tf_op jit(solution)/shard_map/ppermute | solution.py:421
  13.9 4.2 %collective-permute-start.7 = (bf16[64,128]{1,0:T(8,128)(2,1)S(1)}, bf16[64,128]{1,0:T(8,128)(2,1)S(1)}, u32[]{:S(2)}, u32[]{:S(2)}) collective-permute-start(bf16[64,128]{1,0:T(8,128)(2,1)S(1)} %get-tuple-element.28), channel_id=1, source_target_pairs={{0,17},{1,16},{2,19},{3,18},{4,21},{5,20},{6,23},{7,22},{8,9},{9,8... | collective-permute-start | bytes 49160 | tf_op jit(solution)/shard_map/ppermute | solution.py:421
  15.0 3.3 %collective-permute-start.6 = (bf16[64,128]{1,0:T(8,128)(2,1)S(1)}, bf16[64,128]{1,0:T(8,128)(2,1)S(1)}, u32[]{:S(2)}, u32[]{:S(2)}) collective-permute-start(bf16[64,128]{1,0:T(8,128)(2,1)S(1)} %get-tuple-element.29), channel_id=1, source_target_pairs={{0,25},{1,24},{2,27},{3,26},{4,29},{5,28},{6,31},{7,30},{8,1},{9,0... | collective-permute-start | bytes 49160 | tf_op jit(solution)/shard_map/ppermute | solution.py:421
  16.2 2.1 %collective-permute-start.5 = (bf16[64,128]{1,0:T(8,128)(2,1)S(1)}, bf16[64,128]{1,0:T(8,128)(2,1)S(1)}, u32[]{:S(2)}, u32[]{:S(2)}) collective-permute-start(bf16[64,128]{1,0:T(8,128)(2,1)S(1)} %get-tuple-element.30), channel_id=1, source_target_pairs={{0,1},{1,0},{2,3},{3,2},{4,5},{5,4},{6,7},{7,6},{8,17},{9,16},{10,... | collective-permute-start | bytes 49160 | tf_op jit(solution)/shard_map/ppermute | solution.py:421
